TPU v7x, 32 devices: a whole 2x2x4 slice. The times are simulated.
32 devices in a mesh: dp: 4 (over z), fsdp: 8 (over y, x, core).
Axes of the slice: x: 2, y: 2, z: 4, core: 2. Of those that a mesh axis runs over, the one named last changes fastest.
Arguments:
- tokens_in: bfloat16 [32768, 768], P(('dp', 'fsdp')), may hold values from -6 to 6
- w_qkv: bfloat16 [768, 2304], P(('dp', 'fsdp')), may hold values from -0.21875 to 0.21875
- w_attn_out: bfloat16 [768, 768], P(('dp', 'fsdp')), may hold values from -1.75 to 1.75
- gain_attn: bfloat16 [768], P(('dp', 'fsdp')), may hold values from 0.5 to 1.5
- gain_ffn: bfloat16 [768], P(('dp', 'fsdp')), may hold values from 0.5 to 1.5
- rel_bias: bfloat16 [768], P(('dp', 'fsdp')), may hold values from -3 to 3
- router: bfloat16 [768, 4], P(('dp', 'fsdp')), may hold values from -0.15625 to 0.15625
- w_in: bfloat16 [768, 12288], P('dp', 'fsdp'), may hold values from -0.21875 to 0.21875
- w_out: bfloat16 [768, 12288], P('dp', 'fsdp'), may hold values from -0.15625 to 0.15625
- segment_ids: int32 [32, 1024], P(('dp', 'fsdp')), may hold values from 0 to 3, never falling along the last dimension, each value on 1 to 512 neighbouring positions
- expert_ids: int32 [32768, 2], P(('dp', 'fsdp')), may hold values from 0 to 3, all different within a row; in each aligned block of 1024 rows (0 to 1023, 1024 to 2047, ...) at most 640 rows name the same one
- d_out: bfloat16 [32768, 768], P(('dp', 'fsdp')), may hold values from -6 to 6
Outputs:
- out: bfloat16 [32768, 768], P(('dp', 'fsdp'))
- d_tokens: float32 [32768, 768], P(('dp', 'fsdp'))
- d_w_qkv: float32 [768, 2304], P(('dp', 'fsdp'))
- d_w_attn_out: float32 [768, 768], P(('dp', 'fsdp'))
- d_gain_attn: float32 [768], P(('dp', 'fsdp'))
- d_gain_ffn: float32 [768], P(('dp', 'fsdp'))
- d_rel_bias: float32 [768], P(('dp', 'fsdp'))
- d_router: float32 [768, 4], P(('dp', 'fsdp'))
- d_w_in: float32 [768, 12288], P('dp', 'fsdp')
- d_w_out: float32 [768, 12288], P('dp', 'fsdp')
Inputs may be any that keep to these rules, and one draw needn't show every extreme that they name: `segment_ids`: along a sequence the numbers never fall; each document has 1 to 512 positions, and one has exactly 512. `expert_ids`: each row names 2 different experts. Among the rows of one device (aligned blocks of 1024 rows), no expert is named more than 640 times, a bound that some block reaches.
All inputs are finite; a program needn't handle non-finite values.
Results may differ from a plain program's by a relative error of at most 0.014.
Values may be sent and summed in bfloat16 or wider, within the bound.
No kernel may reach another device: no remote copies, remote signals or barrier semaphores. Data moves between devices by JAX's collectives and lax.ppermute only.
A program may use at most 704 MiB of HBM per device.

v0:
```python
import math

import jax
import jax.numpy as jnp
from jax import lax
from jax.sharding import PartitionSpec as P

HEADS = 12
BUCKETS = 64
MAX_DIST = 128


EPS = 1e-06
NEG = -1e30


def bucket_bounds(bucket_count, max_distance):
    halfway = bucket_count // 2
    bounds = []
    for bucket in range(bucket_count):
        if bucket < halfway:
            bounds.append(bucket)
        else:
            bounds.append(
                int(math.ceil(halfway * (max_distance / halfway) ** ((bucket - halfway) / halfway)))
            )
    return bounds


def buckets_of(distance):
    limits = jnp.array(bucket_bounds(BUCKETS, MAX_DIST), dtype=jnp.int32)
    reached = (distance[:, None] >= limits[None, :]).astype(jnp.int32)
    return jnp.sum(reached, axis=1) - 1


def rms_norm(values, gain_vec):
    return values * lax.rsqrt(jnp.mean(values * values, axis=-1, keepdims=True) + EPS) * gain_vec


def rms_back(values, gain_vec, grad_normed):
    _, pull_back = jax.vjp(rms_norm, values, gain_vec)
    return pull_back(grad_normed)


def bias_cells(bias_rel, length):
    places = jnp.arange(length, dtype=jnp.int32)
    rel_dist = jnp.maximum(places[:, None] - places[None, :], 0)
    return jnp.take(bias_rel.astype(jnp.bfloat16), rel_dist, axis=1)


def block_scores(query_rows, key_rows, segments, row_start, bias_block, scaling):
    block_rows = query_rows.shape[0]
    key_count = key_rows.shape[0]
    raw_scores = (
        jnp.einsum("qhd,khd->hqk", query_rows, key_rows, preferred_element_type=jnp.float32)
        * scaling
    )
    raw_scores = raw_scores + bias_block.astype(jnp.float32)
    query_place = row_start + jnp.arange(block_rows, dtype=jnp.int32)
    key_place = jnp.arange(key_count, dtype=jnp.int32)
    same_doc = (
        segments[row_start : row_start + block_rows][:, None] == segments[:key_count][None, :]
    )
    allowed = (query_place[:, None] >= key_place[None, :]) & same_doc
    return jnp.where(allowed[None], raw_scores, NEG)


def attention_forward(qkv_rows, segment_ids, bias_full, group_heads):
    seq_count, length = segment_ids.shape
    head_count = bias_full.shape[0]
    head_width = qkv_rows.shape[1] // (3 * head_count)
    qkv_parts = qkv_rows.reshape(seq_count, length, 3, head_count, head_width)
    block_rows = min(512, length)
    scaling = head_width ** (-0.5)

    def one_sequence(seq_index, carry):
        mixed_out, log_sums = carry
        sequence = lax.dynamic_index_in_dim(qkv_parts, seq_index, 0, keepdims=False)
        segments = lax.dynamic_index_in_dim(segment_ids, seq_index, 0, keepdims=False)
        for head_start in range(0, head_count, group_heads):
            for row_start in range(0, length, block_rows):
                key_count = row_start + block_rows
                key_rows = sequence[:key_count, 1, head_start : head_start + group_heads]
                value_rows = sequence[:key_count, 2, head_start : head_start + group_heads]
                query_rows = sequence[
                    row_start : row_start + block_rows, 0, head_start : head_start + group_heads
                ]
                bias_block = bias_full[
                    head_start : head_start + group_heads,
                    row_start : row_start + block_rows,
                    :key_count,
                ]
                raw_scores = block_scores(
                    query_rows, key_rows, segments, row_start, bias_block, scaling
                )
                row_peak = jnp.max(raw_scores, axis=2, keepdims=True)
                weights = jnp.exp(raw_scores - row_peak)
                row_total = jnp.sum(weights, axis=2, keepdims=True)
                probs_low = (weights / row_total).astype(jnp.bfloat16)
                block_out = jnp.einsum(
                    "hqk,khd->qhd", probs_low, value_rows, preferred_element_type=jnp.float32
                ).astype(jnp.bfloat16)
                mixed_out = lax.dynamic_update_slice(
                    mixed_out, block_out[None], (seq_index, row_start, head_start, 0)
                )
                block_lse = (row_peak + jnp.log(row_total))[:, :, 0]
                log_sums = lax.dynamic_update_slice(
                    log_sums, block_lse[None], (seq_index, head_start, row_start)
                )
        return (mixed_out, log_sums)

    mixed_out = jnp.zeros((seq_count, length, head_count, head_width), jnp.bfloat16)
    log_sums = jnp.zeros((seq_count, head_count, length), jnp.float32)
    return lax.fori_loop(0, seq_count, one_sequence, (mixed_out, log_sums))


def attention_backward(qkv_rows, segment_ids, bias_full, log_sums, d_mixed, group_heads):
    seq_count, length = segment_ids.shape
    head_count = bias_full.shape[0]
    head_width = qkv_rows.shape[1] // (3 * head_count)
    qkv_parts = qkv_rows.reshape(seq_count, length, 3, head_count, head_width)
    grad_parts = d_mixed.reshape(seq_count, length, head_count, head_width)
    block_rows = min(512, length)
    scaling = head_width ** (-0.5)

    def one_sequence(seq_index, carry):
        d_parts, d_band = carry
        sequence = lax.dynamic_index_in_dim(qkv_parts, seq_index, 0, keepdims=False)
        segments = lax.dynamic_index_in_dim(segment_ids, seq_index, 0, keepdims=False)
        grad_seq = lax.dynamic_index_in_dim(grad_parts, seq_index, 0, keepdims=False)
        lse_seq = lax.dynamic_index_in_dim(log_sums, seq_index, 0, keepdims=False)
        for head_start in range(0, head_count, group_heads):
            d_keys = jnp.zeros((length, group_heads, head_width), jnp.float32)
            d_values = jnp.zeros((length, group_heads, head_width), jnp.float32)
            for row_start in range(0, length, block_rows):
                key_count = row_start + block_rows
                key_rows = sequence[:key_count, 1, head_start : head_start + group_heads]
                value_rows = sequence[:key_count, 2, head_start : head_start + group_heads]
                query_rows = sequence[
                    row_start : row_start + block_rows, 0, head_start : head_start + group_heads
                ]
                grad_rows = grad_seq[
                    row_start : row_start + block_rows, head_start : head_start + group_heads
                ]
                bias_block = bias_full[
                    head_start : head_start + group_heads,
                    row_start : row_start + block_rows,
                    :key_count,
                ]
                raw_scores = block_scores(
                    query_rows, key_rows, segments, row_start, bias_block, scaling
                )
                block_lse = lse_seq[
                    head_start : head_start + group_heads, row_start : row_start + block_rows
                ]
                probs_f = jnp.exp(raw_scores - block_lse[:, :, None])
                d_probs = jnp.einsum(
                    "qhd,khd->hqk", grad_rows, value_rows, preferred_element_type=jnp.float32
                )
                inner_sum = jnp.sum(probs_f * d_probs, axis=2, keepdims=True)
                d_scores = (probs_f * (d_probs - inner_sum)).astype(jnp.bfloat16)
                d_query = (
                    jnp.einsum(
                        "hqk,khd->qhd", d_scores, key_rows, preferred_element_type=jnp.float32
                    )
                    * scaling
                )
                key_grad = (
                    jnp.einsum(
                        "hqk,qhd->khd", d_scores, query_rows, preferred_element_type=jnp.float32
                    )
                    * scaling
                )
                value_grad = jnp.einsum(
                    "hqk,qhd->khd",
                    probs_f.astype(jnp.bfloat16),
                    grad_rows,
                    preferred_element_type=jnp.float32,
                )
                d_keys = d_keys.at[:key_count].add(key_grad)
                d_values = d_values.at[:key_count].add(value_grad)
                d_parts = lax.dynamic_update_slice(
                    d_parts, d_query[None, :, None], (seq_index, row_start, 0, head_start, 0)
                )
                d_band = d_band.at[
                    head_start : head_start + group_heads,
                    row_start : row_start + block_rows,
                    :key_count,
                ].add(d_scores.astype(jnp.float32))
            key_value = jnp.stack([d_keys, d_values], axis=1)
            d_parts = lax.dynamic_update_slice(
                d_parts, key_value[None], (seq_index, 0, 1, head_start, 0)
            )
        return (d_parts, d_band)

    d_parts = jnp.zeros((seq_count, length, 3, head_count, head_width), jnp.float32)
    d_band = jnp.zeros((head_count, length, length), jnp.float32)
    return lax.fori_loop(0, seq_count, one_sequence, (d_parts, d_band))


def band_to_table(d_band, length):
    head_count = d_band.shape[0]
    padded_width = 2 * length - 1
    padded = jnp.pad(d_band, ((0, 0), (0, 0), (length - 1, 0))).reshape(
        head_count, length * padded_width
    )
    padded = jnp.pad(padded, ((0, 0), (0, length)))
    skewed = padded.reshape(head_count, length, padded_width + 1)
    by_offset = jnp.sum(skewed[:, :, :length], axis=1)
    distance = length - 1 - jnp.arange(length, dtype=jnp.int32)
    offset_hot = (
        buckets_of(distance)[:, None] == jnp.arange(BUCKETS, dtype=jnp.int32)[None, :]
    ).astype(jnp.float32)
    return jnp.dot(by_offset, offset_hot, precision=lax.Precision.HIGHEST)


def local(
    tokens_in,
    w_qkv,
    w_attn_out,
    gain_attn,
    gain_ffn,
    rel_bias,
    router,
    w_in,
    w_out,
    segment_ids,
    expert_ids,
    d_out,
):
    tok_rows, width = tokens_in.shape
    top_count = expert_ids.shape[1]
    fsdp_size = lax.axis_size("fsdp")
    expert_count = fsdp_size // 2
    capacity = min(tok_rows, tok_rows * top_count * 5 // (4 * expert_count))
    seq_length = segment_ids.shape[1]
    group_heads = math.gcd(HEADS, 4)
    bucket_hot = (
        buckets_of(jnp.arange(seq_length, dtype=jnp.int32))[:, None]
        == jnp.arange(BUCKETS, dtype=jnp.int32)[None, :]
    ).astype(jnp.float32)

    def make_bias(rel_flat):
        bias_table = rel_flat.astype(jnp.float32).reshape(HEADS, BUCKETS)
        return bias_cells(
            jnp.dot(bias_table, bucket_hot.T, precision=lax.Precision.HIGHEST), seq_length
        )

    full_qkv, full_attn, full_router, full_gain_a, full_gain_f, full_rel = (
        lax.all_gather(w_qkv, ("dp", "fsdp"), axis=0, tiled=True),
        lax.all_gather(w_attn_out, ("dp", "fsdp"), axis=0, tiled=True),
        lax.all_gather(router, ("dp", "fsdp"), axis=0, tiled=True),
        lax.all_gather(gain_attn, ("dp", "fsdp"), axis=0, tiled=True),
        lax.all_gather(gain_ffn, ("dp", "fsdp"), axis=0, tiled=True),
        lax.all_gather(rel_bias, ("dp", "fsdp"), axis=0, tiled=True),
    )
    full_in, full_second = (
        lax.all_gather(w_in, "dp", axis=0, tiled=True),
        lax.all_gather(w_out, "dp", axis=0, tiled=True),
    )
    tokens_f32 = tokens_in.astype(jnp.float32)
    normed_attn = rms_norm(tokens_f32, full_gain_a.astype(jnp.float32)).astype(jnp.bfloat16)
    qkv_rows = jnp.dot(normed_attn, full_qkv, preferred_element_type=jnp.float32).astype(
        jnp.bfloat16
    )
    mixed_heads, log_sums = attention_forward(
        qkv_rows, segment_ids, make_bias(full_rel), group_heads
    )
    mixed_rows = mixed_heads.reshape(tok_rows, width)
    residual = tokens_f32 + jnp.dot(mixed_rows, full_attn, preferred_element_type=jnp.float32)
    normed_ffn = rms_norm(residual, full_gain_f.astype(jnp.float32)).astype(jnp.bfloat16)
    logits = jnp.dot(normed_ffn, full_router, preferred_element_type=jnp.float32)
    chosen = jnp.take_along_axis(logits, expert_ids, axis=1)
    gates_soft = jax.nn.softmax(chosen, axis=1)
    assign_count = tok_rows * top_count
    flat_ids = expert_ids.reshape(assign_count)
    expert_hot = (flat_ids[:, None] == jnp.arange(expert_count, dtype=jnp.int32)[None, :]).astype(
        jnp.int32
    )
    earlier = jnp.cumsum(expert_hot, axis=0) - 1
    slot_rank = jnp.sum(expert_hot * earlier, axis=1)
    dest_slot = flat_ids * capacity + slot_rank
    slot_owner = (
        jnp.full((expert_count * capacity,), assign_count, jnp.int32)
        .at[dest_slot]
        .set(jnp.arange(assign_count, dtype=jnp.int32))
    )
    slot_token = slot_owner // top_count
    padded_rows = jnp.concatenate([normed_ffn, jnp.zeros((1, width), jnp.bfloat16)], axis=0)
    expert_rows = padded_rows[slot_token].reshape(expert_count, 1, capacity, width)
    send_rows = jnp.broadcast_to(expert_rows, (expert_count, 2, capacity, width)).reshape(
        fsdp_size, capacity, width
    )
    received = lax.all_to_all(send_rows, "fsdp", split_axis=0, concat_axis=0, tiled=True)
    rows_in = received.reshape(fsdp_size * capacity, width)
    pre_act = jnp.dot(rows_in, full_in, preferred_element_type=jnp.float32)
    hidden = jax.nn.gelu(pre_act, approximate=True).astype(jnp.bfloat16)
    made = jnp.einsum("mf,df->md", hidden, full_second, preferred_element_type=jnp.float32).astype(
        jnp.bfloat16
    )
    returned = lax.all_to_all(
        made.reshape(fsdp_size, capacity, width), "fsdp", split_axis=0, concat_axis=0, tiled=True
    )
    summed = jnp.sum(returned.astype(jnp.float32).reshape(expert_count, 2, capacity, width), axis=1)
    picked_f = summed.reshape(expert_count * capacity, width)[dest_slot].reshape(
        tok_rows, top_count, width
    )
    block_out = (residual + jnp.sum(gates_soft[:, :, None] * picked_f, axis=1)).astype(jnp.bfloat16)
    back_qkv, back_attn, back_router, back_gain_a, back_gain_f, back_rel = (
        lax.all_gather(w_qkv, ("dp", "fsdp"), axis=0, tiled=True),
        lax.all_gather(w_attn_out, ("dp", "fsdp"), axis=0, tiled=True),
        lax.all_gather(router, ("dp", "fsdp"), axis=0, tiled=True),
        lax.all_gather(gain_attn, ("dp", "fsdp"), axis=0, tiled=True),
        lax.all_gather(gain_ffn, ("dp", "fsdp"), axis=0, tiled=True),
        lax.all_gather(rel_bias, ("dp", "fsdp"), axis=0, tiled=True),
    )
    back_in, back_second = (
        lax.all_gather(w_in, "dp", axis=0, tiled=True),
        lax.all_gather(w_out, "dp", axis=0, tiled=True),
    )
    grad_out = d_out.astype(jnp.float32)
    d_gates = jnp.sum(grad_out[:, None, :] * picked_f, axis=2)
    d_picked = (
        (gates_soft[:, :, None] * grad_out[:, None, :])
        .astype(jnp.bfloat16)
        .reshape(assign_count, width)
    )
    d_padded = jnp.concatenate([d_picked, jnp.zeros((1, width), jnp.bfloat16)], axis=0)
    d_expert_rows = d_padded[slot_owner].reshape(expert_count, 1, capacity, width)
    d_send = jnp.broadcast_to(d_expert_rows, (expert_count, 2, capacity, width)).reshape(
        fsdp_size, capacity, width
    )
    d_received = lax.all_to_all(d_send, "fsdp", split_axis=0, concat_axis=0, tiled=True)
    grad_rows = d_received.reshape(fsdp_size * capacity, width)
    pre_again = jnp.dot(rows_in, back_in, preferred_element_type=jnp.float32)
    d_hidden = jnp.dot(grad_rows, back_second, preferred_element_type=jnp.float32)
    _, gelu_pull = jax.vjp(lambda value_in: jax.nn.gelu(value_in, approximate=True), pre_again)
    d_pre = gelu_pull(d_hidden)[0].astype(jnp.bfloat16)
    d_rows = jnp.einsum("mf,df->md", d_pre, back_in, preferred_element_type=jnp.float32).astype(
        jnp.bfloat16
    )
    piece = rows_in
    d_w_in = lax.psum_scatter(
        jnp.einsum("md,mf->df", piece, d_pre, preferred_element_type=jnp.float32).astype(
            jnp.bfloat16
        ),
        "dp",
        scatter_dimension=0,
        tiled=True,
    ).astype(jnp.float32)
    piece = grad_rows
    d_w_out = lax.psum_scatter(
        jnp.einsum("md,mf->df", piece, hidden, preferred_element_type=jnp.float32).astype(
            jnp.bfloat16
        ),
        "dp",
        scatter_dimension=0,
        tiled=True,
    ).astype(jnp.float32)
    d_returned = lax.all_to_all(
        d_rows.reshape(fsdp_size, capacity, width), "fsdp", split_axis=0, concat_axis=0, tiled=True
    )
    d_slots = jnp.sum(
        d_returned.astype(jnp.float32).reshape(expert_count, 2, capacity, width), axis=1
    )
    d_from_experts = jnp.sum(
        d_slots.reshape(expert_count * capacity, width)[dest_slot].reshape(
            tok_rows, top_count, width
        ),
        axis=1,
    )
    inner_gate = jnp.sum(gates_soft * d_gates, axis=1, keepdims=True)
    d_chosen = gates_soft * (d_gates - inner_gate)
    route_hot = (
        expert_ids[:, :, None] == jnp.arange(expert_count, dtype=jnp.int32)[None, None, :]
    ).astype(jnp.float32)
    d_logits = jnp.sum(route_hot * d_chosen[:, :, None], axis=1)
    router_f32 = back_router.astype(jnp.float32)
    d_normed_ffn = d_from_experts + jnp.dot(d_logits, router_f32.T, precision=lax.Precision.HIGHEST)
    d_router = jnp.dot(normed_ffn.astype(jnp.float32).T, d_logits, precision=lax.Precision.HIGHEST)
    d_resid_norm, d_gain_ffn = rms_back(residual, back_gain_f.astype(jnp.float32), d_normed_ffn)
    d_residual = grad_out + d_resid_norm
    d_branch = d_residual.astype(jnp.bfloat16)
    d_w_attn_out = jnp.dot(mixed_rows.T, d_branch, preferred_element_type=jnp.float32)
    d_mixed = jnp.dot(d_branch, back_attn.T, preferred_element_type=jnp.float32).astype(
        jnp.bfloat16
    )
    d_parts, d_band = attention_backward(
        qkv_rows, segment_ids, make_bias(back_rel), log_sums, d_mixed, group_heads
    )
    d_qkv = d_parts.reshape(tok_rows, 3 * width).astype(jnp.bfloat16)
    d_w_qkv = jnp.dot(normed_attn.T, d_qkv, preferred_element_type=jnp.float32)
    d_normed_attn = jnp.dot(d_qkv, back_qkv.T, preferred_element_type=jnp.float32)
    d_tokens_norm, d_gain_attn = rms_back(
        tokens_f32, back_gain_a.astype(jnp.float32), d_normed_attn
    )
    d_tokens = d_residual + d_tokens_norm
    d_table = band_to_table(d_band, seq_length).reshape(HEADS * BUCKETS)
    own_qkv, own_attn, own_router, own_gain_a, own_gain_f, own_rel = (
        lax.psum_scatter(d_w_qkv, ("dp", "fsdp"), scatter_dimension=0, tiled=True),
        lax.psum_scatter(d_w_attn_out, ("dp", "fsdp"), scatter_dimension=0, tiled=True),
        lax.psum_scatter(d_router, ("dp", "fsdp"), scatter_dimension=0, tiled=True),
        lax.psum_scatter(d_gain_attn, ("dp", "fsdp"), scatter_dimension=0, tiled=True),
        lax.psum_scatter(d_gain_ffn, ("dp", "fsdp"), scatter_dimension=0, tiled=True),
        lax.psum_scatter(d_table, ("dp", "fsdp"), scatter_dimension=0, tiled=True),
    )
    return (
        block_out,
        d_tokens,
        own_qkv,
        own_attn,
        own_gain_a,
        own_gain_f,
        own_rel,
        own_router,
        d_w_in,
        d_w_out,
    )


def solution(mesh):
    placed = (
        P(("dp", "fsdp"), None),
        P(("dp", "fsdp"), None),
        P(("dp", "fsdp"), None),
        P(("dp", "fsdp")),
        P(("dp", "fsdp")),
        P(("dp", "fsdp")),
        P(("dp", "fsdp"), None),
        P("dp", "fsdp"),
        P("dp", "fsdp"),
        P(("dp", "fsdp"), None),
        P(("dp", "fsdp"), None),
        P(("dp", "fsdp"), None),
    )
    return jax.shard_map(
        local,
        mesh=mesh,
        in_specs=placed,
        out_specs=(
            P(("dp", "fsdp"), None),
            P(("dp", "fsdp"), None),
            P(("dp", "fsdp"), None),
            P(("dp", "fsdp"), None),
            P(("dp", "fsdp")),
            P(("dp", "fsdp")),
            P(("dp", "fsdp")),
            P(("dp", "fsdp"), None),
            P("dp", "fsdp"),
            P("dp", "fsdp"),
        ),
        check_vma=False,
    )
```

profile of v0, /device:TPU:0, one launch (start us, length us, event | category | flops | bytes accessed | tf_op | source)
XLA Modules:
  0.0 7786.2 jit_solution(12302138780284235626)
XLA Ops:
  17.2 42.4 all-reduce.22
  66.7 3983.3 %gather_fusion.5 = bf16[1048576,12]{1,0:T(8,128)(2,1)} fusion(bf16[12,1024]{0,1:T(8,128)(2,1)S(1)} %copy.275, s32[1048576]{0:T(1024)} %broadcast_clamp_fusion), kind=kCustom, calls=%fused_computation.clone | custom fusion | bytes 54525952 | tf_op jit(solution)/shard_map/jit(_take)/gather | solution.py:48
  4050.0 238.0 %copy.277 = bf16[1024,1024,12]{0,1,2:T(8,128)(2,1)} copy(bf16[1024,1024,12]{2,1,0:T(8,128)(2,1)} %bitcast.6) | data formatting | bytes 50331648 | tf_op jit(solution)/shard_map/jit(_take)/gather | solution.py:48
  4302.8 21.7 select_bitcast_fusion
  4434.4 105.3 %all-gather = bf16[32,24,4]{1,2,0:T(4,128)(2,1)S(1)} all-gather(bf16[1,24,4]{1,2,0:T(4,128)(2,1)S(1)} %bitcast.423), channel_id=1, replica_groups=mesh['dp'=4,'fsdp'=8] {'dp','fsdp'}, dimensions={0}, use_global_device_ids=true | all-gather | bytes 6336 | tf_op jit(solution)/shard_map/all_gather | solution.py:252
  4585.3 21.4 fusion.187
  4606.7 28.6 all-gather.12.cloned.1.call-done
  4635.3 37.8 all-to-all-done.2
  4673.1 35.4 fusion.6
  4738.7 24.5 convolution_convert_fusion.1
  4763.2 56.8 all-to-all-done.3
  5037.7 40.7 scatter-add.56
  5182.7 49.0 copy.356
  5231.7 50.3 pad.93.clone
  5281.9 139.2 %reshape.1308 = f32[25153536]{0:T(1024)} reshape(f32[12,1024,2047]{2,1,0:T(8,128)} %pad.93.clone) | data formatting | bytes 201228288
  5421.1 2024.4 %while.43 = (u32[]{:T(128)}, f32[25153536]{0:T(1024)}, f32[1,12,2096128]{2,1,0:T(8,128)}, u32[]{}, u32[]{}, /*index=5*/u32[]{}, u32[]{}, u32[]{}) while((u32[]{:T(128)}, f32[25153536]{0:T(1024)}, f32[1,12,2096128]{2,1,0:T(8,128)}, u32[]{}, u32[]{}, /*index=5*/u32[]{}, u32[]{}, u32[]{}) %tuple.187), condition=%wide.cond, body=%wide.body.sunk | while | flops 9 | bytes 50307256
  5433.9 155.9 %dynamic-update-slice.62 = f32[1,12,2096128]{2,1,0:T(8,128)} dynamic-update-slice(f32[1,12,2096128]{2,1,0:T(8,128)} %get-tuple-element.520, f32[1,1,2096128]{2,1,0:T(1,128)} %reshape.1311, u32[]{:T(128)S(6)} %multiply.55, u32[]{:T(128)S(6)} %multiply.57, u32[]{} %constant.987..sunk) | dynamic-update-slice | bytes 16769028
  5602.5 155.9 %dynamic-update-slice.62 = f32[1,12,2096128]{2,1,0:T(8,128)} dynamic-update-slice(f32[1,12,2096128]{2,1,0:T(8,128)} %get-tuple-element.520, f32[1,1,2096128]{2,1,0:T(1,128)} %reshape.1311, u32[]{:T(128)S(6)} %multiply.55, u32[]{:T(128)S(6)} %multiply.57, u32[]{} %constant.987..sunk) | dynamic-update-slice | bytes 16769028
  5771.2 155.9 %dynamic-update-slice.62 = f32[1,12,2096128]{2,1,0:T(8,128)} dynamic-update-slice(f32[1,12,2096128]{2,1,0:T(8,128)} %get-tuple-element.520, f32[1,1,2096128]{2,1,0:T(1,128)} %reshape.1311, u32[]{:T(128)S(6)} %multiply.55, u32[]{:T(128)S(6)} %multiply.57, u32[]{} %constant.987..sunk) | dynamic-update-slice | bytes 16769028
  5939.9 155.9 %dynamic-update-slice.62 = f32[1,12,2096128]{2,1,0:T(8,128)} dynamic-update-slice(f32[1,12,2096128]{2,1,0:T(8,128)} %get-tuple-element.520, f32[1,1,2096128]{2,1,0:T(1,128)} %reshape.1311, u32[]{:T(128)S(6)} %multiply.55, u32[]{:T(128)S(6)} %multiply.57, u32[]{} %constant.987..sunk) | dynamic-update-slice | bytes 16769028
  6108.6 155.9 %dynamic-update-slice.62 = f32[1,12,2096128]{2,1,0:T(8,128)} dynamic-update-slice(f32[1,12,2096128]{2,1,0:T(8,128)} %get-tuple-element.520, f32[1,1,2096128]{2,1,0:T(1,128)} %reshape.1311, u32[]{:T(128)S(6)} %multiply.55, u32[]{:T(128)S(6)} %multiply.57, u32[]{} %constant.987..sunk) | dynamic-update-slice | bytes 16769028
  6277.3 155.9 %dynamic-update-slice.62 = f32[1,12,2096128]{2,1,0:T(8,128)} dynamic-update-slice(f32[1,12,2096128]{2,1,0:T(8,128)} %get-tuple-element.520, f32[1,1,2096128]{2,1,0:T(1,128)} %reshape.1311, u32[]{:T(128)S(6)} %multiply.55, u32[]{:T(128)S(6)} %multiply.57, u32[]{} %constant.987..sunk) | dynamic-update-slice | bytes 16769028
  6446.0 155.9 %dynamic-update-slice.62 = f32[1,12,2096128]{2,1,0:T(8,128)} dynamic-update-slice(f32[1,12,2096128]{2,1,0:T(8,128)} %get-tuple-element.520, f32[1,1,2096128]{2,1,0:T(1,128)} %reshape.1311, u32[]{:T(128)S(6)} %multiply.55, u32[]{:T(128)S(6)} %multiply.57, u32[]{} %constant.987..sunk) | dynamic-update-slice | bytes 16769028
  6614.7 155.9 %dynamic-update-slice.62 = f32[1,12,2096128]{2,1,0:T(8,128)} dynamic-update-slice(f32[1,12,2096128]{2,1,0:T(8,128)} %get-tuple-element.520, f32[1,1,2096128]{2,1,0:T(1,128)} %reshape.1311, u32[]{:T(128)S(6)} %multiply.55, u32[]{:T(128)S(6)} %multiply.57, u32[]{} %constant.987..sunk) | dynamic-update-slice | bytes 16769028
  6783.3 156.0 %dynamic-update-slice.62 = f32[1,12,2096128]{2,1,0:T(8,128)} dynamic-update-slice(f32[1,12,2096128]{2,1,0:T(8,128)} %get-tuple-element.520, f32[1,1,2096128]{2,1,0:T(1,128)} %reshape.1311, u32[]{:T(128)S(6)} %multiply.55, u32[]{:T(128)S(6)} %multiply.57, u32[]{} %constant.987..sunk) | dynamic-update-slice | bytes 16769028
  6952.1 156.0 %dynamic-update-slice.62 = f32[1,12,2096128]{2,1,0:T(8,128)} dynamic-update-slice(f32[1,12,2096128]{2,1,0:T(8,128)} %get-tuple-element.520, f32[1,1,2096128]{2,1,0:T(1,128)} %reshape.1311, u32[]{:T(128)S(6)} %multiply.55, u32[]{:T(128)S(6)} %multiply.57, u32[]{} %constant.987..sunk) | dynamic-update-slice | bytes 16769028
  7120.8 156.0 %dynamic-update-slice.62 = f32[1,12,2096128]{2,1,0:T(8,128)} dynamic-update-slice(f32[1,12,2096128]{2,1,0:T(8,128)} %get-tuple-element.520, f32[1,1,2096128]{2,1,0:T(1,128)} %reshape.1311, u32[]{:T(128)S(6)} %multiply.55, u32[]{:T(128)S(6)} %multiply.57, u32[]{} %constant.987..sunk) | dynamic-update-slice | bytes 16769028
  7289.5 156.0 %dynamic-update-slice.62 = f32[1,12,2096128]{2,1,0:T(8,128)} dynamic-update-slice(f32[1,12,2096128]{2,1,0:T(8,128)} %get-tuple-element.520, f32[1,1,2096128]{2,1,0:T(1,128)} %reshape.1311, u32[]{:T(128)S(6)} %multiply.55, u32[]{:T(128)S(6)} %multiply.57, u32[]{} %constant.987..sunk) | dynamic-update-slice | bytes 16769028
  7445.5 85.8 %pad.94 = f32[12,2097152]{1,0:T(8,128)} pad(f32[12,2096128]{1,0:T(8,128)} %bitcast.277, f32[]{:T(128)} %constant.691.clone.1), padding=0_0x0_1024 | pad | bytes 201277440 | tf_op jit(solution)/shard_map/jit(_pad)/pad | solution.py:207
  7531.3 108.8 %copy.359 = f32[2,8,1024,2048]{3,2,1,0:T(8,128)} copy(f32[2,8,1024,2048]{3,1,2,0:T(8,128)} %bitcast.117) | data formatting | bytes 268435456
  7640.1 64.7 slice.857
  7733.9 37.2 all-reduce.21
  (473 shorter events, 726.2 us)
Async XLA Ops:
  8.0 51.7 copy-start.103
  8.1 4317.6 %all-gather.6.cloned.1.call-start = ((), (), s32[]{:S(2)}) async-start(), calls=%async_computation.8 | async-start | bytes 3649536 | tf_op jit(solution)/shard_map/all_gather | solution.py:250
  8.8 4387.1 %all-gather.8.cloned.1.call-start = ((), (), s32[]{:S(2)}) async-start(), calls=%async_computation.9 | async-start | bytes 1216512 | tf_op jit(solution)/shard_map/all_gather | solution.py:251
  4050.0 241.2 %copy-start.101 = (bf16[768]{0:T(1024)(128)(2,1)S(1)}, bf16[768]{0:T(1024)(128)(2,1)}, u32[]{:S(2)}) copy-start(bf16[768]{0:T(1024)(128)(2,1)} %get-tuple-element.437) | copy-start | bytes 4612
  4050.0 241.2 %copy-start.24 = (bf16[1024,768]{1,0:T(8,128)(2,1)S(1)}, bf16[1024,768]{1,0:T(8,128)(2,1)}, u32[]{:S(2)}) copy-start(bf16[1024,768]{1,0:T(8,128)(2,1)} %param.64) | copy-start | bytes 4718596
  4050.0 241.6 %copy-start.88 = (s32[1,1024]{1,0:T(1,128)S(1)}, s32[1,1024]{1,0:T(1,128)}, u32[]{:S(2)}) copy-start(s32[1,1024]{1,0:T(1,128)} %param.73) | copy-start | bytes 12292
  4050.0 242.2 %copy-start.100 = (bf16[768]{0:T(1024)(128)(2,1)S(1)}, bf16[768]{0:T(1024)(128)(2,1)}, u32[]{:S(2)}) copy-start(bf16[768]{0:T(1024)(128)(2,1)} %get-tuple-element.438) | copy-start | bytes 4612
  4050.0 242.2 %copy-start.70 = (s32[1024,2]{0,1:T(2,128)S(1)}, s32[1024,2]{0,1:T(2,128)}, u32[]{:S(2)}) copy-start(s32[1024,2]{0,1:T(2,128)} %broadcast_multiply_fusion) | copy-start | bytes 24580
  4291.2 34.5 copy-start.89
  4291.6 34.1 copy-start.92
  4291.8 51.5 copy-start.28
  4292.2 107.2 %copy-start.48 = (f32[768]{0:T(1024)}, f32[768]{0:T(1024)S(1)}, u32[]{:S(2)}) copy-start(f32[768]{0:T(1024)S(1)} %convert_element_type.300) | copy-start | bytes 9220
  4294.5 30.1 copy-start.72
  4343.3 29.2 copy-start.3
  4349.7 31.4 copy-start.57
  4401.3 139.1 %copy-start.12 = (bf16[1024,768]{1,0:T(8,128)(2,1)}, bf16[1024,768]{1,0:T(8,128)(2,1)S(1)}, u32[]{:S(2)}) copy-start(bf16[1024,768]{1,0:T(8,128)(2,1)S(1)} %multiply_convert_fusion.8) | copy-start | bytes 4718596
  4415.8 158.2 %all-to-all-start = ((bf16[8,640,768]{2,1,0:T(8,128)(2,1)}), bf16[8,640,768]{2,1,0:T(8,128)(2,1)}, u32[]{:S(2)}, u32[]{:S(2)}) async-start(bf16[8,640,768]{2,1,0:T(8,128)(2,1)} %bitcast.363), calls=%async_computation | async-start | bytes 15728640 | tf_op jit(solution)/shard_map/all_to_all | solution.py:294
  4420.8 164.5 %all-gather.10.cloned.1.call-start = ((), (), s32[]{:S(2)}) async-start(), calls=%async_computation.10 | async-start | bytes 2949120 | tf_op jit(solution)/shard_map/all_gather | solution.py:258
  4425.7 114.2 %copy-start.31 = (s32[1024,2]{0,1:T(2,128)S(1)}, s32[1024,2]{0,1:T(2,128)}, u32[]{:S(2)}) copy-start(s32[1024,2]{0,1:T(2,128)} %param.74) | copy-start | bytes 24580
  4579.7 93.4 %all-to-all-start.2 = ((bf16[8,640,768]{2,1,0:T(8,128)(2,1)}), bf16[8,640,768]{2,1,0:T(8,128)(2,1)}, u32[]{:S(2)}, u32[]{:S(2)}) async-start(bf16[8,640,768]{2,1,0:T(8,128)(2,1)} %bitcast.364), calls=%async_computation.2 | async-start | bytes 15728640 | tf_op jit(solution)/shard_map/all_to_all | solution.py:333
  4584.7 50.7 all-gather.12.cloned.1.call-start
  4673.1 35.4 copy-start.105
  4726.5 93.5 %all-to-all-start.3 = ((bf16[8,640,768]{2,1,0:T(8,128)(2,1)}), bf16[8,640,768]{2,1,0:T(8,128)(2,1)}, u32[]{:S(2)}, u32[]{:S(2)}) async-start(bf16[8,640,768]{2,1,0:T(8,128)(2,1)} %bitcast.399), calls=%async_computation.3 | async-start | bytes 15728640 | tf_op jit(solution)/shard_map/all_to_all | solution.py:360
  4820.1 93.6 %all-to-all-start.1 = ((bf16[8,640,768]{2,1,0:T(8,128)(2,1)}), bf16[8,640,768]{2,1,0:T(8,128)(2,1)}, u32[]{:S(2)}, u32[]{:S(2)}) async-start(bf16[8,640,768]{2,1,0:T(8,128)(2,1)} %bitcast.398), calls=%async_computation.1 | async-start | bytes 15728640 | tf_op jit(solution)/shard_map/all_to_all | solution.py:301
  4825.2 353.0 %reduce-scatter.10.cloned.1.call-start = ((), (), s32[]{:S(2)}) async-start(), calls=%async_computation.14 | async-start | bytes 2949120 | tf_op jit(solution)/shard_map/reduce_scatter | solution.py:343
  4843.9 336.6 %reduce-scatter.12.cloned.1.call-start = ((), (), s32[]{:S(2)}) async-start(), calls=%async_computation.15 | async-start | bytes 2949120 | tf_op jit(solution)/shard_map/reduce_scatter | solution.py:352
  4864.8 2913.6 %reduce-scatter.8.cloned.1.call-start = ((), (), s32[]{:S(2)}) async-start(), calls=%async_computation.13 | async-start | bytes 2433024 | tf_op jit(solution)/shard_map/reduce_scatter | solution.py:401
  4984.2 34.7 copy-start.22
  5037.7 40.7 copy-start.39
  5138.4 2640.0 %reduce-scatter.6.cloned.1.call-start = ((), (), s32[]{:S(2)}) async-start(), calls=%async_computation.12 | async-start | bytes 7299072 | tf_op jit(solution)/shard_map/reduce_scatter | solution.py:400
  7723.9 49.6 copy-start.56
  7723.9 49.6 copy-start.20
  (101 other events, 882.1 us)
Sparse Core Ops, SparseCore 0:
  11.8 62.8 all-gather.5
  77.6 52.8 all-gather.7
Sparse Core Ops, SparseCore 1:
  4422.8 50.3 all-gather.9
  4586.7 48.6 all-gather.11
  4844.0 46.1 reduce-scatter.9
  4892.5 47.1 reduce-scatter.11
  5138.4 95.2 reduce-scatter.7
  5240.9 117.9 reduce-scatter.5
where the time goes:
time: 7930 us; the launch traced here: 7790 us
  local copies, waits for them, and re-layouts  6930 us (87%)
  matrix products  295 us (4%)
  other arithmetic  191 us (2%)
  blocking collectives  185 us (2%)
  waiting for transfers between devices  144 us (2%)
    gather x2, local copies, waits for them, and re-layouts, bias_cells(): return jnp.take(bias_rel.astype(jnp.bfloat16), rel_dist, axis=1)  4220 us
    unnamed x294, local copies, waits for them, and re-layouts  2340 us
  transfers between devices with their start and end apart: 12, of which 4 were waited for; matrix products, arithmetic and copies ran while one was open for 94% of the time, Pallas kernels for 0%

commit v1 on v0

v1 whole, which is shorter than its diff:
```python
import functools
import math

import jax
import jax.numpy as jnp
from jax import lax
from jax.experimental import pallas as pl
from jax.experimental.pallas import tpu as pltpu
from jax.sharding import PartitionSpec as P

NEG = -1e30
BLK = 256
SPAN = 2
F32 = jnp.float32
BF16 = jnp.bfloat16
LIGHT = pl.CostEstimate(flops=1000, bytes_accessed=1000, transcendentals=0)


def dot_nt(a, b):
    return lax.dot_general(a, b, (((1,), (1,)), ((), ())), preferred_element_type=F32)


def dot_nn(a, b):
    return lax.dot_general(a, b, (((1,), (0,)), ((), ())), preferred_element_type=F32)


def fill_masks(mask, seg_row, seg_col, blocks):
    key_place = lax.broadcasted_iota(jnp.int32, (BLK, BLK), 0)
    row_place = lax.broadcasted_iota(jnp.int32, (BLK, BLK), 1)
    for kb in range(blocks):
        keys = seg_col[kb * BLK : (kb + 1) * BLK, :]
        for step in range(min(SPAN + 1, blocks - kb)):
            rows = seg_row[:, (kb + step) * BLK : (kb + step + 1) * BLK]
            seen = keys == rows
            if step == 0:
                seen = seen & (row_place >= key_place)
            mask[kb, step] = jnp.where(seen, 0.0, NEG)


def bias_tiles(near_row, far_value):
    key_place = lax.broadcasted_iota(jnp.int32, (BLK, BLK), 0)
    row_place = lax.broadcasted_iota(jnp.int32, (BLK, BLK), 1)
    rolled = pltpu.roll(
        jnp.broadcast_to(near_row, (BLK, BLK)), 0, 1, stride=1, stride_axis=0
    )
    return rolled, jnp.where(row_place < key_place, rolled, far_value)


def head_lanes(values, half):
    lane = lax.broadcasted_iota(jnp.int32, values.shape, 1)
    keep = (lane >= 64) if half else (lane < 64)
    return jnp.where(keep, values, jnp.zeros_like(values))


def attn_fwd_kernel(
    far_ref, q_ref, k_ref, v_ref, near_ref, seg_row, seg_col, *rest
):
    o_ref, lse_ref, mask, turned = rest[-4:]
    pair = pl.program_id(0)
    length = q_ref.shape[0]
    blocks = length // BLK

    @pl.when(pair == 0)
    def _():
        fill_masks(mask, seg_row, seg_col, blocks)

    v_turned = v_ref[...].T
    ones = jnp.ones((16, length), BF16)
    for half in range(2):
        far_value = far_ref[pair * 2 + half]
        diag, below = bias_tiles(near_ref[0, half : half + 1, :], far_value)
        keys = head_lanes(k_ref[...], half)
        values = jnp.concatenate([v_turned[64 * half : 64 * half + 64], ones], axis=0)
        for a in range(blocks):
            first = max(0, a - SPAN)
            q_rows = q_ref[a * BLK : (a + 1) * BLK, :] * jnp.asarray(0.125, BF16)
            parts = []
            for kb in range(first, a + 1):
                part = dot_nt(keys[kb * BLK : (kb + 1) * BLK], q_rows)
                bias = (diag, below, far_value)[a - kb]
                parts.append(part + bias + mask[kb, a - kb])
            peak = functools.reduce(
                jnp.maximum, [jnp.max(part, axis=0, keepdims=True) for part in parts]
            )
            weights = jnp.concatenate(
                [jnp.exp(part - peak).astype(BF16) for part in parts], axis=0
            )
            made = dot_nn(values[:, first * BLK : (a + 1) * BLK], weights)
            total = made[64:65]
            turned[64 * half : 64 * half + 64, a * BLK : (a + 1) * BLK] = made[:64] / total
            lse_ref[0, half : half + 1, a * BLK : (a + 1) * BLK] = peak + jnp.log(total)
    o_ref[...] = turned[...].T.astype(BF16)


def attn_bwd_kernel(
    far_ref, q_ref, k_ref, v_ref, g_ref, o_ref, lse_ref, near_ref, seg_row, seg_col, *rest
):
    d_ref, near_grad, far_grad, mask, turned = rest[-5:]
    pair = pl.program_id(0)
    length = q_ref.shape[0]
    blocks = length // BLK

    @pl.when(pair == 0)
    def _():
        fill_masks(mask, seg_row, seg_col, blocks)

    scaled = q_ref[...] * jnp.asarray(0.125, BF16)
    k_turned = k_ref[...].T
    ones = jnp.ones((16, length), BF16)
    inner = (g_ref[...].astype(F32) * o_ref[...].astype(F32)).T
    key_place = lax.broadcasted_iota(jnp.int32, (BLK, BLK), 0)
    row_place = lax.broadcasted_iota(jnp.int32, (BLK, BLK), 1)
    key_grads = [None] * blocks
    value_grads = [None] * blocks
    for half in range(2):
        far_value = far_ref[pair * 2 + half]
        diag, below = bias_tiles(near_ref[0, half : half + 1, :], far_value)
        keys = head_lanes(k_ref[...], half)
        values = head_lanes(v_ref[...], half)
        q_own = head_lanes(scaled, half)
        g_own = head_lanes(g_ref[...], half)
        keys_turned = jnp.concatenate([k_turned[64 * half : 64 * half + 64], ones], axis=0)
        delta = jnp.sum(inner[64 * half : 64 * half + 64], axis=0, keepdims=True)
        lse = lse_ref[0, half : half + 1, :]
        diag_grad = jnp.zeros((BLK, BLK), F32)
        below_grad = jnp.zeros((BLK, BLK), F32)
        turned[...] = jnp.zeros_like(turned)
        for kb in range(blocks):
            last = min(kb + SPAN + 1, blocks)
            k_rows = keys[kb * BLK : (kb + 1) * BLK]
            v_rows = values[kb * BLK : (kb + 1) * BLK]
            probs, grads = [], []
            for a in range(kb, last):
                rows = slice(a * BLK, (a + 1) * BLK)
                score = dot_nt(k_rows, scaled[rows])
                d_prob = dot_nt(v_rows, g_ref[rows, :])
                bias = (diag, below, far_value)[a - kb]
                prob = jnp.exp(score + bias + mask[kb, a - kb] - lse[:, rows])
                d_score = prob * (d_prob - delta[:, rows])
                if a == kb:
                    diag_grad = diag_grad + d_score
                elif a == kb + 1:
                    below_grad = below_grad + d_score
                probs.append(prob.astype(BF16))
                grads.append(d_score.astype(BF16))
            wide = slice(kb * BLK, last * BLK)
            prob_wide = jnp.concatenate(probs, axis=1)
            grad_wide = jnp.concatenate(grads, axis=1)
            value_grad = dot_nn(prob_wide, g_own[wide])
            key_grad = dot_nn(grad_wide, q_own[wide])
            turned[:, wide] += dot_nn(keys_turned[:, kb * BLK : (kb + 1) * BLK], grad_wide)
            if half == 0:
                value_grads[kb], key_grads[kb] = value_grad, key_grad
            else:
                rows = slice(kb * BLK, (kb + 1) * BLK)
                d_ref[2, rows, :] = (value_grads[kb] + value_grad).astype(BF16)
                d_ref[1, rows, :] = (key_grads[kb] + key_grad).astype(BF16)
        part = (turned[:64] * 0.125).T
        if half == 0:
            first_part = part
        else:
            d_ref[0] = jnp.concatenate([first_part, part], axis=1).astype(BF16)
        by_offset = diag_grad + jnp.where(row_place < key_place, below_grad, 0.0)
        for bit in range(8):
            by_offset = jnp.where(
                ((key_place >> bit) & 1) == 1,
                pltpu.roll(by_offset, BLK - (1 << bit), 1),
                by_offset,
            )
        near = jnp.sum(by_offset, axis=0, keepdims=True)
        near_grad[0, half : half + 1, :] = near
        everything = jnp.sum(turned[64:65, :], axis=1, keepdims=True)
        rest = everything - jnp.sum(near, axis=1, keepdims=True)
        far_grad[0, half : half + 1, :] = jnp.broadcast_to(rest, (1, 128))


def attention_specs(length, pairs):
    def column(offset):
        return pl.BlockSpec((length, 128), lambda p, far: (0, p + offset))

    return column


def attention_forward(qkv_rows, segments, near, far, heads, ahead=()):
    length = qkv_rows.shape[0]
    pairs = heads // 2
    width = heads * 64
    column = attention_specs(length, pairs)
    blocks = length // BLK
    return pl.pallas_call(
        attn_fwd_kernel,
        grid_spec=pltpu.PrefetchScalarGridSpec(
            num_scalar_prefetch=1,
            grid=(pairs,),
            in_specs=[
                column(0),
                column(pairs),
                column(2 * pairs),
                pl.BlockSpec((1, 2, BLK), lambda p, far: (p, 0, 0)),
                pl.BlockSpec((1, length), lambda p, far: (0, 0)),
                pl.BlockSpec((length, 1), lambda p, far: (0, 0)),
            ]
            + [pl.BlockSpec(memory_space=pl.ANY)] * len(ahead),
            out_specs=[
                column(0),
                pl.BlockSpec((1, 2, length), lambda p, far: (p, 0, 0)),
            ],
            scratch_shapes=[
                pltpu.VMEM((blocks, SPAN + 1, BLK, BLK), F32),
                pltpu.VMEM((128, length), F32),
            ],
        ),
        out_shape=[
            jax.ShapeDtypeStruct((length, width), BF16),
            jax.ShapeDtypeStruct((pairs, 2, length), F32),
        ],
        compiler_params=pltpu.CompilerParams(vmem_limit_bytes=60 * 1024 * 1024),
        cost_estimate=LIGHT,
        name="attention_forward",
    )(far, qkv_rows, qkv_rows, qkv_rows, near, segments.reshape(1, length), segments.reshape(length, 1), *ahead)


def attention_backward(qkv_rows, d_mixed, mixed, lse, segments, near, far, heads, ahead=()):
    length = qkv_rows.shape[0]
    pairs = heads // 2
    width = heads * 64
    column = attention_specs(length, pairs)
    blocks = length // BLK
    small = lambda n: pl.BlockSpec((1, 2, n), lambda p, far: (p, 0, 0))
    return pl.pallas_call(
        attn_bwd_kernel,
        grid_spec=pltpu.PrefetchScalarGridSpec(
            num_scalar_prefetch=1,
            grid=(pairs,),
            in_specs=[
                column(0),
                column(pairs),
                column(2 * pairs),
                column(0),
                column(0),
                small(length),
                small(BLK),
                pl.BlockSpec((1, length), lambda p, far: (0, 0)),
                pl.BlockSpec((length, 1), lambda p, far: (0, 0)),
            ]
            + [pl.BlockSpec(memory_space=pl.ANY)] * len(ahead),
            out_specs=[
                pl.BlockSpec((3, length, 128), lambda p, far: (0, 0, p)),
                small(BLK),
                small(128),
            ],
            scratch_shapes=[
                pltpu.VMEM((blocks, SPAN + 1, BLK, BLK), F32),
                pltpu.VMEM((80, length), F32),
            ],
        ),
        out_shape=[
            jax.ShapeDtypeStruct((3, length, width), BF16),
            jax.ShapeDtypeStruct((pairs, 2, BLK), F32),
            jax.ShapeDtypeStruct((pairs, 2, 128), F32),
        ],
        compiler_params=pltpu.CompilerParams(vmem_limit_bytes=60 * 1024 * 1024),
        cost_estimate=LIGHT,
        name="attention_backward",
    )(
        far, qkv_rows, qkv_rows, qkv_rows, d_mixed, mixed, lse, near,
        segments.reshape(1, length), segments.reshape(length, 1), *ahead,
    )


HEADS = 12
BUCKETS = 64
MAX_DIST = 128
EPS = 1e-06
ROWS = 256
TAIL = 16
COEF = math.sqrt(2.0 / math.pi)
CUBIC = 0.044715
MIB = 1024 * 1024


def bucket_bounds(bucket_count, max_distance):
    halfway = bucket_count // 2
    bounds = []
    for bucket in range(bucket_count):
        if bucket < halfway:
            bounds.append(bucket)
        else:
            bounds.append(
                int(math.ceil(halfway * (max_distance / halfway) ** ((bucket - halfway) / halfway)))
            )
    return bounds


def buckets_of(distance):
    limits = jnp.array(bucket_bounds(BUCKETS, MAX_DIST), dtype=jnp.int32)
    reached = (distance[:, None] >= limits[None, :]).astype(jnp.int32)
    return jnp.sum(reached, axis=1) - 1


def whole(shape):
    return pl.BlockSpec(shape, lambda *_: (0,) * len(shape))


def split_three(values):
    high = values.astype(BF16)
    rest = values - high.astype(F32)
    middle = rest.astype(BF16)
    low = (rest - middle.astype(F32)).astype(BF16)
    return high, middle, low


ANY = pl.BlockSpec(memory_space=pl.ANY)


def dispatch_kernel(experts, dest_ref, values_ref, gate_ref, *rest):
    out_refs = rest[-experts:]
    slots = out_refs[0].shape[0] - TAIL
    tokens = values_ref.shape[0]
    place = lax.broadcasted_iota(jnp.int32, (slots, tokens), 0)
    hot = (place == dest_ref[0]).astype(F32).astype(BF16)
    rows = dot_nn(hot, values_ref[...]).astype(BF16)
    pieces = split_three(jnp.broadcast_to(gate_ref[0], (TAIL, tokens)))
    line = lax.broadcasted_iota(jnp.int32, (TAIL, tokens), 0)
    stacked = jnp.zeros((TAIL, tokens), F32)
    for index, piece in enumerate(pieces):
        stacked = jnp.where(line == index, piece.astype(F32), stacked)
    tail = dot_nt(stacked.astype(BF16), hot).astype(BF16)
    for index, out_ref in enumerate(out_refs):

        @pl.when(pl.program_id(0) == index)
        def _():
            out_ref[:slots, :] = rows
            out_ref[slots:, :] = jnp.zeros((TAIL, out_ref.shape[1]), BF16)
            out_ref[slots:, :slots] = tail


def dispatch(dest_row, values, gate_row, slots, ahead=()):
    experts = dest_row.shape[0]
    tokens, width = values.shape
    return pl.pallas_call(
        functools.partial(dispatch_kernel, experts),
        grid=(experts,),
        in_specs=[
            pl.BlockSpec((1, 1, tokens), lambda m: (m, 0, 0)),
            whole((tokens, width)),
            pl.BlockSpec((1, 1, tokens), lambda m: (m, 0, 0)),
        ]
        + [ANY] * len(ahead),
        out_specs=[whole((slots + TAIL, width))] * experts,
        out_shape=[jax.ShapeDtypeStruct((slots + TAIL, width), BF16)] * experts,
        compiler_params=pltpu.CompilerParams(vmem_limit_bytes=40 * MIB),
        cost_estimate=LIGHT,
        name="dispatch_rows",
    )(dest_row, values, gate_row, *ahead)


def nothing_kernel(*refs):
    pass


def held(values, ahead):
    count = len(values)
    return pl.pallas_call(
        nothing_kernel,
        in_specs=[ANY] * (count + len(ahead)),
        out_specs=[ANY] * count,
        out_shape=[jax.ShapeDtypeStruct(value.shape, value.dtype) for value in values],
        input_output_aliases={index: index for index in range(count)},
        cost_estimate=LIGHT,
        name="held",
    )(*values, *ahead)


def post_kernel(
    mixed_ref, w_ref, tokens_ref, gain_ref, router_ref, dest_ref, move_ref, *rest
):
    residual_ref, normed_ref, gates_ref, moved_ref = rest[-4:]
    moved = dot_nn(mixed_ref[...], move_ref[...]).astype(BF16)
    moved_ref[...] = moved
    residual = tokens_ref[...].astype(F32) + dot_nn(moved, w_ref[...])
    residual_ref[...] = residual
    scale = lax.rsqrt(jnp.mean(residual * residual, axis=1, keepdims=True) + EPS)
    normed = (residual * scale * gain_ref[...]).astype(BF16)
    normed_ref[...] = normed
    logits = dot_nn(normed, router_ref[...])
    chosen = dest_ref[...] >= 0
    logits = jnp.where(chosen, logits, NEG)
    peak = jnp.max(logits, axis=1, keepdims=True)
    weights = jnp.where(chosen, jnp.exp(logits - peak), 0.0)
    gates_ref[...] = weights / jnp.sum(weights, axis=1, keepdims=True)


def post_attention(mixed, w_out, tokens, gain, router, dest_col, move, ahead=()):
    rows, width = tokens.shape
    block = lambda n: pl.BlockSpec((ROWS, n), lambda i: (i, 0))
    return pl.pallas_call(
        post_kernel,
        grid=(rows // ROWS,),
        in_specs=[
            block(width), pl.BlockSpec((width, width), lambda i: (0, 3)), block(width),
            whole((1, width)), whole((width, 128)), block(128), whole((width, width)),
        ]
        + [ANY] * len(ahead),
        out_specs=[block(width), block(width), block(128), block(width)],
        out_shape=[
            jax.ShapeDtypeStruct((rows, width), F32),
            jax.ShapeDtypeStruct((rows, width), BF16),
            jax.ShapeDtypeStruct((rows, 128), F32),
            jax.ShapeDtypeStruct((rows, width), BF16),
        ],
        compiler_params=pltpu.CompilerParams(vmem_limit_bytes=32 * MIB),
        cost_estimate=LIGHT,
        name="post_attention",
    )(mixed, w_out, tokens, gain, router, dest_col, move, *ahead)


def expert_kernel(
    rows_ref, grads_ref, in_own, out_own, in_other, out_other, *rest
):
    hid_own, hid_other, dpre_own, dpre_other, back_ref, made_ref = rest[-11:-5]
    rows_turned, gexp_turned, gexp, made_sum, back_sum = rest[-5:]
    step = pl.program_id(0)
    slots = gexp.shape[0]

    @pl.when(step == 0)
    def _():
        turned = rows_ref[slots:, :slots].astype(F32).T
        gate = jnp.sum(turned, axis=1, keepdims=True)
        gexp[...] = (grads_ref[:slots, :].astype(F32) * gate).astype(BF16)
        gexp_turned[...] = gexp[...].T
        rows_turned[...] = rows_ref[:slots, :].T
        made_sum[...] = jnp.zeros_like(made_sum)
        back_sum[...] = jnp.zeros_like(back_sum)

    rows = rows_ref[:slots, :]
    for w_in, w_out, hid, dpre in (
        (in_own, out_own, hid_own, dpre_own),
        (in_other, out_other, hid_other, dpre_other),
    ):
        pre = dot_nn(rows, w_in[...])
        d_hidden = dot_nn(gexp[...], w_out[...])
        square = pre * pre
        half = 0.5 + 0.5 * jnp.tanh(pre * (COEF + COEF * CUBIC * square))
        hidden = pre * half
        slope = half + hidden * (1.0 - half) * (2.0 * COEF + 6.0 * COEF * CUBIC * square)
        hidden_low = hidden.astype(BF16)
        d_pre = (d_hidden * slope).astype(BF16)
        hid[...] = hidden_low
        dpre[...] = d_pre
        made_sum[...] += dot_nt(hidden_low, w_out[...])
        back_sum[...] += dot_nt(d_pre, w_in[...])

    @pl.when(step == pl.num_programs(0) - 1)
    def _():
        made = made_sum[...]
        made_ref[...] = made.astype(BF16)
        back_ref[:slots, :] = back_sum[...].astype(BF16)
        by_gate = jnp.sum(grads_ref[:slots, :].astype(F32) * made, axis=1, keepdims=True)
        pieces = split_three(jnp.broadcast_to(by_gate, (slots, 128)))
        lane = lax.broadcasted_iota(jnp.int32, (slots, 128), 1)
        stacked = jnp.zeros((slots, 128), F32)
        for index, piece in enumerate(pieces):
            stacked = jnp.where(lane == index, piece.astype(F32), stacked)
        back_ref[slots:, :] = jnp.zeros((TAIL, back_ref.shape[1]), BF16)
        back_ref[slots:, :slots] = stacked.T[:TAIL].astype(BF16)


def expert_chunk(rows, grads, own_in, own_out, other_in, other_out, ahead=()):
    slots, width = rows.shape[0] - TAIL, rows.shape[1]
    half = own_in.shape[1]
    cols = 256
    steps = half // cols
    weights = pl.BlockSpec((width, cols), lambda f: (0, f))
    out = pl.BlockSpec((slots, cols), lambda f: (0, f))
    acts = jax.ShapeDtypeStruct((slots, half), BF16)
    return pl.pallas_call(
        expert_kernel,
        grid=(steps,),
        in_specs=[
            whole((slots + TAIL, width)), whole((slots + TAIL, width)),
            weights, weights, weights, weights,
        ]
        + [ANY] * len(ahead),
        out_specs=[
            out, out, out, out,
            whole((slots + TAIL, width)), whole((slots, width)),
            whole((width, slots)), whole((width, slots)),
        ],
        out_shape=[
            acts, acts, acts, acts,
            jax.ShapeDtypeStruct((slots + TAIL, width), BF16),
            jax.ShapeDtypeStruct((slots, width), BF16),
            jax.ShapeDtypeStruct((width, slots), BF16),
            jax.ShapeDtypeStruct((width, slots), BF16),
        ],
        scratch_shapes=[
            pltpu.VMEM((slots, width), BF16),
            pltpu.VMEM((slots, width), F32),
            pltpu.VMEM((slots, width), F32),
        ],
        compiler_params=pltpu.CompilerParams(vmem_limit_bytes=60 * MIB),
        cost_estimate=LIGHT,
        name="expert_chunk",
    )(rows, grads, own_in, own_out, other_in, other_out, *ahead)


def weight_grad_kernel(count, *refs):
    turned = refs[:count]
    acts = refs[count : 2 * count]
    out_ref = refs[-1]
    total = dot_nn(turned[0][...], acts[0][...])
    for index in range(1, count):
        total = total + dot_nn(turned[index][...], acts[index][...])
    out_ref[...] = total.astype(BF16)


def weight_grad(turned, acts, ahead=()):
    count = len(turned)
    width, slots = turned[0].shape
    half = acts[0].shape[1]
    cols = 512
    return pl.pallas_call(
        functools.partial(weight_grad_kernel, count),
        grid=(half // cols,),
        in_specs=[whole((width, slots))] * count
        + [pl.BlockSpec((slots, cols), lambda f: (0, f))] * count
        + [ANY] * len(ahead),
        out_specs=pl.BlockSpec((width, cols), lambda f: (0, f)),
        out_shape=jax.ShapeDtypeStruct((width, half), BF16),
        compiler_params=pltpu.CompilerParams(vmem_limit_bytes=60 * MIB),
        cost_estimate=LIGHT,
        name="weight_grad",
    )(*turned, *acts, *ahead)


def combine_kernel(count, *refs):
    backs, ends = refs[:count], refs[count : 2 * count]
    (dest_ref, gates_ref, residual_ref, grad_ref, gain_ref, router_ref, w_ref) = refs[
        2 * count : 2 * count + 7
    ]
    (d_residual_ref, branch_ref, mixed_ref, gain_grad, logit_grad, stacked, tails) = refs[-7:]
    slots = backs[0].shape[0]

    @pl.when(pl.program_id(0) == 0)
    def _():
        gain_grad[...] = jnp.zeros_like(gain_grad)
        tails[...] = jnp.zeros_like(tails)
        for index, (back, end) in enumerate(zip(backs, ends)):
            columns = slice(index * slots, (index + 1) * slots)
            stacked[columns, :] = back[...]
            tails[index * TAIL : (index + 1) * TAIL, columns] = end[:, :slots]

    place = lax.broadcasted_iota(jnp.int32, (ROWS, slots), 1)
    lane = lax.broadcasted_iota(jnp.int32, (ROWS, 128), 1)
    hot = jnp.concatenate(
        [
            (place == dest_ref[:, index : index + 1]).astype(F32).astype(BF16)
            for index in range(count)
        ],
        axis=1,
    )
    d_normed = dot_nn(hot, stacked[...])
    picked = dot_nt(hot, tails[...])
    d_gates = jnp.zeros((ROWS, 128), F32)
    for index in range(count):
        part = picked[:, index * TAIL : index * TAIL + 1]
        for extra in (1, 2):
            part = part + picked[:, index * TAIL + extra : index * TAIL + extra + 1]
        d_gates = jnp.where(lane == index, part, d_gates)
    gates = gates_ref[...]
    inner = jnp.sum(gates * d_gates, axis=1, keepdims=True)
    d_logits = gates * (d_gates - inner)
    logit_grad[...] = d_logits
    for index in range(count):
        d_normed = d_normed + d_logits[:, index : index + 1] * router_ref[index : index + 1, :]
    residual = residual_ref[...]
    scale = lax.rsqrt(jnp.mean(residual * residual, axis=1, keepdims=True) + EPS)
    unit = residual * scale
    scaled = gain_ref[...] * d_normed
    pull = jnp.mean(scaled * unit, axis=1, keepdims=True)
    d_residual = grad_ref[...].astype(F32) + scale * (scaled - unit * pull)
    d_residual_ref[...] = d_residual
    branch = d_residual.astype(BF16)
    branch_ref[...] = branch
    mixed_ref[...] = dot_nt(branch, w_ref[...]).astype(BF16)
    gain_grad[...] += jnp.sum(d_normed * unit, axis=0, keepdims=True)


def combine_back(backs, dest_col, gates, residual, grad, gain, router_rows, w_out, ahead=()):
    rows, width = residual.shape
    count = len(backs)
    slots = backs[0].shape[0] - TAIL
    block = lambda n: pl.BlockSpec((ROWS, n), lambda i: (i, 0))
    return pl.pallas_call(
        functools.partial(combine_kernel, count),
        grid=(rows // ROWS,),
        in_specs=[pl.BlockSpec((slots, width), lambda i: (0, 0))] * count
        + [pl.BlockSpec((TAIL, width), lambda i: (slots // TAIL, 0))] * count
        + [
            block(128), block(128), block(width), block(width), whole((1, width)),
            whole(router_rows.shape), whole((width, width)),
        ]
        + [ANY] * len(ahead),
        out_specs=[block(width), block(width), block(width), whole((1, width)), block(128)],
        out_shape=[
            jax.ShapeDtypeStruct((rows, width), F32),
            jax.ShapeDtypeStruct((rows, width), BF16),
            jax.ShapeDtypeStruct((rows, width), BF16),
            jax.ShapeDtypeStruct((1, width), F32),
            jax.ShapeDtypeStruct((rows, 128), F32),
        ],
        scratch_shapes=[
            pltpu.VMEM((count * slots, width), BF16),
            pltpu.VMEM((count * TAIL, count * slots), BF16),
        ],
        compiler_params=pltpu.CompilerParams(vmem_limit_bytes=48 * MIB),
        cost_estimate=LIGHT,
        name="combine_back",
    )(*backs, *backs, dest_col, gates, residual, grad, gain, router_rows, w_out, *ahead)


def output_kernel(count, *refs):
    mades = refs[:count]
    dest_ref, gates_ref, residual_ref = refs[count : count + 3]
    out_ref = refs[-1]
    slots = mades[0].shape[0]
    place = lax.broadcasted_iota(jnp.int32, (ROWS, slots), 1)
    total = residual_ref[...]
    for index, made in enumerate(mades):
        hot = (place == dest_ref[:, index : index + 1]).astype(F32).astype(BF16)
        total = total + gates_ref[:, index : index + 1] * dot_nn(hot, made[...])
    out_ref[...] = total.astype(BF16)


def combine_output(mades, dest_col, gates, residual, ahead=()):
    rows, width = residual.shape
    count = len(mades)
    slots = mades[0].shape[0]
    block = lambda n: pl.BlockSpec((ROWS, n), lambda i: (i, 0))
    return pl.pallas_call(
        functools.partial(output_kernel, count),
        grid=(rows // ROWS,),
        in_specs=[pl.BlockSpec((slots, width), lambda i: (0, 0))] * count
        + [block(128), block(128), block(width)]
        + [ANY] * len(ahead),
        out_specs=block(width),
        out_shape=jax.ShapeDtypeStruct((rows, width), BF16),
        compiler_params=pltpu.CompilerParams(vmem_limit_bytes=40 * MIB),
        cost_estimate=LIGHT,
        name="combine_output",
    )(*mades, dest_col, gates, residual, *ahead)


def final_kernel(dqkv_ref, w_ref, tokens_ref, gain_ref, d_residual_ref, *rest):
    out_ref = rest[-1]
    width = tokens_ref.shape[1]
    d_normed = (
        dot_nt(dqkv_ref[0], w_ref[:, :width])
        + dot_nt(dqkv_ref[1], w_ref[:, width : 2 * width])
        + dot_nt(dqkv_ref[2], w_ref[:, 2 * width : 3 * width])
    )
    tokens = tokens_ref[...].astype(F32)
    scale = lax.rsqrt(jnp.mean(tokens * tokens, axis=1, keepdims=True) + EPS)
    unit = tokens * scale
    scaled = gain_ref[...] * d_normed
    pull = jnp.mean(scaled * unit, axis=1, keepdims=True)
    out_ref[...] = d_residual_ref[...] + scale * (scaled - unit * pull)


def final_tokens(d_qkv, w_all, tokens, gain, d_residual, ahead=()):
    rows, width = tokens.shape
    block = lambda n: pl.BlockSpec((ROWS, n), lambda i: (i, 0))
    return pl.pallas_call(
        final_kernel,
        grid=(rows // ROWS,),
        in_specs=[
            pl.BlockSpec((3, ROWS, width), lambda i: (0, i, 0)), whole((width, 3 * width)),
            block(width), whole((1, width)), block(width),
        ]
        + [ANY] * len(ahead),
        out_specs=block(width),
        out_shape=jax.ShapeDtypeStruct((rows, width), F32),
        compiler_params=pltpu.CompilerParams(vmem_limit_bytes=40 * MIB),
        cost_estimate=LIGHT,
        name="final_tokens",
    )(d_qkv, w_all, tokens, gain, d_residual, *ahead)


def qkv_grad_kernel(parts, turned_ref, grad_ref, mixed_ref, branch_ref, extra_ref, *rest):
    step = pl.program_id(0)
    keep_ref, send_ref = rest[-2:]
    half = keep_ref.shape[0]

    def store(made):
        keep_ref[...] = made[:half]
        send_ref[...] = made[half:]

    @pl.when(step < 3 * parts)
    def _():
        store(dot_nn(turned_ref[...], grad_ref[0]).astype(BF16))

    @pl.when((step >= 3 * parts) & (step < 4 * parts))
    def _():
        store(dot_nn(mixed_ref[...], branch_ref[...]).astype(BF16))

    @pl.when(step == 4 * parts)
    def _():
        store(extra_ref[...])


def qkv_grad(turned, d_qkv, mixed_turned, branch, extra, ahead=()):
    width, rows = turned.shape
    parts = width // BLK

    def place(j):
        j = jnp.minimum(j, 3 * parts - 1)
        return (j // parts, 0, j % parts)

    def place_branch(j):
        return (0, jnp.clip(j - 3 * parts, 0, parts - 1))

    return pl.pallas_call(
        functools.partial(qkv_grad_kernel, parts),
        grid=(4 * parts + 1,),
        in_specs=[
            whole((width, rows)), pl.BlockSpec((1, rows, BLK), place),
            whole((width, rows)), pl.BlockSpec((rows, BLK), place_branch), whole((width, BLK)),
        ]
        + [ANY] * len(ahead),
        out_specs=[pl.BlockSpec((width // 2, BLK), lambda j: (0, j))] * 2,
        out_shape=[jax.ShapeDtypeStruct((width // 2, 4 * width + BLK), BF16)] * 2,
        compiler_params=pltpu.CompilerParams(vmem_limit_bytes=40 * MIB),
        cost_estimate=LIGHT,
        name="qkv_grad",
    )(turned, d_qkv, mixed_turned, branch, extra, *ahead)


def pairs_of(size, offset):
    return [(i, i ^ offset) for i in range(size)]


def gather_rows(block, ahead):
    dp_size, fsdp_size = lax.axis_size("dp"), lax.axis_size("fsdp")
    line = [block]
    for m in range(1, dp_size):
        line.append(lax.ppermute(block, "dp", pairs_of(dp_size, m)))
    line = jnp.concatenate(line, axis=0)
    plane = [line]
    for m in range(1, fsdp_size // 2):
        plane.append(lax.ppermute(line, "fsdp", pairs_of(fsdp_size, 2 * m)))
    (plane,) = held([jnp.concatenate(plane, axis=0)], ahead)
    other = lax.ppermute(plane, "fsdp", pairs_of(fsdp_size, 1))
    return plane, jnp.concatenate([plane, other], axis=0)


def scatter_pair(keep, send):
    fsdp_size = lax.axis_size("fsdp")
    got = lax.ppermute(send, "fsdp", pairs_of(fsdp_size, 1))
    return (keep.astype(F32) + got.astype(F32)).astype(BF16)


def scatter_plane(plane):
    fsdp_size = lax.axis_size("fsdp")
    rows = 2 * plane.shape[0] // fsdp_size
    line = plane[:rows].astype(F32)
    for m in range(1, fsdp_size // 2):
        got = lax.ppermute(plane[m * rows : (m + 1) * rows], "fsdp", pairs_of(fsdp_size, 2 * m))
        line = line + got.astype(F32)
    return line.astype(BF16)


def scatter_line(line):
    dp_size = lax.axis_size("dp")
    rows = line.shape[0] // dp_size
    total = line[:rows].astype(F32)
    for m in range(1, dp_size):
        got = lax.ppermute(line[m * rows : (m + 1) * rows], "dp", pairs_of(dp_size, m))
        total = total + got.astype(F32)
    return total


def position_matrix(width):
    dp_size, fsdp_size = lax.axis_size("dp"), lax.axis_size("fsdp")
    layer, place = lax.axis_index("dp"), lax.axis_index("fsdp")
    chips = fsdp_size // 2
    rows = width // (dp_size * fsdp_size)
    position = jnp.arange(width, dtype=jnp.int32)
    row = position % rows
    layer_of = (position // rows) % dp_size ^ layer
    chip_of = (position // (rows * dp_size)) % chips ^ (place // 2)
    core_of = position // (rows * dp_size * chips) ^ (place % 2)
    source = ((layer_of * chips + chip_of) * 2 + core_of) * rows + row
    return (position[:, None] == source[None, :]).astype(BF16)


def local(
    tokens_in, w_qkv, w_attn_out, gain_attn, gain_ffn, rel_bias, router, w_in, w_out,
    segment_ids, expert_ids, d_out,
):
    tok_rows, width = tokens_in.shape
    top_count = expert_ids.shape[1]
    fsdp_size = lax.axis_size("fsdp")
    experts = fsdp_size // 2
    slots = min(tok_rows, tok_rows * top_count * 5 // (4 * experts))
    me = lax.axis_index("fsdp") // 2

    own_in = lax.all_gather(w_in, "dp", axis=0, tiled=True)
    own_out = lax.all_gather(w_out, "dp", axis=0, tiled=True)
    small = jnp.concatenate(
        [router, gain_attn[:, None], gain_ffn[:, None], rel_bias[:, None]], axis=1
    )
    small = jnp.pad(small, ((0, 0), (0, 128 - small.shape[1])))
    relative = expert_ids ^ me
    hot = jnp.sum(
        (relative[:, :, None] == jnp.arange(experts, dtype=jnp.int32)).astype(jnp.int32), axis=1
    )
    rank = jnp.cumsum(hot, axis=0) - hot
    dest = jnp.where(hot > 0, rank, -1)
    dest_col = jnp.pad(dest, ((0, 0), (0, 128 - experts)), constant_values=-1)
    dest_row = dest.T.reshape(experts, 1, tok_rows)

    def exchange(pieces):
        return [pieces[0]] + [
            lax.ppermute(pieces[m], "fsdp", pairs_of(fsdp_size, 2 * m)) for m in range(1, experts)
        ]

    sent_grads = dispatch(dest_row, d_out, jnp.zeros((experts, 1, tok_rows), F32), slots)
    move = position_matrix(width)
    moved_tokens = jnp.dot(tokens_in, move, preferred_element_type=F32)
    plane, full = gather_rows(
        jnp.concatenate([w_qkv, w_attn_out, small], axis=1), tuple(sent_grads[1:2])
    )
    grads_in = exchange([sent_grads[0]] + list(held(sent_grads[1:], (plane,))))

    moved_gain = full[:, 4 * width + experts].astype(F32).reshape(1, width)
    columns = jnp.dot(move, full[:, 4 * width :], preferred_element_type=F32).astype(BF16)
    back_qkv = jnp.dot(move, full[:, : 3 * width], preferred_element_type=F32).astype(BF16)
    back_attn = jnp.dot(
        move, full[:, 3 * width : 4 * width], preferred_element_type=F32
    ).astype(BF16)
    by_row = columns.T
    gain_a = by_row[experts : experts + 1].astype(F32)
    gain_f = by_row[experts + 1 : experts + 2].astype(F32)
    table = by_row[experts + 2].reshape(HEADS, BUCKETS)
    bucket_hot = (
        buckets_of(jnp.arange(BLK, dtype=jnp.int32))[:, None]
        == jnp.arange(BUCKETS, dtype=jnp.int32)[None, :]
    )
    near = jnp.dot(table, bucket_hot.T.astype(BF16), preferred_element_type=F32)
    near = near.reshape(HEADS // 2, 2, BLK)
    far = table[:, BUCKETS - 1].astype(F32)
    place = jnp.arange(128, dtype=jnp.int32)
    swap = ((place[:, None] ^ me) == place[None, :]) & (place[:, None] < experts)
    router_cols = jnp.dot(columns, swap.astype(BF16), preferred_element_type=F32).astype(BF16)
    router_rows = router_cols.T[: max(8, experts)].astype(F32)

    tokens = tokens_in.astype(F32)
    scale = lax.rsqrt(jnp.mean(tokens * tokens, axis=1, keepdims=True) + EPS)
    normed_attn = (moved_tokens * scale * moved_gain).astype(BF16)
    qkv_rows = jnp.dot(normed_attn, full[:, : 3 * width], preferred_element_type=F32).astype(BF16)
    segments = segment_ids.reshape(tok_rows)
    mixed, lse = attention_forward(
        qkv_rows, segments, near, far, HEADS, tuple(grads_in[1:3])
    )
    residual, normed_ffn, gates, moved_mixed = post_attention(
        mixed, full, tokens_in, gain_f, router_cols, dest_col, move
    )
    gate_row = gates[:, :experts].T.reshape(experts, 1, tok_rows)
    sent_rows = dispatch(dest_row, normed_ffn, gate_row, slots)
    rows_in = exchange(sent_rows)
    (own_in,) = held([own_in], (mixed,))
    (own_out,) = held([own_out], (sent_rows[0],))
    other_in = lax.ppermute(own_in, "fsdp", pairs_of(fsdp_size, 1))
    other_out = lax.ppermute(own_out, "fsdp", pairs_of(fsdp_size, 1))

    chunks, backs = [], []
    for m in range(experts):
        ahead = tuple(backs[1 : m - 1]) + ((chunks[-1][4],) if chunks else ())
        chunks.append(
            expert_chunk(rows_in[m], grads_in[m], own_in, own_out, other_in, other_out, ahead)
        )
        back = chunks[-1][4]
        backs.append(
            lax.ppermute(back, "fsdp", pairs_of(fsdp_size, 2 * m)) if m > 0 else back
        )
    hid_own, hid_other, dpre_own, dpre_other, _, made, rows_turned, gexp_turned = zip(*chunks)
    mades = exchange(made)

    def pair_sum(own, other):
        got = lax.ppermute(other, "fsdp", pairs_of(fsdp_size, 1))
        return (own.astype(F32) + got.astype(F32)).astype(BF16)

    def owners(pair):
        return lax.psum_scatter(pair, "dp", scatter_dimension=0, tiled=True).astype(F32)

    grad_in_own = weight_grad(rows_turned, dpre_own, tuple(backs[-2:-1]))
    grad_out_own = weight_grad(gexp_turned, hid_own, (grad_in_own,))
    grad_in_other = weight_grad(rows_turned, dpre_other, (grad_out_own,) + tuple(backs[-1:]))
    grad_out_other = weight_grad(gexp_turned, hid_other, (grad_in_other,))
    pair_in = pair_sum(grad_in_own, grad_in_other)
    pair_out = pair_sum(grad_out_own, grad_out_other)
    d_w_in, d_w_out = owners(pair_in), owners(pair_out)

    d_residual, d_branch, d_mixed, d_gain_f, d_logits = combine_back(
        backs, dest_col, gates, residual, d_out, gain_f, router_rows, back_attn, (grad_out_other, pair_in)
    )
    d_qkv, near_grad, far_grad = attention_backward(
        qkv_rows, d_mixed, mixed, lse, segments, near, far, HEADS, (pair_out,)
    )
    d_router = jnp.dot(normed_ffn.T, d_logits.astype(BF16), preferred_element_type=F32)
    d_router = jnp.dot(d_router, swap.T.astype(F32), precision=lax.Precision.HIGHEST)
    d_table = jnp.dot(
        near_grad.reshape(HEADS, BLK), bucket_hot.astype(F32), precision=lax.Precision.HIGHEST
    )
    last = jnp.arange(BUCKETS, dtype=jnp.int32)[None, :] == BUCKETS - 1
    d_table = d_table + jnp.where(last, far_grad[:, :, :1].reshape(HEADS, 1), 0.0)
    late_cols = jnp.where(place[None, :] == experts, d_gain_f.reshape(width, 1), d_router)
    late_cols = jnp.where(place[None, :] == experts + 1, d_table.reshape(width, 1), late_cols)
    late_cols = jnp.dot(move.T, late_cols.astype(BF16), preferred_element_type=F32)
    late_cols = jnp.pad(late_cols.astype(BF16), ((0, 0), (0, BLK - 128)))
    keep, send = qkv_grad(
        normed_attn.T, d_qkv, moved_mixed.T, d_branch, late_cols, (d_w_in,) + tuple(mades[1:])
    )
    late = scatter_line(scatter_plane(scatter_pair(keep, send)))
    block_out = combine_output(mades, dest_col, gates, residual, (keep,))
    d_tokens = final_tokens(d_qkv, back_qkv, tokens_in, gain_a, d_residual, (d_w_out,))
    own_qkv = late[:, : 3 * width]
    own_gain_a = jnp.sum(own_qkv * w_qkv.astype(F32), axis=1) / gain_attn.astype(F32)
    return (
        block_out,
        d_tokens,
        own_qkv,
        late[:, 3 * width : 4 * width],
        own_gain_a,
        late[:, 4 * width + experts],
        late[:, 4 * width + experts + 1],
        late[:, 4 * width : 4 * width + experts],
        d_w_in,
        d_w_out,
    )


def solution(mesh):
    both = P(("dp", "fsdp"), None)
    line = P(("dp", "fsdp"))
    tiles = P("dp", "fsdp")
    return jax.shard_map(
        local,
        mesh=mesh,
        in_specs=(both, both, both, line, line, line, both, tiles, tiles, both, both, both),
        out_specs=(both, both, both, both, line, line, line, both, tiles, tiles),
        check_vma=False,
    )
```

time: 7930 us -> 493 us (0.06); the launches traced: 7790 us -> 486 us
  local copies, waits for them, and re-layouts: 6930 us -> 42.7 us
  matrix products: 295 us -> 24.9 us
  Pallas kernels: 0 us -> 249 us
  blocking collectives: 185 us -> 0 us
  other arithmetic: 191 us -> 28.6 us
    gather x11 -> x0, local copies, waits for them, and re-layouts: 4290 us -> none  [the longest x2 4220 us: bias_cells(): return jnp.take(bias_rel.astype(jnp.bfloat16), rel_dist, axis=1)]
    unnamed x294 -> x107, local copies, waits for them, and re-layouts: 2340 us -> 30.5 us
    dot_general x53 -> x11, matrix products: 295 us -> 24.9 us  [the longest x1 7.62 us: local(): jnp.dot(normed_attn, full[:, :3 * width], preferred_element_type=F32)]
    pallas_call x0 -> x21, Pallas kernels: none -> 249 us  [the longest x4 91.4 us: expert_chunk(): pl.pallas_call(expert_kernel, grid=(steps,), in_specs=[whole((slots + TAI...]
    pad x2 -> x3, local copies, waits for them, and re-layouts: 136 us -> 0.08 us  [the longest x1 0.04 us: local(): dest_col = jnp.pad(dest, ((0, 0), (0, 128 - experts)), constant_values=-1)]
    all_to_all x4 -> x0, waiting for transfers between devices: 113 us -> none  [the longest x1 56.8 us: local(): lax.all_to_all(d_rows.reshape(fsdp_size, capacity, width), 'fsdp', split_...]
    all_gather x1 -> x0, blocking collectives: 105 us -> none  [local(): lax.all_gather(router, ('dp', 'fsdp'), axis=0, tiled=True)]
    ppermute x0 -> x30, waiting for transfers between devices: none -> 87 us  [the longest x3 27.9 us: scatter_plane(): lax.ppermute(plane[m * rows:(m + 1) * rows], 'fsdp', pairs_of(fsdp_size,...]
  transfers between devices with their start and end apart: 12 -> 34, of which waited for: 4 -> 12; matrix products, arithmetic and copies ran while one was open for 94% -> 12% of each run, Pallas kernels for 0% -> 46%
where the time goes in v1:
time: 493 us; the launch traced here: 486 us
  Pallas kernels  249 us (51%)
  waiting for transfers between devices  87.1 us (18%)
  local copies, waits for them, and re-layouts  42.7 us (9%)
  starting transfers between devices  39.4 us (8%)
  other arithmetic  28.6 us (6%)
  matrix products  24.9 us (5%)
  between operations  14.8 us (3%)
    pallas_call x4, Pallas kernels, expert_chunk(): pl.pallas_call(expert_kernel, grid=(steps,), in_specs=[whole((slots + TAI...  91.4 us
    pallas_call x4, Pallas kernels, weight_grad(): pl.pallas_call(functools.partial(weight_grad_kernel, count), grid=(half /...  47.8 us
    pallas_call x1, Pallas kernels, attention_backward(): pl.pallas_call(attn_bwd_kernel, grid_spec=pltpu.PrefetchScalarGridSpec(nu...  30.7 us
    unnamed x107, local copies, waits for them, and re-layouts  30.5 us
    ppermute x3, waiting for transfers between devices, scatter_plane(): lax.ppermute(plane[m * rows:(m + 1) * rows], 'fsdp', pairs_of(fsdp_size,...  27.9 us
    ppermute x3, waiting for transfers between devices, gather_rows(): plane.append(lax.ppermute(line, 'fsdp', pairs_of(fsdp_size, 2 * m)))  23.5 us
    ppermute x9, waiting for transfers between devices, exchange(): lax.ppermute(pieces[m], 'fsdp', pairs_of(fsdp_size, 2 * m))  22.5 us
    pallas_call x1, Pallas kernels, attention_forward(): pl.pallas_call(attn_fwd_kernel, grid_spec=pltpu.PrefetchScalarGridSpec(nu...  20.4 us
  transfers between devices with their start and end apart: 34, of which 12 were waited for; matrix products, arithmetic and copies ran while one was open for 12% of the time, Pallas kernels for 46%

profile of v1, /device:TPU:0, one launch (start us, length us, event | category | flops | bytes accessed | tf_op | source)
XLA Modules:
  0.0 486.0 jit_solution(9369040835591403569)
XLA Ops:
  9.9 4.0 collective-permute-start.1
  18.9 6.5 %dispatch_rows.2 = (bf16[656,768]{1,0:T(8,128)(2,1)S(1)}, bf16[656,768]{1,0:T(8,128)(2,1)S(1)}, bf16[656,768]{1,0:T(8,128)(2,1)S(1)}, bf16[656,768]{1,0:T(8,128)(2,1)S(1)}) custom-call(s32[4,1,1024]{2,1,0:T(1,128)S(1)} %copy.113.dest_ref, bf16[1024,768]{1,0:T(8,128)(2,1)S(1)} %copy-done.12, f32[4,1,1024]{2,1,0:T(1,128)S(1)} %broadcast_in_dim.89.gate_ref), custom_call_target="tpu_custom_call" | custom-call | flops 1000 | bytes 1000 | tf_op jit(solution)/shard_map/dispatch_rows/pallas_call | solution.py:341
  32.8 23.5 %collective-permute-done.3 = bf16[96,3200]{1,0:T(8,128)(2,1)S(1)} collective-permute-done((bf16[96,3200]{1,0:T(8,128)(2,1)S(1)}, bf16[96,3200]{1,0:T(8,128)(2,1)S(1)}, u32[]{:S(2)}, u32[]{:S(2)}) %collective-permute-start.3) | collective-permute-done | bytes 614432 | tf_op jit(solution)/shard_map/ppermute | solution.py:751
  70.7 7.6 %convolution_convert_fusion.q_ref.k_ref.v_ref = bf16[1024,2304]{1,0:T(8,128)(2,1)} fusion(bf16[768,1024]{1,0:T(8,128)(2,1)S(1)} %multiply_convert_fusion.turned_ref, bf16[384,3200]{1,0:T(8,128)(2,1)S(1)} %copy-done.40, bf16[384,3200]{1,0:T(8,128)(2,1)} %collective-permute-done.6), kind=kOutput, calls=%fused_computation.9 | convolution fusion | flops 3633315840 | bytes 11206656 | tf_op jit(solution)/shard_map/dot_general | solution.py:861
  78.3 8.6 %collective-permute-done.7.rest_0_.grads_ref = bf16[656,768]{1,0:T(8,128)(2,1)} collective-permute-done((bf16[656,768]{1,0:T(8,128)(2,1)}, bf16[656,768]{1,0:T(8,128)(2,1)}, u32[]{:S(2)}, u32[]{:S(2)}) %collective-permute-start.7) | collective-permute-done | bytes 1007648 | tf_op jit(solution)/shard_map/ppermute | solution.py:825
  88.1 20.4 %attention_forward.1 = (bf16[1024,768]{1,0:T(8,128)(2,1)}, f32[6,2,1024]{2,1,0:T(2,128)}) custom-call(f32[12]{0:T(128)} %bitcast_convert_fusion.far_ref, bf16[1024,2304]{1,0:T(8,128)(2,1)} %convolution_convert_fusion.q_ref.k_ref.v_ref, bf16[1024,2304]{1,0:T(8,128)(2,1)} %convolution_convert_fusion.q_ref.k_ref.v_ref, ...), custom_call_target="tpu_custom_call" | custom-call | flops 1000 | bytes 1000 | tf_op jit(solution)/shard_map/attention_forward/pallas_call | solution.py:190
  112.3 5.5 %post_attention.1 = (f32[1024,768]{1,0:T(8,128)S(1)}, bf16[1024,768]{1,0:T(8,128)(2,1)S(1)}, f32[1024,128]{1,0:T(8,128)S(1)}, bf16[1024,768]{1,0:T(8,128)(2,1)S(1)}) custom-call(bf16[1024,768]{1,0:T(8,128)(2,1)S(1)} %copy-done.2, bf16[768,3200]{1,0:T(8,128)(2,1)S(1)} %pad_maximum_fusion.w_ref, bf16[1024,768]{1,0:T(8,128)(2,1)S(1)} %copy-done.1, ...), custom_call_target="tpu_custom_call" | custom-call | flops 1000 | bytes 1000 | tf_op jit(solution)/shard_map/post_attention/pallas_call | solution.py:397
  125.0 6.5 %dispatch_rows.3 = (bf16[656,768]{1,0:T(8,128)(2,1)S(1)}, bf16[656,768]{1,0:T(8,128)(2,1)S(1)}, bf16[656,768]{1,0:T(8,128)(2,1)S(1)}, bf16[656,768]{1,0:T(8,128)(2,1)S(1)}) custom-call(s32[4,1,1024]{2,1,0:T(1,128)S(1)} %copy.113.dest_ref, bf16[1024,768]{1,0:T(8,128)(2,1)S(1)} %copy-done.14, f32[4,1,1024]{2,1,0:T(1,128)S(1)} %reshape.163.gate_ref), custom_call_target="tpu_custom_call" | custom-call | flops 1000 | bytes 1000 | tf_op jit(solution)/shard_map/dispatch_rows/pallas_call | solution.py:341
  143.6 22.9 %expert_chunk.4 = (bf16[640,1536]{1,0:T(8,128)(2,1)}, bf16[640,1536]{1,0:T(8,128)(2,1)}, bf16[640,1536]{1,0:T(8,128)(2,1)}, bf16[640,1536]{1,0:T(8,128)(2,1)}, b...) custom-call(bf16[656,768]{1,0:T(8,128)(2,1)} %copy-done.22, ...), custom_call_target="tpu_custom_call" | custom-call | flops 1000 | bytes 1000 | tf_op jit(solution)/shard_map/expert_chunk/pallas_call | solution.py:477
  167.5 22.7 %expert_chunk.5 = (bf16[640,1536]{1,0:T(8,128)(2,1)}, bf16[640,1536]{1,0:T(8,128)(2,1)}, bf16[640,1536]{1,0:T(8,128)(2,1)}, bf16[640,1536]{1,0:T(8,128)(2,1)}, b...) custom-call(bf16[656,768]{1,0:T(8,128)(2,1)} %copy-done.44, ...), custom_call_target="tpu_custom_call" | custom-call | flops 1000 | bytes 1000 | tf_op jit(solution)/shard_map/expert_chunk/pallas_call | solution.py:477
  190.8 12.6 %collective-permute-done.13.rows_ref = bf16[656,768]{1,0:T(8,128)(2,1)} collective-permute-done((bf16[656,768]{1,0:T(8,128)(2,1)}, bf16[656,768]{1,0:T(8,128)(2,1)}, u32[]{:S(2)}, u32[]{:S(2)}) %collective-permute-start.13) | collective-permute-done | bytes 1007648 | tf_op jit(solution)/shard_map/ppermute | solution.py:825
  203.4 22.7 %expert_chunk.6 = (bf16[640,1536]{1,0:T(8,128)(2,1)}, bf16[640,1536]{1,0:T(8,128)(2,1)}, bf16[640,1536]{1,0:T(8,128)(2,1)}, bf16[640,1536]{1,0:T(8,128)(2,1)}, b...) custom-call(bf16[656,768]{1,0:T(8,128)(2,1)} %collective-permute-done.1, ...), custom_call_target="tpu_custom_call" | custom-call | flops 1000 | bytes 1000 | tf_op jit(solution)/shard_map/expert_chunk/pallas_call | solution.py:477
  228.6 23.1 %expert_chunk.7 = (bf16[640,1536]{1,0:T(8,128)(2,1)}, bf16[640,1536]{1,0:T(8,128)(2,1)}, bf16[640,1536]{1,0:T(8,128)(2,1)}, bf16[640,1536]{1,0:T(8,128)(2,1)}, b...) custom-call(bf16[656,768]{1,0:T(8,128)(2,1)} %collective-permute-done.1, ...), custom_call_target="tpu_custom_call" | custom-call | flops 1000 | bytes 1000 | tf_op jit(solution)/shard_map/expert_chunk/pallas_call | solution.py:477
  253.1 11.8 %weight_grad.4.refs_8_ = bf16[768,1536]{1,0:T(8,128)(2,1)} custom-call(bf16[768,640]{1,0:T(8,128)(2,1)} %get-tuple-element.100.refs_0_, bf16[768,640]{1,0:T(8,128)(2,1)} %get-tuple-element.101.refs_1_, bf16[768,640]{1,0:T(8,128)(2,1)} %get-tuple-element.102.refs_2_, bf16[768,640]{1,0:T(8,128)(2,1)} %get-tuple-element.103.refs_3_, ...), custom_call_target="tpu_custom_call" | custom-call | flops 1000 | bytes 1000 | tf_op jit(solution)/shard_map/weight_grad/pallas_call | solution.py:523
  265.0 11.9 %weight_grad.5.refs_8_ = bf16[768,1536]{1,0:T(8,128)(2,1)} custom-call(bf16[768,640]{1,0:T(8,128)(2,1)} %get-tuple-element.92.refs_0_, bf16[768,640]{1,0:T(8,128)(2,1)} %get-tuple-element.93.refs_1_, bf16[768,640]{1,0:T(8,128)(2,1)} %get-tuple-element.94.refs_2_, bf16[768,640]{1,0:T(8,128)(2,1)} %get-tuple-element.95.refs_3_, ...), custom_call_target="tpu_custom_call" | custom-call | flops 1000 | bytes 1000 | tf_op jit(solution)/shard_map/weight_grad/pallas_call | solution.py:523
  277.9 11.9 %weight_grad.6.refs_8_ = bf16[768,1536]{1,0:T(8,128)(2,1)} custom-call(bf16[768,640]{1,0:T(8,128)(2,1)} %get-tuple-element.100.refs_0_, bf16[768,640]{1,0:T(8,128)(2,1)} %get-tuple-element.101.refs_1_, bf16[768,640]{1,0:T(8,128)(2,1)} %get-tuple-element.102.refs_2_, bf16[768,640]{1,0:T(8,128)(2,1)} %get-tuple-element.103.refs_3_, ...), custom_call_target="tpu_custom_call" | custom-call | flops 1000 | bytes 1000 | tf_op jit(solution)/shard_map/weight_grad/pallas_call | solution.py:523
  289.7 4.7 collective-permute-done.21
  294.5 3.7 add_convert_fusion.2.refs_16_
  298.3 12.1 %weight_grad.7.refs_15_ = bf16[768,1536]{1,0:T(8,128)(2,1)} custom-call(bf16[768,640]{1,0:T(8,128)(2,1)} %get-tuple-element.92.refs_0_, bf16[768,640]{1,0:T(8,128)(2,1)} %get-tuple-element.93.refs_1_, bf16[768,640]{1,0:T(8,128)(2,1)} %get-tuple-element.94.refs_2_, bf16[768,640]{1,0:T(8,128)(2,1)} %get-tuple-element.95.refs_3_, ...), custom_call_target="tpu_custom_call" | custom-call | flops 1000 | bytes 1000 | tf_op jit(solution)/shard_map/weight_grad/pallas_call | solution.py:523
  313.3 3.6 fusion.5.refs_14_
  320.4 13.2 %combine_back.1 = (f32[1024,768]{1,0:T(8,128)}, bf16[1024,768]{1,0:T(8,128)(2,1)}, bf16[1024,768]{1,0:T(8,128)(2,1)}, f32[1,768]{1,0:T(1,128)S(1)}, f32[1024,128]{1,0:T(8,128)S(1)}) custom-call(bf16[656,768]{1,0:T(8,128)(2,1)S(1)} %copy-done.9, bf16[656,768]{1,0:T(8,128)(2,1)S(1)} %copy-done.8, ...), custom_call_target="tpu_custom_call" | custom-call | flops 1000 | bytes 1000 | tf_op jit(solution)/shard_map/combine_back/pallas_call | solution.py:595
  334.5 3.7 add_convert_fusion.1.rest_0_
  338.1 30.7 %attention_backward.1 = (bf16[3,1024,768]{2,1,0:T(8,128)(2,1)}, f32[6,2,256]{2,1,0:T(2,128)}, f32[6,2,128]{2,1,0:T(2,128)}) custom-call(f32[12]{0:T(128)} %bitcast_convert_fusion.far_ref, bf16[1024,2304]{1,0:T(8,128)(2,1)} %convolution_convert_fusion.q_ref.k_ref.v_ref, bf16[1024,2304]{1,0:T(8,128)(2,1)} %convolution_convert_fusion.q_ref.k_ref.v_ref, ...), custom_call_target="tpu_custom_call" | custom-call | flops 1000 | bytes 1000 | tf_op jit(solution)/shard_map/attention_backward/pallas_call | solution.py:230
  378.8 11.5 %qkv_grad.1 = (bf16[384,3328]{1,0:T(8,128)(2,1)S(1)}, bf16[384,3328]{1,0:T(8,128)(2,1)}) custom-call(bf16[768,1024]{1,0:T(8,128)(2,1)S(1)} %copy-done.27, bf16[3,1024,768]{2,1,0:T(8,128)(2,1)} %get-tuple-element.118.grad_ref.dqkv_ref, bf16[768,1024]{1,0:T(8,128)(2,1)S(1)} %bitcast.39, bf16[1024,768]{1,0:T(8,128)(2,1)S(1)} %copy-done.28, ...), custom_call_target="tpu_custom_call" | custom-call | flops 1000 | bytes 1000 | tf_op jit(solution)/shard_map/qkv_grad/pallas_call | solution.py:723
  391.7 5.1 %collective-permute-done.23 = bf16[384,3328]{1,0:T(8,128)(2,1)} collective-permute-done((bf16[384,3328]{1,0:T(8,128)(2,1)}, bf16[384,3328]{1,0:T(8,128)(2,1)}, u32[]{:S(2)}, u32[]{:S(2)}) %collective-permute-start.23) | collective-permute-done | bytes 2555936 | tf_op jit(solution)/shard_map/ppermute | solution.py:759
  396.9 3.1 add_convert_fusion
  403.6 13.7 %collective-permute-done.24 = bf16[96,3328]{1,0:T(8,128)(2,1)S(1)} collective-permute-done((bf16[96,3328]{1,0:T(8,128)(2,1)S(1)}, bf16[96,3328]{1,0:T(8,128)(2,1)S(1)}, u32[]{:S(2)}, u32[]{:S(2)}) %collective-permute-start.24) | collective-permute-done | bytes 639008 | tf_op jit(solution)/shard_map/ppermute | solution.py:768
  417.4 12.7 %collective-permute-done.26 = bf16[96,3328]{1,0:T(8,128)(2,1)S(1)} collective-permute-done((bf16[96,3328]{1,0:T(8,128)(2,1)S(1)}, bf16[96,3328]{1,0:T(8,128)(2,1)S(1)}, u32[]{:S(2)}, u32[]{:S(2)}) %collective-permute-start.26) | collective-permute-done | bytes 639008 | tf_op jit(solution)/shard_map/ppermute | solution.py:768
  433.5 9.2 %collective-permute-start.27 = (bf16[24,3328]{1,0:T(8,128)(2,1)}, bf16[24,3328]{1,0:T(8,128)(2,1)}, u32[]{:S(2)}, u32[]{:S(2)}) collective-permute-start(bf16[24,3328]{1,0:T(8,128)(2,1)} %get-tuple-element.185), channel_id=1, source_target_pairs={{0,8},{8,0},{16,24},{24,16},{1,9},{9,1},{17,25},{25,17},{2,10},{10... | collective-permute-start | bytes 479240 | tf_op jit(solution)/shard_map/ppermute | solution.py:778
  445.3 6.4 %convolution_convert_fusion.1.w_ref = bf16[768,2304]{1,0:T(8,128)(2,1)} fusion(s32[768]{0:T(1024)S(1)} %fusion.51, bf16[384,3200]{1,0:T(8,128)(2,1)S(1)} %copy-done.41, bf16[384,3200]{1,0:T(8,128)(2,1)} %collective-permute-done.6), kind=kOutput, calls=%fused_computation.11 | convolution fusion | flops 2727346176 | bytes 8457216 | tf_op jit(solution)/shard_map/dot_general | solution.py:838
  459.5 6.6 %final_tokens.1 = f32[1024,768]{1,0:T(8,128)} custom-call(bf16[3,1024,768]{2,1,0:T(8,128)(2,1)S(1)} %copy-done, bf16[768,2304]{1,0:T(8,128)(2,1)S(1)} %copy-done.23, bf16[1024,768]{1,0:T(8,128)(2,1)S(1)} %copy-done.1, f32[1,768]{1,0:T(1,128)S(1)} %get-tuple-element.188.gain_ref, f32[1024,768]{1,0:T(8,128)S(1)} %copy-done.24, ...), custom_call_target="tpu_custom_call" | custom-call | flops 1000 | bytes 1000 | tf_op jit(solution)/shard_map/final_tokens/pallas_call | solution.py:674
  466.1 8.6 %combine_output.1 = bf16[1024,768]{1,0:T(8,128)(2,1)} custom-call(bf16[640,768]{1,0:T(8,128)(2,1)S(1)} %copy-done.32, bf16[640,768]{1,0:T(8,128)(2,1)} %collective-permute-done.12.rest_1_.refs_1_, bf16[640,768]{1,0:T(8,128)(2,1)} %collective-permute-done.14.rest_2_.refs_2_, bf16[640,768]{1,0:T(8,128)(2,1)} %collective-permute-done.18.rest_3_.refs_3_, ...), custom_call_target="tpu_custom_call" | custom-call | flops 1000 | bytes 1000 | tf_op jit(solution)/shard_map/combine_output/pallas_call | solution.py:641
  (246 shorter events, 100.3 us)
Async XLA Ops:
  7.2 128.2 %all-gather.3.cloned.1.call-start = ((), (), s32[]{:S(2)}) async-start(), calls=%async_computation.2 | async-start | bytes 2949120 | tf_op jit(solution)/shard_map/all_gather | solution.py:808
  9.9 15.6 %collective-permute-start.1 = (bf16[24,3200]{1,0:T(8,128)(2,1)}, bf16[24,3200]{1,0:T(8,128)(2,1)S(1)}, u32[]{:S(2)}, u32[]{:S(2)}) collective-permute-start(bf16[24,3200]{1,0:T(8,128)(2,1)} %get-tuple-element.191), channel_id=1, source_target_pairs={{0,16},{8,24},{16,0},{24,8},{1,17},{9,25},{17,1},{25,9},{2,18},{10... | collective-permute-start | bytes 460808 | tf_op jit(solution)/shard_map/ppermute | solution.py:747
  13.9 11.6 %collective-permute-start = (bf16[24,3200]{1,0:T(8,128)(2,1)}, bf16[24,3200]{1,0:T(8,128)(2,1)}, u32[]{:S(2)}, u32[]{:S(2)}) collective-permute-start(bf16[24,3200]{1,0:T(8,128)(2,1)} %get-tuple-element.191), channel_id=1, source_target_pairs={{0,8},{8,0},{16,24},{24,16},{1,9},{9,1},{17,25},{25,17},{2,10},{10... | collective-permute-start | bytes 460808 | tf_op jit(solution)/shard_map/ppermute | solution.py:747
  15.5 10.5 %collective-permute-start.2 = (bf16[24,3200]{1,0:T(8,128)(2,1)}, bf16[24,3200]{1,0:T(8,128)(2,1)}, u32[]{:S(2)}, u32[]{:S(2)}) collective-permute-start(bf16[24,3200]{1,0:T(8,128)(2,1)} %get-tuple-element.191), channel_id=1, source_target_pairs={{0,24},{8,16},{16,8},{24,0},{1,25},{9,17},{17,9},{25,1},{2,26},{10... | collective-permute-start | bytes 460808 | tf_op jit(solution)/shard_map/ppermute | solution.py:747
  15.5 119.8 %all-gather.5.cloned.1.call-start = ((), (), s32[]{:S(2)}) async-start(), calls=%async_computation.3 | async-start | bytes 2949120 | tf_op jit(solution)/shard_map/all_gather | solution.py:809
  27.4 29.1 %collective-permute-start.5 = (bf16[96,3200]{1,0:T(8,128)(2,1)S(1)}, bf16[96,3200]{1,0:T(8,128)(2,1)S(1)}, u32[]{:S(2)}, u32[]{:S(2)}) collective-permute-start(bf16[96,3200]{1,0:T(8,128)(2,1)S(1)} %pad_maximum_fusion.1), channel_id=1, source_target_pairs={{0,6},{1,7},{2,4},{3,5},{4,2},{5,3},{6,0},{7,1},{8,14},{9,15},{10,... | collective-permute-start | bytes 1843208 | tf_op jit(solution)/shard_map/ppermute | solution.py:751
  29.9 26.5 %collective-permute-start.4 = (bf16[96,3200]{1,0:T(8,128)(2,1)S(1)}, bf16[96,3200]{1,0:T(8,128)(2,1)S(1)}, u32[]{:S(2)}, u32[]{:S(2)}) collective-permute-start(bf16[96,3200]{1,0:T(8,128)(2,1)S(1)} %pad_maximum_fusion.1), channel_id=1, source_target_pairs={{0,4},{1,5},{2,6},{3,7},{4,0},{5,1},{6,2},{7,3},{8,12},{9,13},{10,... | collective-permute-start | bytes 1843208 | tf_op jit(solution)/shard_map/ppermute | solution.py:751
  30.4 25.9 %collective-permute-start.3 = (bf16[96,3200]{1,0:T(8,128)(2,1)S(1)}, bf16[96,3200]{1,0:T(8,128)(2,1)S(1)}, u32[]{:S(2)}, u32[]{:S(2)}) collective-permute-start(bf16[96,3200]{1,0:T(8,128)(2,1)S(1)} %pad_maximum_fusion.1), channel_id=1, source_target_pairs={{0,2},{1,3},{2,0},{3,1},{4,6},{5,7},{6,4},{7,5},{8,10},{9,11},{10,... | collective-permute-start | bytes 1843208 | tf_op jit(solution)/shard_map/ppermute | solution.py:751
  58.0 6.6 %collective-permute-start.6 = (bf16[384,3200]{1,0:T(8,128)(2,1)}, bf16[384,3200]{1,0:T(8,128)(2,1)}, u32[]{:S(2)}, u32[]{:S(2)}) collective-permute-start(bf16[384,3200]{1,0:T(8,128)(2,1)} %held.4.refs_3_), channel_id=1, source_target_pairs={{0,1},{1,0},{2,3},{3,2},{4,5},{5,4},{6,7},{7,6},{8,9},{9,8},{10,11... | collective-permute-start | bytes 7372808 | tf_op jit(solution)/shard_map/ppermute | solution.py:753
  58.1 316.2 %reduce-scatter.3.cloned.1.call-start = ((), (), s32[]{:S(2)}) async-start(), calls=%async_computation.4 | async-start | bytes 2949120 | tf_op jit(solution)/shard_map/reduce_scatter | solution.py:895
  62.5 24.4 %collective-permute-start.7 = (bf16[656,768]{1,0:T(8,128)(2,1)}, bf16[656,768]{1,0:T(8,128)(2,1)}, u32[]{:S(2)}, u32[]{:S(2)}) collective-permute-start(bf16[656,768]{1,0:T(8,128)(2,1)} %get-tuple-element.72), channel_id=1, source_target_pairs={{0,2},{1,3},{2,0},{3,1},{4,6},{5,7},{6,4},{7,5},{8,10},{9,11},{10,... | collective-permute-start | bytes 3022856 | tf_op jit(solution)/shard_map/ppermute | solution.py:825
  64.0 24.2 %collective-permute-start.8 = (bf16[656,768]{1,0:T(8,128)(2,1)}, bf16[656,768]{1,0:T(8,128)(2,1)}, u32[]{:S(2)}, u32[]{:S(2)}) collective-permute-start(bf16[656,768]{1,0:T(8,128)(2,1)} %get-tuple-element.73), channel_id=1, source_target_pairs={{0,4},{1,5},{2,6},{3,7},{4,0},{5,1},{6,2},{7,3},{8,12},{9,13},{10,... | collective-permute-start | bytes 3022856 | tf_op jit(solution)/shard_map/ppermute | solution.py:825
  135.4 8.2 %collective-permute-start.10 = (bf16[768,1536]{1,0:T(8,128)(2,1)}, bf16[768,1536]{1,0:T(8,128)(2,1)}, u32[]{:S(2)}, u32[]{:S(2)}) collective-permute-start(bf16[768,1536]{1,0:T(8,128)(2,1)} %held.7.out_own), channel_id=1, source_target_pairs={{0,1},{1,0},{2,3},{3,2},{4,5},{5,4},{6,7},{7,6},{8,9},{9,8},{10,11... | collective-permute-start | bytes 7077896 | tf_op jit(solution)/shard_map/ppermute | solution.py:875
  135.9 30.7 %collective-permute-start.11 = (bf16[656,768]{1,0:T(8,128)(2,1)}, bf16[656,768]{1,0:T(8,128)(2,1)S(1)}, u32[]{:S(2)}, u32[]{:S(2)}) collective-permute-start(bf16[656,768]{1,0:T(8,128)(2,1)} %copy-done.37), channel_id=1, source_target_pairs={{0,2},{1,3},{2,0},{3,1},{4,6},{5,7},{6,4},{7,5},{8,10},{9,11},{10,... | collective-permute-start | bytes 3022856 | tf_op jit(solution)/shard_map/ppermute | solution.py:825
  136.4 67.0 %collective-permute-start.13 = (bf16[656,768]{1,0:T(8,128)(2,1)}, bf16[656,768]{1,0:T(8,128)(2,1)}, u32[]{:S(2)}, u32[]{:S(2)}) collective-permute-start(bf16[656,768]{1,0:T(8,128)(2,1)} %copy-done.36), channel_id=1, source_target_pairs={{0,4},{1,5},{2,6},{3,7},{4,0},{5,1},{6,2},{7,3},{8,12},{9,13},{10,... | collective-permute-start | bytes 3022856 | tf_op jit(solution)/shard_map/ppermute | solution.py:825
  137.9 89.7 %collective-permute-start.16 = (bf16[656,768]{1,0:T(8,128)(2,1)}, bf16[656,768]{1,0:T(8,128)(2,1)}, u32[]{:S(2)}, u32[]{:S(2)}) collective-permute-start(bf16[656,768]{1,0:T(8,128)(2,1)} %get-tuple-element.87), channel_id=1, source_target_pairs={{0,6},{1,7},{2,4},{3,5},{4,2},{5,3},{6,0},{7,1},{8,14},{9,15},{10,... | collective-permute-start | bytes 3022856 | tf_op jit(solution)/shard_map/ppermute | solution.py:825
  140.2 87.4 %collective-permute-start.15 = (bf16[656,768]{1,0:T(8,128)(2,1)}, bf16[656,768]{1,0:T(8,128)(2,1)}, u32[]{:S(2)}, u32[]{:S(2)}) collective-permute-start(bf16[656,768]{1,0:T(8,128)(2,1)} %copy-done.35), channel_id=1, source_target_pairs={{0,6},{1,7},{2,4},{3,5},{4,2},{5,3},{6,0},{7,1},{8,14},{9,15},{10,... | collective-permute-start | bytes 3022856 | tf_op jit(solution)/shard_map/ppermute | solution.py:825
  190.2 37.5 %collective-permute-start.17 = (bf16[656,768]{1,0:T(8,128)(2,1)}, bf16[656,768]{1,0:T(8,128)(2,1)S(1)}, u32[]{:S(2)}, u32[]{:S(2)}) collective-permute-start(bf16[656,768]{1,0:T(8,128)(2,1)} %get-tuple-element.84.rest_0_), channel_id=1, source_target_pairs={{0,2},{1,3},{2,0},{3,1},{4,6},{5,7},{6,4},{7,5},{8,10},{9,11},{10,... | collective-permute-start | bytes 3022856 | tf_op jit(solution)/shard_map/ppermute | solution.py:885
  226.1 27.0 %collective-permute-start.19 = (bf16[656,768]{1,0:T(8,128)(2,1)}, bf16[656,768]{1,0:T(8,128)(2,1)}, u32[]{:S(2)}, u32[]{:S(2)}) collective-permute-start(bf16[656,768]{1,0:T(8,128)(2,1)} %get-tuple-element.88.rest_1_), channel_id=1, source_target_pairs={{0,4},{1,5},{2,6},{3,7},{4,0},{5,1},{6,2},{7,3},{8,12},{9,13},{10,... | collective-permute-start | bytes 3022856 | tf_op jit(solution)/shard_map/ppermute | solution.py:885
  251.7 25.2 %collective-permute-start.20 = (bf16[656,768]{1,0:T(8,128)(2,1)}, bf16[656,768]{1,0:T(8,128)(2,1)S(1)}, u32[]{:S(2)}, u32[]{:S(2)}) collective-permute-start(bf16[656,768]{1,0:T(8,128)(2,1)} %get-tuple-element.91), channel_id=1, source_target_pairs={{0,6},{1,7},{2,4},{3,5},{4,2},{5,3},{6,0},{7,1},{8,14},{9,15},{10,... | collective-permute-start | bytes 3022856 | tf_op jit(solution)/shard_map/ppermute | solution.py:885
  298.2 153.4 %reduce-scatter.5.cloned.1.call-start = ((), (), s32[]{:S(2)}) async-start(), calls=%async_computation.5 | async-start | bytes 2949120 | tf_op jit(solution)/shard_map/reduce_scatter | solution.py:895
  310.4 24.1 %collective-permute-start.22 = (bf16[768,1536]{1,0:T(8,128)(2,1)}, bf16[768,1536]{1,0:T(8,128)(2,1)}, u32[]{:S(2)}, u32[]{:S(2)}) collective-permute-start(bf16[768,1536]{1,0:T(8,128)(2,1)} %weight_grad.7.refs_15_), channel_id=1, source_target_pairs={{0,1},{1,0},{2,3},{3,2},{4,5},{5,4},{6,7},{7,6},{8,9},{9,8},{10,11... | collective-permute-start | bytes 7077896 | tf_op jit(solution)/shard_map/ppermute | solution.py:891
  316.9 58.7 %collective-permute-start.12 = (bf16[640,768]{1,0:T(8,128)(2,1)}, bf16[640,768]{1,0:T(8,128)(2,1)}, u32[]{:S(2)}, u32[]{:S(2)}) collective-permute-start(bf16[640,768]{1,0:T(8,128)(2,1)} %get-tuple-element.82), channel_id=1, source_target_pairs={{0,2},{1,3},{2,0},{3,1},{4,6},{5,7},{6,4},{7,5},{8,10},{9,11},{10,... | collective-permute-start | bytes 2949128 | tf_op jit(solution)/shard_map/ppermute | solution.py:825
  317.5 58.1 %collective-permute-start.14 = (bf16[640,768]{1,0:T(8,128)(2,1)}, bf16[640,768]{1,0:T(8,128)(2,1)}, u32[]{:S(2)}, u32[]{:S(2)}) collective-permute-start(bf16[640,768]{1,0:T(8,128)(2,1)} %get-tuple-element.85), channel_id=1, source_target_pairs={{0,4},{1,5},{2,6},{3,7},{4,0},{5,1},{6,2},{7,3},{8,12},{9,13},{10,... | collective-permute-start | bytes 2949128 | tf_op jit(solution)/shard_map/ppermute | solution.py:825
  318.9 56.7 %collective-permute-start.18 = (bf16[640,768]{1,0:T(8,128)(2,1)}, bf16[640,768]{1,0:T(8,128)(2,1)}, u32[]{:S(2)}, u32[]{:S(2)}) collective-permute-start(bf16[640,768]{1,0:T(8,128)(2,1)} %get-tuple-element.89), channel_id=1, source_target_pairs={{0,6},{1,7},{2,4},{3,5},{4,2},{5,3},{6,0},{7,1},{8,14},{9,15},{10,... | collective-permute-start | bytes 2949128 | tf_op jit(solution)/shard_map/ppermute | solution.py:825
  391.7 5.2 %collective-permute-start.23 = (bf16[384,3328]{1,0:T(8,128)(2,1)}, bf16[384,3328]{1,0:T(8,128)(2,1)}, u32[]{:S(2)}, u32[]{:S(2)}) collective-permute-start(bf16[384,3328]{1,0:T(8,128)(2,1)} %get-tuple-element.127), channel_id=1, source_target_pairs={{0,1},{1,0},{2,3},{3,2},{4,5},{5,4},{6,7},{7,6},{8,9},{9,8},{10,11... | collective-permute-start | bytes 7667720 | tf_op jit(solution)/shard_map/ppermute | solution.py:759
  400.1 17.3 %collective-permute-start.24 = (bf16[96,3328]{1,0:T(8,128)(2,1)S(1)}, bf16[96,3328]{1,0:T(8,128)(2,1)S(1)}, u32[]{:S(2)}, u32[]{:S(2)}) collective-permute-start(bf16[96,3328]{1,0:T(8,128)(2,1)S(1)} %get-tuple-element.182), channel_id=1, source_target_pairs={{0,2},{1,3},{2,0},{3,1},{4,6},{5,7},{6,4},{7,5},{8,10},{9,11},{10,... | collective-permute-start | bytes 1916936 | tf_op jit(solution)/shard_map/ppermute | solution.py:768
  400.8 29.4 %collective-permute-start.26 = (bf16[96,3328]{1,0:T(8,128)(2,1)S(1)}, bf16[96,3328]{1,0:T(8,128)(2,1)S(1)}, u32[]{:S(2)}, u32[]{:S(2)}) collective-permute-start(bf16[96,3328]{1,0:T(8,128)(2,1)S(1)} %get-tuple-element.183), channel_id=1, source_target_pairs={{0,6},{1,7},{2,4},{3,5},{4,2},{5,3},{6,0},{7,1},{8,14},{9,15},{10,... | collective-permute-start | bytes 1916936 | tf_op jit(solution)/shard_map/ppermute | solution.py:768
  401.7 29.8 %collective-permute-start.25 = (bf16[96,3328]{1,0:T(8,128)(2,1)S(1)}, bf16[96,3328]{1,0:T(8,128)(2,1)S(1)}, u32[]{:S(2)}, u32[]{:S(2)}) collective-permute-start(bf16[96,3328]{1,0:T(8,128)(2,1)S(1)} %get-tuple-element.184), channel_id=1, source_target_pairs={{0,4},{1,5},{2,6},{3,7},{4,0},{5,1},{6,2},{7,3},{8,12},{9,13},{10,... | collective-permute-start | bytes 1916936 | tf_op jit(solution)/shard_map/ppermute | solution.py:768
  433.5 41.2 %collective-permute-start.27 = (bf16[24,3328]{1,0:T(8,128)(2,1)}, bf16[24,3328]{1,0:T(8,128)(2,1)}, u32[]{:S(2)}, u32[]{:S(2)}) collective-permute-start(bf16[24,3328]{1,0:T(8,128)(2,1)} %get-tuple-element.185), channel_id=1, source_target_pairs={{0,8},{8,0},{16,24},{24,16},{1,9},{9,1},{17,25},{25,17},{2,10},{10... | collective-permute-start | bytes 479240 | tf_op jit(solution)/shard_map/ppermute | solution.py:778
  442.6 32.0 %collective-permute-start.29 = (bf16[24,3328]{1,0:T(8,128)(2,1)}, bf16[24,3328]{1,0:T(8,128)(2,1)}, u32[]{:S(2)}, u32[]{:S(2)}) collective-permute-start(bf16[24,3328]{1,0:T(8,128)(2,1)} %get-tuple-element.186), channel_id=1, source_target_pairs={{0,24},{8,16},{16,8},{24,0},{1,25},{9,17},{17,9},{25,1},{2,26},{10... | collective-permute-start | bytes 479240 | tf_op jit(solution)/shard_map/ppermute | solution.py:778
  445.3 29.4 %collective-permute-start.28 = (bf16[24,3328]{1,0:T(8,128)(2,1)}, bf16[24,3328]{1,0:T(8,128)(2,1)}, u32[]{:S(2)}, u32[]{:S(2)}) collective-permute-start(bf16[24,3328]{1,0:T(8,128)(2,1)} %get-tuple-element.187), channel_id=1, source_target_pairs={{0,16},{8,24},{16,0},{24,8},{1,17},{9,25},{17,1},{25,9},{2,18},{10... | collective-permute-start | bytes 479240 | tf_op jit(solution)/shard_map/ppermute | solution.py:778
  (52 other events, 602.0 us)
Sparse Core Ops, SparseCore 0:
  15.6 51.9 all-gather.2
  69.2 50.6 all-gather.4
  298.3 54.6 reduce-scatter.2
  391.9 55.3 reduce-scatter.4

commit v2 on v1

--- a/solution.py
+++ b/solution.py
@@ -317,10 +317,11 @@
     out_refs = rest[-experts:]
     slots = out_refs[0].shape[0] - TAIL
     tokens = values_ref.shape[0]
+    own = pl.ds(pl.program_id(0), 1)
     place = lax.broadcasted_iota(jnp.int32, (slots, tokens), 0)
-    hot = (place == dest_ref[0]).astype(F32).astype(BF16)
+    hot = (place == dest_ref[own, :]).astype(F32).astype(BF16)
     rows = dot_nn(hot, values_ref[...]).astype(BF16)
-    pieces = split_three(jnp.broadcast_to(gate_ref[0], (TAIL, tokens)))
+    pieces = split_three(jnp.broadcast_to(gate_ref[own, :], (TAIL, tokens)))
     line = lax.broadcasted_iota(jnp.int32, (TAIL, tokens), 0)
     stacked = jnp.zeros((TAIL, tokens), F32)
     for index, piece in enumerate(pieces):
@@ -335,21 +336,18 @@
             out_ref[slots:, :slots] = tail
 
 
-def dispatch(dest_row, values, gate_row, slots, ahead=()):
-    experts = dest_row.shape[0]
+def dispatch(experts, dest_row, values, gate_row, slots, ahead=()):
     tokens, width = values.shape
     return pl.pallas_call(
         functools.partial(dispatch_kernel, experts),
         grid=(experts,),
         in_specs=[
-            pl.BlockSpec((1, 1, tokens), lambda m: (m, 0, 0)),
-            whole((tokens, width)),
-            pl.BlockSpec((1, 1, tokens), lambda m: (m, 0, 0)),
+            whole(dest_row.shape), whole((tokens, width)), whole(gate_row.shape),
         ]
         + [ANY] * len(ahead),
         out_specs=[whole((slots + TAIL, width))] * experts,
         out_shape=[jax.ShapeDtypeStruct((slots + TAIL, width), BF16)] * experts,
-        compiler_params=pltpu.CompilerParams(vmem_limit_bytes=40 * MIB),
+        compiler_params=pltpu.CompilerParams(vmem_limit_bytes=60 * MIB),
         cost_estimate=LIGHT,
         name="dispatch_rows",
     )(dest_row, values, gate_row, *ahead)
@@ -372,47 +370,64 @@
     )(*values, *ahead)
 
 
+def as_columns(ref):
+    rows = ref[...].astype(F32)
+    filler = jnp.full((128 - rows.shape[0], rows.shape[1]), -1.0, F32)
+    return jnp.concatenate([rows, filler], axis=0).T.astype(jnp.int32)
+
+
 def post_kernel(
-    mixed_ref, w_ref, tokens_ref, gain_ref, router_ref, dest_ref, move_ref, *rest
+    mixed_ref, w_ref, w_rest, tokens_ref, gain_ref, router_ref, dest_ref, move_ref, *rest
 ):
-    residual_ref, normed_ref, gates_ref, moved_ref = rest[-4:]
+    residual_ref, normed_ref, gates_ref, turned_ref, moved_ref = rest[-5:]
+    half = w_ref.shape[0]
     moved = dot_nn(mixed_ref[...], move_ref[...]).astype(BF16)
     moved_ref[...] = moved
-    residual = tokens_ref[...].astype(F32) + dot_nn(moved, w_ref[...])
+    residual = dot_nn(moved[:, :half], w_ref[...]) + dot_nn(moved[:, half:], w_rest[...])
+    residual = tokens_ref[...].astype(F32) + residual
     residual_ref[...] = residual
     scale = lax.rsqrt(jnp.mean(residual * residual, axis=1, keepdims=True) + EPS)
     normed = (residual * scale * gain_ref[...]).astype(BF16)
     normed_ref[...] = normed
     logits = dot_nn(normed, router_ref[...])
-    chosen = dest_ref[...] >= 0
+    chosen = as_columns(dest_ref) >= 0
     logits = jnp.where(chosen, logits, NEG)
     peak = jnp.max(logits, axis=1, keepdims=True)
     weights = jnp.where(chosen, jnp.exp(logits - peak), 0.0)
-    gates_ref[...] = weights / jnp.sum(weights, axis=1, keepdims=True)
-
-
-def post_attention(mixed, w_out, tokens, gain, router, dest_col, move, ahead=()):
+    gates = weights / jnp.sum(weights, axis=1, keepdims=True)
+    gates_ref[...] = gates
+    turned_ref[...] = gates.T[: turned_ref.shape[0]]
+
+
+def post_attention(mixed, w_top, w_rest, tokens, gain, router, dest_row, move, ahead=()):
     rows, width = tokens.shape
+    lines = dest_row.shape[0]
     block = lambda n: pl.BlockSpec((ROWS, n), lambda i: (i, 0))
     return pl.pallas_call(
         post_kernel,
         grid=(rows // ROWS,),
         in_specs=[
-            block(width), pl.BlockSpec((width, width), lambda i: (0, 3)), block(width),
-            whole((1, width)), whole((width, 128)), block(128), whole((width, width)),
+            block(width), pl.BlockSpec((width // 2, width), lambda i: (0, 3)),
+            pl.BlockSpec((width // 2, width), lambda i: (0, 3)), block(width),
+            whole((1, width)), whole((width, 128)),
+            pl.BlockSpec((lines, ROWS), lambda i: (0, i)), whole((width, width)),
         ]
         + [ANY] * len(ahead),
-        out_specs=[block(width), block(width), block(128), block(width)],
+        out_specs=[
+            block(width), block(width), block(128),
+            pl.BlockSpec((lines, ROWS), lambda i: (0, i)), block(width),
+        ],
         out_shape=[
             jax.ShapeDtypeStruct((rows, width), F32),
             jax.ShapeDtypeStruct((rows, width), BF16),
             jax.ShapeDtypeStruct((rows, 128), F32),
+            jax.ShapeDtypeStruct((lines, rows), F32),
             jax.ShapeDtypeStruct((rows, width), BF16),
         ],
-        compiler_params=pltpu.CompilerParams(vmem_limit_bytes=32 * MIB),
+        compiler_params=pltpu.CompilerParams(vmem_limit_bytes=60 * MIB),
         cost_estimate=LIGHT,
         name="post_attention",
-    )(mixed, w_out, tokens, gain, router, dest_col, move, *ahead)
+    )(mixed, w_top, w_rest, tokens, gain, router, dest_row, move, *ahead)
 
 
 def expert_kernel(
@@ -434,6 +449,7 @@
         back_sum[...] = jnp.zeros_like(back_sum)
 
     rows = rows_ref[:slots, :]
+    hiddens, d_pres = [], []
     for w_in, w_out, hid, dpre in (
         (in_own, out_own, hid_own, dpre_own),
         (in_other, out_other, hid_other, dpre_other),
@@ -448,8 +464,12 @@
         d_pre = (d_hidden * slope).astype(BF16)
         hid[...] = hidden_low
         dpre[...] = d_pre
-        made_sum[...] += dot_nt(hidden_low, w_out[...])
-        back_sum[...] += dot_nt(d_pre, w_in[...])
+        hiddens.append(hidden_low)
+        d_pres.append(d_pre)
+    both_out = jnp.concatenate([out_own[...], out_other[...]], axis=1)
+    both_in = jnp.concatenate([in_own[...], in_other[...]], axis=1)
+    made_sum[...] += dot_nt(jnp.concatenate(hiddens, axis=1), both_out)
+    back_sum[...] += dot_nt(jnp.concatenate(d_pres, axis=1), both_in)
 
     @pl.when(step == pl.num_programs(0) - 1)
     def _():
@@ -509,10 +529,9 @@
     turned = refs[:count]
     acts = refs[count : 2 * count]
     out_ref = refs[-1]
-    total = dot_nn(turned[0][...], acts[0][...])
-    for index in range(1, count):
-        total = total + dot_nn(turned[index][...], acts[index][...])
-    out_ref[...] = total.astype(BF16)
+    both_rows = jnp.concatenate([ref[...] for ref in turned], axis=1)
+    both_acts = jnp.concatenate([ref[...] for ref in acts], axis=0)
+    out_ref[...] = dot_nn(both_rows, both_acts).astype(BF16)
 
 
 def weight_grad(turned, acts, ahead=()):
@@ -553,9 +572,10 @@
 
     place = lax.broadcasted_iota(jnp.int32, (ROWS, slots), 1)
     lane = lax.broadcasted_iota(jnp.int32, (ROWS, 128), 1)
+    dest = as_columns(dest_ref)
     hot = jnp.concatenate(
         [
-            (place == dest_ref[:, index : index + 1]).astype(F32).astype(BF16)
+            (place == dest[:, index : index + 1]).astype(F32).astype(BF16)
             for index in range(count)
         ],
         axis=1,
@@ -587,7 +607,7 @@
     gain_grad[...] += jnp.sum(d_normed * unit, axis=0, keepdims=True)
 
 
-def combine_back(backs, dest_col, gates, residual, grad, gain, router_rows, w_out, ahead=()):
+def combine_back(backs, dest_row, gates, residual, grad, gain, router_rows, w_out, ahead=()):
     rows, width = residual.shape
     count = len(backs)
     slots = backs[0].shape[0] - TAIL
@@ -598,7 +618,8 @@
         in_specs=[pl.BlockSpec((slots, width), lambda i: (0, 0))] * count
         + [pl.BlockSpec((TAIL, width), lambda i: (slots // TAIL, 0))] * count
         + [
-            block(128), block(128), block(width), block(width), whole((1, width)),
+            pl.BlockSpec((dest_row.shape[0], ROWS), lambda i: (0, i)),
+            block(128), block(width), block(width), whole((1, width)),
             whole(router_rows.shape), whole((width, width)),
         ]
         + [ANY] * len(ahead),
@@ -614,10 +635,10 @@
             pltpu.VMEM((count * slots, width), BF16),
             pltpu.VMEM((count * TAIL, count * slots), BF16),
         ],
-        compiler_params=pltpu.CompilerParams(vmem_limit_bytes=48 * MIB),
+        compiler_params=pltpu.CompilerParams(vmem_limit_bytes=60 * MIB),
         cost_estimate=LIGHT,
         name="combine_back",
-    )(*backs, *backs, dest_col, gates, residual, grad, gain, router_rows, w_out, *ahead)
+    )(*backs, *backs, dest_row, gates, residual, grad, gain, router_rows, w_out, *ahead)
 
 
 def output_kernel(count, *refs):
@@ -626,14 +647,15 @@
     out_ref = refs[-1]
     slots = mades[0].shape[0]
     place = lax.broadcasted_iota(jnp.int32, (ROWS, slots), 1)
+    dest = as_columns(dest_ref)
     total = residual_ref[...]
     for index, made in enumerate(mades):
-        hot = (place == dest_ref[:, index : index + 1]).astype(F32).astype(BF16)
+        hot = (place == dest[:, index : index + 1]).astype(F32).astype(BF16)
         total = total + gates_ref[:, index : index + 1] * dot_nn(hot, made[...])
     out_ref[...] = total.astype(BF16)
 
 
-def combine_output(mades, dest_col, gates, residual, ahead=()):
+def combine_output(mades, dest_row, gates, residual, ahead=()):
     rows, width = residual.shape
     count = len(mades)
     slots = mades[0].shape[0]
@@ -642,14 +664,14 @@
         functools.partial(output_kernel, count),
         grid=(rows // ROWS,),
         in_specs=[pl.BlockSpec((slots, width), lambda i: (0, 0))] * count
-        + [block(128), block(128), block(width)]
+        + [pl.BlockSpec((dest_row.shape[0], ROWS), lambda i: (0, i)), block(128), block(width)]
         + [ANY] * len(ahead),
         out_specs=block(width),
         out_shape=jax.ShapeDtypeStruct((rows, width), BF16),
-        compiler_params=pltpu.CompilerParams(vmem_limit_bytes=40 * MIB),
+        compiler_params=pltpu.CompilerParams(vmem_limit_bytes=60 * MIB),
         cost_estimate=LIGHT,
         name="combine_output",
-    )(*mades, dest_col, gates, residual, *ahead)
+    )(*mades, dest_row, gates, residual, *ahead)
 
 
 def final_kernel(dqkv_ref, w_ref, tokens_ref, gain_ref, d_residual_ref, *rest):
@@ -681,7 +703,7 @@
         + [ANY] * len(ahead),
         out_specs=block(width),
         out_shape=jax.ShapeDtypeStruct((rows, width), F32),
-        compiler_params=pltpu.CompilerParams(vmem_limit_bytes=40 * MIB),
+        compiler_params=pltpu.CompilerParams(vmem_limit_bytes=60 * MIB),
         cost_estimate=LIGHT,
         name="final_tokens",
     )(d_qkv, w_all, tokens, gain, d_residual, *ahead)
@@ -730,7 +752,7 @@
         + [ANY] * len(ahead),
         out_specs=[pl.BlockSpec((width // 2, BLK), lambda j: (0, j))] * 2,
         out_shape=[jax.ShapeDtypeStruct((width // 2, 4 * width + BLK), BF16)] * 2,
-        compiler_params=pltpu.CompilerParams(vmem_limit_bytes=40 * MIB),
+        compiler_params=pltpu.CompilerParams(vmem_limit_bytes=60 * MIB),
         cost_estimate=LIGHT,
         name="qkv_grad",
     )(turned, d_qkv, mixed_turned, branch, extra, *ahead)
@@ -740,18 +762,22 @@
     return [(i, i ^ offset) for i in range(size)]
 
 
-def gather_rows(block, ahead):
-    dp_size, fsdp_size = lax.axis_size("dp"), lax.axis_size("fsdp")
+def gather_line(block):
+    dp_size = lax.axis_size("dp")
     line = [block]
     for m in range(1, dp_size):
         line.append(lax.ppermute(block, "dp", pairs_of(dp_size, m)))
-    line = jnp.concatenate(line, axis=0)
+    return jnp.concatenate(line, axis=0)
+
+
+def gather_plane(line, ahead):
+    fsdp_size = lax.axis_size("fsdp")
     plane = [line]
     for m in range(1, fsdp_size // 2):
         plane.append(lax.ppermute(line, "fsdp", pairs_of(fsdp_size, 2 * m)))
     (plane,) = held([jnp.concatenate(plane, axis=0)], ahead)
     other = lax.ppermute(plane, "fsdp", pairs_of(fsdp_size, 1))
-    return plane, jnp.concatenate([plane, other], axis=0)
+    return plane, other, jnp.concatenate([plane, other], axis=0)
 
 
 def scatter_pair(keep, send):
@@ -817,20 +843,24 @@
     )
     rank = jnp.cumsum(hot, axis=0) - hot
     dest = jnp.where(hot > 0, rank, -1)
-    dest_col = jnp.pad(dest, ((0, 0), (0, 128 - experts)), constant_values=-1)
-    dest_row = dest.T.reshape(experts, 1, tok_rows)
+    lines = max(8, experts)
+    dest_row = jnp.pad(dest.T, ((0, lines - experts), (0, 0)), constant_values=-1)
 
     def exchange(pieces):
         return [pieces[0]] + [
             lax.ppermute(pieces[m], "fsdp", pairs_of(fsdp_size, 2 * m)) for m in range(1, experts)
         ]
 
-    sent_grads = dispatch(dest_row, d_out, jnp.zeros((experts, 1, tok_rows), F32), slots)
+    line = gather_line(jnp.concatenate([w_qkv, w_attn_out, small], axis=1))
+    sent_grads = dispatch(
+        experts, dest_row, d_out, jnp.zeros((lines, tok_rows), F32), slots, (line,)
+    )
     move = position_matrix(width)
-    moved_tokens = jnp.dot(tokens_in, move, preferred_element_type=F32)
-    plane, full = gather_rows(
-        jnp.concatenate([w_qkv, w_attn_out, small], axis=1), tuple(sent_grads[1:2])
-    )
+    (tokens_after,) = held([tokens_in], (line,))
+    tokens = tokens_after.astype(F32)
+    scale = lax.rsqrt(jnp.mean(tokens * tokens, axis=1, keepdims=True) + EPS)
+    unit = jnp.dot(tokens_after, move, preferred_element_type=F32) * scale
+    plane, plane_rest, full = gather_plane(line, (sent_grads[1], unit))
     grads_in = exchange([sent_grads[0]] + list(held(sent_grads[1:], (plane,))))
 
     moved_gain = full[:, 4 * width + experts].astype(F32).reshape(1, width)
@@ -855,19 +885,15 @@
     router_cols = jnp.dot(columns, swap.astype(BF16), preferred_element_type=F32).astype(BF16)
     router_rows = router_cols.T[: max(8, experts)].astype(F32)
 
-    tokens = tokens_in.astype(F32)
-    scale = lax.rsqrt(jnp.mean(tokens * tokens, axis=1, keepdims=True) + EPS)
-    normed_attn = (moved_tokens * scale * moved_gain).astype(BF16)
+    normed_attn = (unit * moved_gain).astype(BF16)
     qkv_rows = jnp.dot(normed_attn, full[:, : 3 * width], preferred_element_type=F32).astype(BF16)
     segments = segment_ids.reshape(tok_rows)
-    mixed, lse = attention_forward(
-        qkv_rows, segments, near, far, HEADS, tuple(grads_in[1:3])
-    )
-    residual, normed_ffn, gates, moved_mixed = post_attention(
-        mixed, full, tokens_in, gain_f, router_cols, dest_col, move
-    )
-    gate_row = gates[:, :experts].T.reshape(experts, 1, tok_rows)
-    sent_rows = dispatch(dest_row, normed_ffn, gate_row, slots)
+    mixed, lse = attention_forward(qkv_rows, segments, near, far, HEADS)
+    residual, normed_ffn, gates, gate_row, moved_mixed = post_attention(
+        mixed, plane, plane_rest, tokens_in, gain_f, router_cols, dest_row, move,
+        tuple(grads_in[1:3]),
+    )
+    sent_rows = dispatch(experts, dest_row, normed_ffn, gate_row, slots, tuple(grads_in[3:]))
     rows_in = exchange(sent_rows)
     (own_in,) = held([own_in], (mixed,))
     (own_out,) = held([own_out], (sent_rows[0],))
@@ -885,7 +911,6 @@
             lax.ppermute(back, "fsdp", pairs_of(fsdp_size, 2 * m)) if m > 0 else back
         )
     hid_own, hid_other, dpre_own, dpre_other, _, made, rows_turned, gexp_turned = zip(*chunks)
-    mades = exchange(made)
 
     def pair_sum(own, other):
         got = lax.ppermute(other, "fsdp", pairs_of(fsdp_size, 1))
@@ -897,17 +922,19 @@
     grad_in_own = weight_grad(rows_turned, dpre_own, tuple(backs[-2:-1]))
     grad_out_own = weight_grad(gexp_turned, hid_own, (grad_in_own,))
     grad_in_other = weight_grad(rows_turned, dpre_other, (grad_out_own,) + tuple(backs[-1:]))
-    grad_out_other = weight_grad(gexp_turned, hid_other, (grad_in_other,))
     pair_in = pair_sum(grad_in_own, grad_in_other)
+    grad_out_other = weight_grad(gexp_turned, hid_other, (pair_in,))
     pair_out = pair_sum(grad_out_own, grad_out_other)
     d_w_in, d_w_out = owners(pair_in), owners(pair_out)
+    mades = exchange([made[0]] + list(held(made[1:], (pair_out,))))
 
     d_residual, d_branch, d_mixed, d_gain_f, d_logits = combine_back(
-        backs, dest_col, gates, residual, d_out, gain_f, router_rows, back_attn, (grad_out_other, pair_in)
+        backs, dest_row, gates, residual, d_out, gain_f, router_rows, back_attn, (grad_out_other, pair_in, pair_out)
     )
     d_qkv, near_grad, far_grad = attention_backward(
-        qkv_rows, d_mixed, mixed, lse, segments, near, far, HEADS, (pair_out,)
-    )
+        qkv_rows, d_mixed, mixed, lse, segments, near, far, HEADS
+    )
+    near_grad, far_grad = held([near_grad, far_grad], tuple(mades[1:]))
     d_router = jnp.dot(normed_ffn.T, d_logits.astype(BF16), preferred_element_type=F32)
     d_router = jnp.dot(d_router, swap.T.astype(F32), precision=lax.Precision.HIGHEST)
     d_table = jnp.dot(
@@ -920,11 +947,14 @@
     late_cols = jnp.dot(move.T, late_cols.astype(BF16), preferred_element_type=F32)
     late_cols = jnp.pad(late_cols.astype(BF16), ((0, 0), (0, BLK - 128)))
     keep, send = qkv_grad(
-        normed_attn.T, d_qkv, moved_mixed.T, d_branch, late_cols, (d_w_in,) + tuple(mades[1:])
-    )
-    late = scatter_line(scatter_plane(scatter_pair(keep, send)))
-    block_out = combine_output(mades, dest_col, gates, residual, (keep,))
-    d_tokens = final_tokens(d_qkv, back_qkv, tokens_in, gain_a, d_residual, (d_w_out,))
+        normed_attn.T, d_qkv, moved_mixed.T, d_branch, late_cols, (d_w_in,)
+    )
+    keep, send = held([keep, send], (d_w_out,))
+    late = scatter_plane(scatter_pair(keep, send))
+    block_out = combine_output(mades, dest_row, gates, residual)
+    d_tokens = final_tokens(d_qkv, back_qkv, tokens_in, gain_a, d_residual, (block_out,))
+    (late,) = held([late], (d_tokens,))
+    late = scatter_line(late)
     own_qkv = late[:, : 3 * width]
     own_gain_a = jnp.sum(own_qkv * w_qkv.astype(F32), axis=1) / gain_attn.astype(F32)
     return (

time: 493 us -> 465 us (0.943)
  waiting for transfers between devices: 87.1 us -> 58.8 us
  local copies, waits for them, and re-layouts: 42.7 us -> 35.6 us
  starting transfers between devices: 39.4 us -> 32.8 us
  Pallas kernels: 249 us -> 255 us
    ppermute x3, waiting for transfers between devices: 27.9 us -> 3.53 us  [scatter_plane(): lax.ppermute(plane[m * rows:(m + 1) * rows], 'fsdp', pairs_of(fsdp_size,...]
    ppermute x7, waiting for transfers between devices: 24 us -> 9.13 us  [the longest x3 5.37 us: gather_plane(): plane.append(lax.ppermute(line, 'fsdp', pairs_of(fsdp_size, 2 * m)))]
    ppermute x9, waiting for transfers between devices: 22.5 us -> 7.99 us  [exchange(): lax.ppermute(pieces[m], 'fsdp', pairs_of(fsdp_size, 2 * m))]
    unnamed x107 -> x63, local copies, waits for them, and re-layouts: 30.5 us -> 17.6 us
    ppermute x3, waiting for transfers between devices: 0.01 us -> 12.1 us  [scatter_line(): lax.ppermute(line[m * rows:(m + 1) * rows], 'dp', pairs_of(dp_size, m))]
    pallas_call x4, Pallas kernels: 91.4 us -> 83.2 us  [expert_chunk(): pl.pallas_call(expert_kernel, grid=(steps,), in_specs=[whole((slots + TAI...]
    pallas_call x2, Pallas kernels: 13 us -> 19.8 us  [dispatch(): pl.pallas_call(functools.partial(dispatch_kernel, experts), grid=(experts...]
  transfers between devices with their start and end apart: 34 -> 34, of which waited for: 12 -> 16; matrix products, arithmetic and copies ran while one was open for 12% -> 14% of each run, Pallas kernels for 46% -> 54%
where the time goes in v2:
time: 465 us; the launch traced here: 456 us
  Pallas kernels  255 us (55%)
  waiting for transfers between devices  58.8 us (13%)
  local copies, waits for them, and re-layouts  35.6 us (8%)
  starting transfers between devices  32.8 us (7%)
  other arithmetic  31 us (7%)
  matrix products  27.7 us (6%)
  between operations  14.4 us (3%)
    pallas_call x4, Pallas kernels, expert_chunk(): pl.pallas_call(expert_kernel, grid=(steps,), in_specs=[whole((slots + TAI...  83.2 us
    pallas_call x4, Pallas kernels, weight_grad(): pl.pallas_call(functools.partial(weight_grad_kernel, count), grid=(half /...  43.4 us
    pallas_call x1, Pallas kernels, attention_backward(): pl.pallas_call(attn_bwd_kernel, grid_spec=pltpu.PrefetchScalarGridSpec(nu...  30.5 us
    pallas_call x1, Pallas kernels, attention_forward(): pl.pallas_call(attn_fwd_kernel, grid_spec=pltpu.PrefetchScalarGridSpec(nu...  21 us
    pallas_call x2, Pallas kernels, dispatch(): pl.pallas_call(functools.partial(dispatch_kernel, experts), grid=(experts...  19.8 us
    unnamed x63, local copies, waits for them, and re-layouts  17.6 us
    pallas_call x1, Pallas kernels, combine_back(): pl.pallas_call(functools.partial(combine_kernel, count), grid=(rows // RO...  14.9 us
    pallas_call x1, Pallas kernels, qkv_grad(): pl.pallas_call(functools.partial(qkv_grad_kernel, parts), grid=(4 * parts...  13.4 us
  transfers between devices with their start and end apart: 34, of which 16 were waited for; matrix products, arithmetic and copies ran while one was open for 14% of the time, Pallas kernels for 54%

profile of v2, /device:TPU:0, one launch (start us, length us, event | category | flops | bytes accessed | tf_op | source)
XLA Modules:
  0.0 455.7 jit_solution(14553702348903230640)
XLA Ops:
  9.0 4.1 collective-permute-start.1
  36.1 9.9 %dispatch_rows.2 = (bf16[656,768]{1,0:T(8,128)(2,1)}, bf16[656,768]{1,0:T(8,128)(2,1)}, bf16[656,768]{1,0:T(8,128)(2,1)}, bf16[656,768]{1,0:T(8,128)(2,1)}) custom-call(s32[8,1024]{1,0:T(8,128)} %pad.12.dest_ref.refs_4_.refs_8_, bf16[1024,768]{1,0:T(8,128)(2,1)} %refs_11_.1, f32[8,1024]{1,0:T(8,128)} %broadcast_in_dim.87.gate_ref, bf16[96,3200]{1,0:T(8,128)(2,1)} %copy-done.12), custom_call_target="tpu_custom_call" | custom-call | flops 1000 | bytes 1000 | tf_op jit(solution)/shard_map/dispatch_rows/pallas_call | solution.py:341
  46.0 3.6 copy.83.refs_2_
  49.6 5.4 %collective-permute-done.3 = bf16[96,3200]{1,0:T(8,128)(2,1)} collective-permute-done((bf16[96,3200]{1,0:T(8,128)(2,1)S(1)}, bf16[96,3200]{1,0:T(8,128)(2,1)}, u32[]{:S(2)}, u32[]{:S(2)}) %collective-permute-start.3) | collective-permute-done | bytes 614432 | tf_op jit(solution)/shard_map/ppermute | solution.py:777
  72.4 7.7 %convolution_convert_fusion.q_ref.k_ref.v_ref = bf16[1024,2304]{1,0:T(8,128)(2,1)} fusion(f32[1024,768]{0,1:T(8,128)S(1)} %copy-done.7, f32[768]{0:T(1024)S(1)} %convert_reduce_fusion, bf16[384,3200]{1,0:T(8,128)(2,1)S(1)} %copy-done.1, bf16[384,3200]{1,0:T(8,128)(2,1)} %collective-permute-done.6.w_rest), kind=kOutput, calls=%fused_computation | convolution fusion | flops 3634888704 | bytes 12782592 | tf_op jit(solution)/shard_map/dot_general | solution.py:889
  80.2 21.0 %attention_forward.1 = (bf16[1024,768]{1,0:T(8,128)(2,1)}, f32[6,2,1024]{2,1,0:T(2,128)}) custom-call(f32[12]{0:T(128)} %bitcast_convert_fusion.far_ref, bf16[1024,2304]{1,0:T(8,128)(2,1)} %convolution_convert_fusion.q_ref.k_ref.v_ref, bf16[1024,2304]{1,0:T(8,128)(2,1)} %convolution_convert_fusion.q_ref.k_ref.v_ref, ...), custom_call_target="tpu_custom_call" | custom-call | flops 1000 | bytes 1000 | tf_op jit(solution)/shard_map/attention_forward/pallas_call | solution.py:190
  102.3 8.0 %collective-permute-done.8.rest_1_.grads_ref = bf16[656,768]{1,0:T(8,128)(2,1)} collective-permute-done((bf16[656,768]{1,0:T(8,128)(2,1)}, bf16[656,768]{1,0:T(8,128)(2,1)}, u32[]{:S(2)}, u32[]{:S(2)}) %collective-permute-start.8) | collective-permute-done | bytes 1007648 | tf_op jit(solution)/shard_map/ppermute | solution.py:851
  110.3 9.8 %post_attention.1 = (f32[1024,768]{1,0:T(8,128)}, bf16[1024,768]{1,0:T(8,128)(2,1)}, f32[1024,128]{1,0:T(8,128)}, f32[8,1024]{1,0:T(8,128)}, bf16[1024,768]{1,0:T(8,128)(2,1)}) custom-call(bf16[1024,768]{1,0:T(8,128)(2,1)} %get-tuple-element.78.mixed_ref.refs_1_.o_ref, bf16[384,3200]{1,0:T(8,128)(2,1)} %held.10.refs_3_.w_ref, ...), custom_call_target="tpu_custom_call" | custom-call | flops 1000 | bytes 1000 | tf_op jit(solution)/shard_map/post_attention/pallas_call | solution.py:406
  121.0 9.9 %dispatch_rows.3 = (bf16[656,768]{1,0:T(8,128)(2,1)}, bf16[656,768]{1,0:T(8,128)(2,1)}, bf16[656,768]{1,0:T(8,128)(2,1)}, bf16[656,768]{1,0:T(8,128)(2,1)}) custom-call(s32[8,1024]{1,0:T(8,128)} %pad.12.dest_ref.refs_4_.refs_8_, bf16[1024,768]{1,0:T(8,128)(2,1)} %get-tuple-element.83.values_ref, f32[8,1024]{1,0:T(8,128)} %get-tuple-element.84.gate_ref, ...), custom_call_target="tpu_custom_call" | custom-call | flops 1000 | bytes 1000 | tf_op jit(solution)/shard_map/dispatch_rows/pallas_call | solution.py:341
  139.3 20.7 %expert_chunk.4 = (bf16[640,1536]{1,0:T(8,128)(2,1)}, bf16[640,1536]{1,0:T(8,128)(2,1)}, bf16[640,1536]{1,0:T(8,128)(2,1)}, bf16[640,1536]{1,0:T(8,128)(2,1)}, b...) custom-call(bf16[656,768]{1,0:T(8,128)(2,1)} %get-tuple-element.86.refs, ...), custom_call_target="tpu_custom_call" | custom-call | flops 1000 | bytes 1000 | tf_op jit(solution)/shard_map/expert_chunk/pallas_call | solution.py:497
  161.0 21.0 %expert_chunk.5 = (bf16[640,1536]{1,0:T(8,128)(2,1)}, bf16[640,1536]{1,0:T(8,128)(2,1)}, bf16[640,1536]{1,0:T(8,128)(2,1)}, bf16[640,1536]{1,0:T(8,128)(2,1)}, b...) custom-call(bf16[656,768]{1,0:T(8,128)(2,1)} %copy-done.15, ...), custom_call_target="tpu_custom_call" | custom-call | flops 1000 | bytes 1000 | tf_op jit(solution)/shard_map/expert_chunk/pallas_call | solution.py:497
  182.6 20.8 %expert_chunk.6 = (bf16[640,1536]{1,0:T(8,128)(2,1)}, bf16[640,1536]{1,0:T(8,128)(2,1)}, bf16[640,1536]{1,0:T(8,128)(2,1)}, bf16[640,1536]{1,0:T(8,128)(2,1)}, b...) custom-call(bf16[656,768]{1,0:T(8,128)(2,1)} %collective-permute-done.1, ...), custom_call_target="tpu_custom_call" | custom-call | flops 1000 | bytes 1000 | tf_op jit(solution)/shard_map/expert_chunk/pallas_call | solution.py:497
  203.4 3.1 collective-permute-done.15.rest_0_.refs_1_.refs_5_
  207.5 20.8 %expert_chunk.7 = (bf16[640,1536]{1,0:T(8,128)(2,1)}, bf16[640,1536]{1,0:T(8,128)(2,1)}, bf16[640,1536]{1,0:T(8,128)(2,1)}, bf16[640,1536]{1,0:T(8,128)(2,1)}, b...) custom-call(bf16[656,768]{1,0:T(8,128)(2,1)} %collective-permute-done.1, ...), custom_call_target="tpu_custom_call" | custom-call | flops 1000 | bytes 1000 | tf_op jit(solution)/shard_map/expert_chunk/pallas_call | solution.py:497
  229.6 10.7 %weight_grad.4.refs_8_ = bf16[768,1536]{1,0:T(8,128)(2,1)} custom-call(bf16[768,640]{1,0:T(8,128)(2,1)} %get-tuple-element.106.refs_0_, bf16[768,640]{1,0:T(8,128)(2,1)} %get-tuple-element.107.refs_1_, bf16[768,640]{1,0:T(8,128)(2,1)} %get-tuple-element.108.refs_2_, bf16[768,640]{1,0:T(8,128)(2,1)} %get-tuple-element.109.refs_3_, ...), custom_call_target="tpu_custom_call" | custom-call | flops 1000 | bytes 1000 | tf_op jit(solution)/shard_map/weight_grad/pallas_call | solution.py:542
  240.2 11.1 %weight_grad.5.refs_8_ = bf16[768,1536]{1,0:T(8,128)(2,1)} custom-call(bf16[768,640]{1,0:T(8,128)(2,1)} %get-tuple-element.98.refs_0_, bf16[768,640]{1,0:T(8,128)(2,1)} %get-tuple-element.99.refs_1_, bf16[768,640]{1,0:T(8,128)(2,1)} %get-tuple-element.100.refs_2_, bf16[768,640]{1,0:T(8,128)(2,1)} %get-tuple-element.101.refs_3_, ...), custom_call_target="tpu_custom_call" | custom-call | flops 1000 | bytes 1000 | tf_op jit(solution)/shard_map/weight_grad/pallas_call | solution.py:542
  253.9 10.8 %weight_grad.6 = bf16[768,1536]{1,0:T(8,128)(2,1)} custom-call(bf16[768,640]{1,0:T(8,128)(2,1)} %get-tuple-element.106.refs_0_, bf16[768,640]{1,0:T(8,128)(2,1)} %get-tuple-element.107.refs_1_, bf16[768,640]{1,0:T(8,128)(2,1)} %get-tuple-element.108.refs_2_, bf16[768,640]{1,0:T(8,128)(2,1)} %get-tuple-element.109.refs_3_, ...), custom_call_target="tpu_custom_call" | custom-call | flops 1000 | bytes 1000 | tf_op jit(solution)/shard_map/weight_grad/pallas_call | solution.py:542
  264.8 4.7 %collective-permute-done.18 = bf16[768,1536]{1,0:T(8,128)(2,1)S(1)} collective-permute-done((bf16[768,1536]{1,0:T(8,128)(2,1)}, bf16[768,1536]{1,0:T(8,128)(2,1)S(1)}, u32[]{:S(2)}, u32[]{:S(2)}) %collective-permute-start.18) | collective-permute-done | bytes 2359328 | tf_op jit(solution)/shard_map/ppermute | solution.py:916
  271.6 10.8 %weight_grad.7.refs_15_ = bf16[768,1536]{1,0:T(8,128)(2,1)} custom-call(bf16[768,640]{1,0:T(8,128)(2,1)} %get-tuple-element.98.refs_0_, bf16[768,640]{1,0:T(8,128)(2,1)} %get-tuple-element.99.refs_1_, bf16[768,640]{1,0:T(8,128)(2,1)} %get-tuple-element.100.refs_2_, bf16[768,640]{1,0:T(8,128)(2,1)} %get-tuple-element.101.refs_3_, ...), custom_call_target="tpu_custom_call" | custom-call | flops 1000 | bytes 1000 | tf_op jit(solution)/shard_map/weight_grad/pallas_call | solution.py:542
  282.6 4.6 %collective-permute-done.19 = bf16[768,1536]{1,0:T(8,128)(2,1)S(1)} collective-permute-done((bf16[768,1536]{1,0:T(8,128)(2,1)}, bf16[768,1536]{1,0:T(8,128)(2,1)S(1)}, u32[]{:S(2)}, u32[]{:S(2)}) %collective-permute-start.19) | collective-permute-done | bytes 2359328 | tf_op jit(solution)/shard_map/ppermute | solution.py:916
  292.0 3.2 fusion.7.refs_14_
  300.1 3.3 fusion.64.turned_ref
  303.4 14.9 %combine_back.1 = (f32[1024,768]{1,0:T(8,128)}, bf16[1024,768]{1,0:T(8,128)(2,1)}, bf16[1024,768]{1,0:T(8,128)(2,1)}, f32[1,768]{1,0:T(1,128)}, f32[1024,128]{1,0:T(8,128)}) custom-call(bf16[656,768]{1,0:T(8,128)(2,1)} %get-tuple-element.90.rest_0_.refs_0_.refs_4_, bf16[656,768]{1,0:T(8,128)(2,1)} %copy-done.9, bf16[656,768]{1,0:T(8,128)(2,1)} %copy-done.11, ...), custom_call_target="tpu_custom_call" | custom-call | flops 1000 | bytes 1000 | tf_op jit(solution)/shard_map/combine_back/pallas_call | solution.py:615
  318.3 30.5 %attention_backward.1 = (bf16[3,1024,768]{2,1,0:T(8,128)(2,1)}, f32[6,2,256]{2,1,0:T(2,128)}, f32[6,2,128]{2,1,0:T(2,128)}) custom-call(f32[12]{0:T(128)} %bitcast_convert_fusion.far_ref, bf16[1024,2304]{1,0:T(8,128)(2,1)} %convolution_convert_fusion.q_ref.k_ref.v_ref, bf16[1024,2304]{1,0:T(8,128)(2,1)} %convolution_convert_fusion.q_ref.k_ref.v_ref, ...), custom_call_target="tpu_custom_call" | custom-call | flops 1000 | bytes 1000 | tf_op jit(solution)/shard_map/attention_backward/pallas_call | solution.py:230
  359.8 13.4 %qkv_grad.1 = (bf16[384,3328]{1,0:T(8,128)(2,1)}, bf16[384,3328]{1,0:T(8,128)(2,1)}) custom-call(bf16[768,1024]{1,0:T(8,128)(2,1)} %fusion.64.turned_ref, bf16[3,1024,768]{2,1,0:T(8,128)(2,1)} %get-tuple-element.130.dqkv_ref.grad_ref, bf16[768,1024]{1,0:T(8,128)(2,1)} %bitcast.36, bf16[1024,768]{1,0:T(8,128)(2,1)} %get-tuple-element.133.branch_ref, ...), custom_call_target="tpu_custom_call" | custom-call | flops 1000 | bytes 1000 | tf_op jit(solution)/shard_map/qkv_grad/pallas_call | solution.py:745
  377.9 5.0 %collective-permute-done.23 = bf16[384,3328]{1,0:T(8,128)(2,1)S(1)} collective-permute-done((bf16[384,3328]{1,0:T(8,128)(2,1)}, bf16[384,3328]{1,0:T(8,128)(2,1)S(1)}, u32[]{:S(2)}, u32[]{:S(2)}) %collective-permute-start.23) | collective-permute-done | bytes 2555936 | tf_op jit(solution)/shard_map/ppermute | solution.py:785
  391.6 6.3 %convolution_convert_fusion.1.w_ref = bf16[768,2304]{1,0:T(8,128)(2,1)} fusion(s32[768]{0:T(1024)S(1)} %fusion.48, bf16[384,3200]{1,0:T(8,128)(2,1)S(1)} %copy-done.2, bf16[384,3200]{1,0:T(8,128)(2,1)} %collective-permute-done.6.w_rest), kind=kOutput, calls=%fused_computation.2 | convolution fusion | flops 2727346176 | bytes 8457216 | tf_op jit(solution)/shard_map/dot_general | solution.py:868
  397.9 9.8 %combine_output.1.rest_0_ = bf16[1024,768]{1,0:T(8,128)(2,1)} custom-call(bf16[640,768]{1,0:T(8,128)(2,1)} %get-tuple-element.88.refs_0_, bf16[640,768]{1,0:T(8,128)(2,1)} %copy-done.14, bf16[640,768]{1,0:T(8,128)(2,1)} %collective-permute-done.21.refs_2_.refs_3_, bf16[640,768]{1,0:T(8,128)(2,1)} %collective-permute-done.22.refs_3_.refs_4_, ...), custom_call_target="tpu_custom_call" | custom-call | flops 1000 | bytes 1000 | tf_op jit(solution)/shard_map/combine_output/pallas_call | solution.py:663
  407.7 9.7 %final_tokens.1.refs_1_ = f32[1024,768]{1,0:T(8,128)} custom-call(bf16[3,1024,768]{2,1,0:T(8,128)(2,1)} %get-tuple-element.130.dqkv_ref.grad_ref, bf16[768,2304]{1,0:T(8,128)(2,1)} %convolution_convert_fusion.1.w_ref, bf16[1024,768]{1,0:T(8,128)(2,1)} %tokens_ref.3, f32[1,768]{1,0:T(1,128)} %get-tuple-element.194.gain_ref, ...), custom_call_target="tpu_custom_call" | custom-call | flops 1000 | bytes 1000 | tf_op jit(solution)/shard_map/final_tokens/pallas_call | solution.py:696
  427.8 4.8 %collective-permute-start.29 = (bf16[24,3328]{1,0:T(8,128)(2,1)S(1)}, bf16[24,3328]{1,0:T(8,128)(2,1)S(1)}, u32[]{:S(2)}, u32[]{:S(2)}) collective-permute-start(bf16[24,3328]{1,0:T(8,128)(2,1)S(1)} %get-tuple-element.192), channel_id=1, source_target_pairs={{0,24},{8,16},{16,8},{24,0},{1,25},{9,17},{17,9},{25,1},{2,26},{10... | collective-permute-start | bytes 479240 | tf_op jit(solution)/shard_map/ppermute | solution.py:804
  432.6 7.1 %collective-permute-done.29 = bf16[24,3328]{1,0:T(8,128)(2,1)S(1)} collective-permute-done((bf16[24,3328]{1,0:T(8,128)(2,1)S(1)}, bf16[24,3328]{1,0:T(8,128)(2,1)S(1)}, u32[]{:S(2)}, u32[]{:S(2)}) %collective-permute-start.29) | collective-permute-done | bytes 159776 | tf_op jit(solution)/shard_map/ppermute | solution.py:804
  439.6 5.1 %collective-permute-done.28 = bf16[24,3328]{1,0:T(8,128)(2,1)S(1)} collective-permute-done((bf16[24,3328]{1,0:T(8,128)(2,1)S(1)}, bf16[24,3328]{1,0:T(8,128)(2,1)S(1)}, u32[]{:S(2)}, u32[]{:S(2)}) %collective-permute-start.28) | collective-permute-done | bytes 159776 | tf_op jit(solution)/shard_map/ppermute | solution.py:804
  (198 shorter events, 109.9 us)
Async XLA Ops:
  7.2 123.7 %all-gather.3.cloned.1.call-start = ((), (), s32[]{:S(2)}) async-start(), calls=%async_computation.2 | async-start | bytes 2949120 | tf_op jit(solution)/shard_map/all_gather | solution.py:834
  9.0 13.0 %collective-permute-start.1 = (bf16[24,3200]{1,0:T(8,128)(2,1)S(1)}, bf16[24,3200]{1,0:T(8,128)(2,1)S(1)}, u32[]{:S(2)}, u32[]{:S(2)}) collective-permute-start(bf16[24,3200]{1,0:T(8,128)(2,1)S(1)} %get-tuple-element.197), channel_id=1, source_target_pairs={{0,16},{8,24},{16,0},{24,8},{1,17},{9,25},{17,1},{25,9},{2,18},{10... | collective-permute-start | bytes 460808 | tf_op jit(solution)/shard_map/ppermute | solution.py:769
  13.1 8.9 %collective-permute-start = (bf16[24,3200]{1,0:T(8,128)(2,1)S(1)}, bf16[24,3200]{1,0:T(8,128)(2,1)S(1)}, u32[]{:S(2)}, u32[]{:S(2)}) collective-permute-start(bf16[24,3200]{1,0:T(8,128)(2,1)S(1)} %get-tuple-element.197), channel_id=1, source_target_pairs={{0,8},{8,0},{16,24},{24,16},{1,9},{9,1},{17,25},{25,17},{2,10},{10... | collective-permute-start | bytes 460808 | tf_op jit(solution)/shard_map/ppermute | solution.py:769
  14.7 10.2 %collective-permute-start.2 = (bf16[24,3200]{1,0:T(8,128)(2,1)S(1)}, bf16[24,3200]{1,0:T(8,128)(2,1)S(1)}, u32[]{:S(2)}, u32[]{:S(2)}) collective-permute-start(bf16[24,3200]{1,0:T(8,128)(2,1)S(1)} %get-tuple-element.197), channel_id=1, source_target_pairs={{0,24},{8,16},{16,8},{24,0},{1,25},{9,17},{17,9},{25,1},{2,26},{10... | collective-permute-start | bytes 460808 | tf_op jit(solution)/shard_map/ppermute | solution.py:769
  14.7 116.2 %all-gather.5.cloned.1.call-start = ((), (), s32[]{:S(2)}) async-start(), calls=%async_computation.3 | async-start | bytes 2949120 | tf_op jit(solution)/shard_map/all_gather | solution.py:835
  25.9 31.3 %collective-permute-start.5 = (bf16[96,3200]{1,0:T(8,128)(2,1)S(1)}, bf16[96,3200]{1,0:T(8,128)(2,1)}, u32[]{:S(2)}, u32[]{:S(2)}) collective-permute-start(bf16[96,3200]{1,0:T(8,128)(2,1)S(1)} %pad_maximum_fusion.2.rest_0_.refs_1_), channel_id=1, source_target_pairs={{0,6},{1,7},{2,4},{3,5},{4,2},{5,3},{6,0},{7,1},{8,14},{9,15},{10,... | collective-permute-start | bytes 1843208 | tf_op jit(solution)/shard_map/ppermute | solution.py:777
  28.4 27.7 %collective-permute-start.4 = (bf16[96,3200]{1,0:T(8,128)(2,1)S(1)}, bf16[96,3200]{1,0:T(8,128)(2,1)}, u32[]{:S(2)}, u32[]{:S(2)}) collective-permute-start(bf16[96,3200]{1,0:T(8,128)(2,1)S(1)} %pad_maximum_fusion.2.rest_0_.refs_1_), channel_id=1, source_target_pairs={{0,4},{1,5},{2,6},{3,7},{4,0},{5,1},{6,2},{7,3},{8,12},{9,13},{10,... | collective-permute-start | bytes 1843208 | tf_op jit(solution)/shard_map/ppermute | solution.py:777
  28.9 26.0 %collective-permute-start.3 = (bf16[96,3200]{1,0:T(8,128)(2,1)S(1)}, bf16[96,3200]{1,0:T(8,128)(2,1)}, u32[]{:S(2)}, u32[]{:S(2)}) collective-permute-start(bf16[96,3200]{1,0:T(8,128)(2,1)S(1)} %pad_maximum_fusion.2.rest_0_.refs_1_), channel_id=1, source_target_pairs={{0,2},{1,3},{2,0},{3,1},{4,6},{5,7},{6,4},{7,5},{8,10},{9,11},{10,... | collective-permute-start | bytes 1843208 | tf_op jit(solution)/shard_map/ppermute | solution.py:777
  59.8 6.7 %collective-permute-start.6 = (bf16[384,3200]{1,0:T(8,128)(2,1)}, bf16[384,3200]{1,0:T(8,128)(2,1)}, u32[]{:S(2)}, u32[]{:S(2)}) collective-permute-start(bf16[384,3200]{1,0:T(8,128)(2,1)} %held.10.refs_3_.w_ref), channel_id=1, source_target_pairs={{0,1},{1,0},{2,3},{3,2},{4,5},{5,4},{6,7},{7,6},{8,9},{9,8},{10,11... | collective-permute-start | bytes 7372808 | tf_op jit(solution)/shard_map/ppermute | solution.py:779
  59.9 297.7 %reduce-scatter.3.cloned.1.call-start = ((), (), s32[]{:S(2)}) async-start(), calls=%async_computation.4 | async-start | bytes 2949120 | tf_op jit(solution)/shard_map/reduce_scatter | solution.py:920
  63.1 39.2 %collective-permute-start.7 = (bf16[656,768]{1,0:T(8,128)(2,1)}, bf16[656,768]{1,0:T(8,128)(2,1)}, u32[]{:S(2)}, u32[]{:S(2)}) collective-permute-start(bf16[656,768]{1,0:T(8,128)(2,1)} %get-tuple-element.81), channel_id=1, source_target_pairs={{0,2},{1,3},{2,0},{3,1},{4,6},{5,7},{6,4},{7,5},{8,10},{9,11},{10,... | collective-permute-start | bytes 3022856 | tf_op jit(solution)/shard_map/ppermute | solution.py:851
  64.6 45.7 %collective-permute-start.8 = (bf16[656,768]{1,0:T(8,128)(2,1)}, bf16[656,768]{1,0:T(8,128)(2,1)}, u32[]{:S(2)}, u32[]{:S(2)}) collective-permute-start(bf16[656,768]{1,0:T(8,128)(2,1)} %get-tuple-element.82), channel_id=1, source_target_pairs={{0,4},{1,5},{2,6},{3,7},{4,0},{5,1},{6,2},{7,3},{8,12},{9,13},{10,... | collective-permute-start | bytes 3022856 | tf_op jit(solution)/shard_map/ppermute | solution.py:851
  65.1 55.0 %collective-permute-start.9 = (bf16[656,768]{1,0:T(8,128)(2,1)}, bf16[656,768]{1,0:T(8,128)(2,1)S(1)}, u32[]{:S(2)}, u32[]{:S(2)}) collective-permute-start(bf16[656,768]{1,0:T(8,128)(2,1)} %get-tuple-element.85), channel_id=1, source_target_pairs={{0,6},{1,7},{2,4},{3,5},{4,2},{5,3},{6,0},{7,1},{8,14},{9,15},{10,... | collective-permute-start | bytes 3022856 | tf_op jit(solution)/shard_map/ppermute | solution.py:851
  130.9 7.0 %collective-permute-start.10 = (bf16[768,1536]{1,0:T(8,128)(2,1)}, bf16[768,1536]{1,0:T(8,128)(2,1)S(1)}, u32[]{:S(2)}, u32[]{:S(2)}) collective-permute-start(bf16[768,1536]{1,0:T(8,128)(2,1)} %held.12.in_own), channel_id=1, source_target_pairs={{0,1},{1,0},{2,3},{3,2},{4,5},{5,4},{6,7},{7,6},{8,9},{9,8},{10,11... | collective-permute-start | bytes 7077896 | tf_op jit(solution)/shard_map/ppermute | solution.py:900
  130.9 8.2 %collective-permute-start.11 = (bf16[768,1536]{1,0:T(8,128)(2,1)}, bf16[768,1536]{1,0:T(8,128)(2,1)}, u32[]{:S(2)}, u32[]{:S(2)}) collective-permute-start(bf16[768,1536]{1,0:T(8,128)(2,1)} %held.13.out_own), channel_id=1, source_target_pairs={{0,1},{1,0},{2,3},{3,2},{4,5},{5,4},{6,7},{7,6},{8,9},{9,8},{10,11... | collective-permute-start | bytes 7077896 | tf_op jit(solution)/shard_map/ppermute | solution.py:901
  131.4 28.6 %collective-permute-start.12 = (bf16[656,768]{1,0:T(8,128)(2,1)}, bf16[656,768]{1,0:T(8,128)(2,1)S(1)}, u32[]{:S(2)}, u32[]{:S(2)}) collective-permute-start(bf16[656,768]{1,0:T(8,128)(2,1)} %get-tuple-element.89), channel_id=1, source_target_pairs={{0,2},{1,3},{2,0},{3,1},{4,6},{5,7},{6,4},{7,5},{8,10},{9,11},{10,... | collective-permute-start | bytes 3022856 | tf_op jit(solution)/shard_map/ppermute | solution.py:851
  131.9 50.6 %collective-permute-start.13 = (bf16[656,768]{1,0:T(8,128)(2,1)}, bf16[656,768]{1,0:T(8,128)(2,1)}, u32[]{:S(2)}, u32[]{:S(2)}) collective-permute-start(bf16[656,768]{1,0:T(8,128)(2,1)} %get-tuple-element.92), channel_id=1, source_target_pairs={{0,4},{1,5},{2,6},{3,7},{4,0},{5,1},{6,2},{7,3},{8,12},{9,13},{10,... | collective-permute-start | bytes 3022856 | tf_op jit(solution)/shard_map/ppermute | solution.py:851
  131.9 71.5 %collective-permute-start.14 = (bf16[656,768]{1,0:T(8,128)(2,1)}, bf16[656,768]{1,0:T(8,128)(2,1)}, u32[]{:S(2)}, u32[]{:S(2)}) collective-permute-start(bf16[656,768]{1,0:T(8,128)(2,1)} %get-tuple-element.95), channel_id=1, source_target_pairs={{0,6},{1,7},{2,4},{3,5},{4,2},{5,3},{6,0},{7,1},{8,14},{9,15},{10,... | collective-permute-start | bytes 3022856 | tf_op jit(solution)/shard_map/ppermute | solution.py:851
  182.0 24.6 %collective-permute-start.15 = (bf16[656,768]{1,0:T(8,128)(2,1)}, bf16[656,768]{1,0:T(8,128)(2,1)S(1)}, u32[]{:S(2)}, u32[]{:S(2)}) collective-permute-start(bf16[656,768]{1,0:T(8,128)(2,1)} %get-tuple-element.93.rest_0_), channel_id=1, source_target_pairs={{0,2},{1,3},{2,0},{3,1},{4,6},{5,7},{6,4},{7,5},{8,10},{9,11},{10,... | collective-permute-start | bytes 3022856 | tf_op jit(solution)/shard_map/ppermute | solution.py:911
  203.3 25.3 %collective-permute-start.16 = (bf16[656,768]{1,0:T(8,128)(2,1)}, bf16[656,768]{1,0:T(8,128)(2,1)S(1)}, u32[]{:S(2)}, u32[]{:S(2)}) collective-permute-start(bf16[656,768]{1,0:T(8,128)(2,1)} %get-tuple-element.96.rest_1_), channel_id=1, source_target_pairs={{0,4},{1,5},{2,6},{3,7},{4,0},{5,1},{6,2},{7,3},{8,12},{9,13},{10,... | collective-permute-start | bytes 3022856 | tf_op jit(solution)/shard_map/ppermute | solution.py:911
  228.3 24.7 %collective-permute-start.17 = (bf16[656,768]{1,0:T(8,128)(2,1)}, bf16[656,768]{1,0:T(8,128)(2,1)S(1)}, u32[]{:S(2)}, u32[]{:S(2)}) collective-permute-start(bf16[656,768]{1,0:T(8,128)(2,1)} %get-tuple-element.122), channel_id=1, source_target_pairs={{0,6},{1,7},{2,4},{3,5},{4,2},{5,3},{6,0},{7,1},{8,14},{9,15},{10,... | collective-permute-start | bytes 3022856 | tf_op jit(solution)/shard_map/ppermute | solution.py:911
  271.6 104.1 %reduce-scatter.5.cloned.1.call-start = ((), (), s32[]{:S(2)}) async-start(), calls=%async_computation.5 | async-start | bytes 2949120 | tf_op jit(solution)/shard_map/reduce_scatter | solution.py:920
  295.3 56.8 %collective-permute-start.20 = (bf16[640,768]{1,0:T(8,128)(2,1)}, bf16[640,768]{1,0:T(8,128)(2,1)S(1)}, u32[]{:S(2)}, u32[]{:S(2)}) collective-permute-start(bf16[640,768]{1,0:T(8,128)(2,1)} %get-tuple-element.123), channel_id=1, source_target_pairs={{0,2},{1,3},{2,0},{3,1},{4,6},{5,7},{6,4},{7,5},{8,10},{9,11},{10,... | collective-permute-start | bytes 2949128 | tf_op jit(solution)/shard_map/ppermute | solution.py:851
  295.8 56.3 %collective-permute-start.21 = (bf16[640,768]{1,0:T(8,128)(2,1)}, bf16[640,768]{1,0:T(8,128)(2,1)}, u32[]{:S(2)}, u32[]{:S(2)}) collective-permute-start(bf16[640,768]{1,0:T(8,128)(2,1)} %get-tuple-element.124), channel_id=1, source_target_pairs={{0,4},{1,5},{2,6},{3,7},{4,0},{5,1},{6,2},{7,3},{8,12},{9,13},{10,... | collective-permute-start | bytes 2949128 | tf_op jit(solution)/shard_map/ppermute | solution.py:851
  296.9 55.1 %collective-permute-start.22 = (bf16[640,768]{1,0:T(8,128)(2,1)}, bf16[640,768]{1,0:T(8,128)(2,1)}, u32[]{:S(2)}, u32[]{:S(2)}) collective-permute-start(bf16[640,768]{1,0:T(8,128)(2,1)} %get-tuple-element.125), channel_id=1, source_target_pairs={{0,6},{1,7},{2,4},{3,5},{4,2},{5,3},{6,0},{7,1},{8,14},{9,15},{10,... | collective-permute-start | bytes 2949128 | tf_op jit(solution)/shard_map/ppermute | solution.py:851
  377.9 5.0 %collective-permute-start.23 = (bf16[384,3328]{1,0:T(8,128)(2,1)}, bf16[384,3328]{1,0:T(8,128)(2,1)S(1)}, u32[]{:S(2)}, u32[]{:S(2)}) collective-permute-start(bf16[384,3328]{1,0:T(8,128)(2,1)} %get-tuple-element.143), channel_id=1, source_target_pairs={{0,1},{1,0},{2,3},{3,2},{4,5},{5,4},{6,7},{7,6},{8,9},{9,8},{10,11... | collective-permute-start | bytes 7667720 | tf_op jit(solution)/shard_map/ppermute | solution.py:785
  388.1 29.3 %collective-permute-start.24 = (bf16[96,3328]{1,0:T(8,128)(2,1)}, bf16[96,3328]{1,0:T(8,128)(2,1)S(1)}, u32[]{:S(2)}, u32[]{:S(2)}) collective-permute-start(bf16[96,3328]{1,0:T(8,128)(2,1)} %get-tuple-element.188), channel_id=1, source_target_pairs={{0,2},{1,3},{2,0},{3,1},{4,6},{5,7},{6,4},{7,5},{8,10},{9,11},{10,... | collective-permute-start | bytes 1916936 | tf_op jit(solution)/shard_map/ppermute | solution.py:794
  389.6 30.0 %collective-permute-start.26 = (bf16[96,3328]{1,0:T(8,128)(2,1)}, bf16[96,3328]{1,0:T(8,128)(2,1)}, u32[]{:S(2)}, u32[]{:S(2)}) collective-permute-start(bf16[96,3328]{1,0:T(8,128)(2,1)} %get-tuple-element.189), channel_id=1, source_target_pairs={{0,6},{1,7},{2,4},{3,5},{4,2},{5,3},{6,0},{7,1},{8,14},{9,15},{10,... | collective-permute-start | bytes 1916936 | tf_op jit(solution)/shard_map/ppermute | solution.py:794
  391.0 29.9 %collective-permute-start.25 = (bf16[96,3328]{1,0:T(8,128)(2,1)}, bf16[96,3328]{1,0:T(8,128)(2,1)}, u32[]{:S(2)}, u32[]{:S(2)}) collective-permute-start(bf16[96,3328]{1,0:T(8,128)(2,1)} %get-tuple-element.190), channel_id=1, source_target_pairs={{0,4},{1,5},{2,6},{3,7},{4,0},{5,1},{6,2},{7,3},{8,12},{9,13},{10,... | collective-permute-start | bytes 1916936 | tf_op jit(solution)/shard_map/ppermute | solution.py:794
  424.7 7.9 %collective-permute-start.27 = (bf16[24,3328]{1,0:T(8,128)(2,1)S(1)}, bf16[24,3328]{1,0:T(8,128)(2,1)S(1)}, u32[]{:S(2)}, u32[]{:S(2)}) collective-permute-start(bf16[24,3328]{1,0:T(8,128)(2,1)S(1)} %get-tuple-element.191), channel_id=1, source_target_pairs={{0,8},{8,0},{16,24},{24,16},{1,9},{9,1},{17,25},{25,17},{2,10},{10... | collective-permute-start | bytes 479240 | tf_op jit(solution)/shard_map/ppermute | solution.py:804
  427.8 11.8 %collective-permute-start.29 = (bf16[24,3328]{1,0:T(8,128)(2,1)S(1)}, bf16[24,3328]{1,0:T(8,128)(2,1)S(1)}, u32[]{:S(2)}, u32[]{:S(2)}) collective-permute-start(bf16[24,3328]{1,0:T(8,128)(2,1)S(1)} %get-tuple-element.192), channel_id=1, source_target_pairs={{0,24},{8,16},{16,8},{24,0},{1,25},{9,17},{17,9},{25,1},{2,26},{10... | collective-permute-start | bytes 479240 | tf_op jit(solution)/shard_map/ppermute | solution.py:804
  432.6 12.1 %collective-permute-start.28 = (bf16[24,3328]{1,0:T(8,128)(2,1)S(1)}, bf16[24,3328]{1,0:T(8,128)(2,1)S(1)}, u32[]{:S(2)}, u32[]{:S(2)}) collective-permute-start(bf16[24,3328]{1,0:T(8,128)(2,1)S(1)} %get-tuple-element.193), channel_id=1, source_target_pairs={{0,16},{8,24},{16,0},{24,8},{1,17},{9,25},{17,1},{25,9},{2,18},{10... | collective-permute-start | bytes 479240 | tf_op jit(solution)/shard_map/ppermute | solution.py:804
  (29 other events, 223.1 us)
Sparse Core Ops, SparseCore 0:
  14.9 51.9 all-gather.2
  68.5 50.4 all-gather.4
  271.7 54.2 reduce-scatter.2
  328.1 47.5 reduce-scatter.4

commit v3 on v2

--- a/solution.py
+++ b/solution.py
@@ -709,49 +709,39 @@
     )(d_qkv, w_all, tokens, gain, d_residual, *ahead)
 
 
-def qkv_grad_kernel(parts, turned_ref, grad_ref, mixed_ref, branch_ref, extra_ref, *rest):
-    step = pl.program_id(0)
+def qkv_grad_kernel(turned_ref, grad_ref, mixed_ref, branch_ref, extra_ref, *rest):
     keep_ref, send_ref = rest[-2:]
-    half = keep_ref.shape[0]
-
-    def store(made):
-        keep_ref[...] = made[:half]
-        send_ref[...] = made[half:]
-
-    @pl.when(step < 3 * parts)
-    def _():
-        store(dot_nn(turned_ref[...], grad_ref[0]).astype(BF16))
-
-    @pl.when((step >= 3 * parts) & (step < 4 * parts))
-    def _():
-        store(dot_nn(mixed_ref[...], branch_ref[...]).astype(BF16))
-
-    @pl.when(step == 4 * parts)
-    def _():
-        store(extra_ref[...])
+    half, width = keep_ref.shape[0], branch_ref.shape[1]
+
+    def store(made, column):
+        keep_ref[:, column : column + made.shape[1]] = made[:half]
+        send_ref[:, column : column + made.shape[1]] = made[half:]
+
+    for index in range(4):
+
+        @pl.when(pl.program_id(0) == index)
+        def _():
+            if index < 3:
+                made = dot_nn(turned_ref[...], grad_ref[0])
+            else:
+                made = dot_nn(mixed_ref[...], branch_ref[...])
+                store(extra_ref[...], 4 * width)
+            store(made.astype(BF16), index * width)
 
 
 def qkv_grad(turned, d_qkv, mixed_turned, branch, extra, ahead=()):
     width, rows = turned.shape
-    parts = width // BLK
-
-    def place(j):
-        j = jnp.minimum(j, 3 * parts - 1)
-        return (j // parts, 0, j % parts)
-
-    def place_branch(j):
-        return (0, jnp.clip(j - 3 * parts, 0, parts - 1))
-
-    return pl.pallas_call(
-        functools.partial(qkv_grad_kernel, parts),
-        grid=(4 * parts + 1,),
+    return pl.pallas_call(
+        qkv_grad_kernel,
+        grid=(4,),
         in_specs=[
-            whole((width, rows)), pl.BlockSpec((1, rows, BLK), place),
-            whole((width, rows)), pl.BlockSpec((rows, BLK), place_branch), whole((width, BLK)),
+            whole((width, rows)),
+            pl.BlockSpec((1, rows, width), lambda j: (jnp.minimum(j, 2), 0, 0)),
+            whole((width, rows)), whole((rows, width)), whole((width, 128)),
         ]
         + [ANY] * len(ahead),
-        out_specs=[pl.BlockSpec((width // 2, BLK), lambda j: (0, j))] * 2,
-        out_shape=[jax.ShapeDtypeStruct((width // 2, 4 * width + BLK), BF16)] * 2,
+        out_specs=[whole((width // 2, 4 * width + 128))] * 2,
+        out_shape=[jax.ShapeDtypeStruct((width // 2, 4 * width + 128), BF16)] * 2,
         compiler_params=pltpu.CompilerParams(vmem_limit_bytes=60 * MIB),
         cost_estimate=LIGHT,
         name="qkv_grad",
@@ -891,9 +881,8 @@
     mixed, lse = attention_forward(qkv_rows, segments, near, far, HEADS)
     residual, normed_ffn, gates, gate_row, moved_mixed = post_attention(
         mixed, plane, plane_rest, tokens_in, gain_f, router_cols, dest_row, move,
-        tuple(grads_in[1:3]),
-    )
-    sent_rows = dispatch(experts, dest_row, normed_ffn, gate_row, slots, tuple(grads_in[3:]))
+    )
+    sent_rows = dispatch(experts, dest_row, normed_ffn, gate_row, slots, tuple(grads_in[1:]))
     rows_in = exchange(sent_rows)
     (own_in,) = held([own_in], (mixed,))
     (own_out,) = held([own_out], (sent_rows[0],))
@@ -912,24 +901,31 @@
         )
     hid_own, hid_other, dpre_own, dpre_other, _, made, rows_turned, gexp_turned = zip(*chunks)
 
-    def pair_sum(own, other):
-        got = lax.ppermute(other, "fsdp", pairs_of(fsdp_size, 1))
-        return (own.astype(F32) + got.astype(F32)).astype(BF16)
-
     def owners(pair):
-        return lax.psum_scatter(pair, "dp", scatter_dimension=0, tiled=True).astype(F32)
-
+        return lax.psum_scatter(pair, "dp", scatter_dimension=0, tiled=True)
+
+    swapped = pairs_of(fsdp_size, 1)
+    normed_turned, mixed_turned = normed_attn.T, moved_mixed.T
     grad_in_own = weight_grad(rows_turned, dpre_own, tuple(backs[-2:-1]))
     grad_out_own = weight_grad(gexp_turned, hid_own, (grad_in_own,))
-    grad_in_other = weight_grad(rows_turned, dpre_other, (grad_out_own,) + tuple(backs[-1:]))
-    pair_in = pair_sum(grad_in_own, grad_in_other)
-    grad_out_other = weight_grad(gexp_turned, hid_other, (pair_in,))
-    pair_out = pair_sum(grad_out_own, grad_out_other)
+    grad_in_other = weight_grad(
+        rows_turned, dpre_other, (grad_out_own,) + tuple(backs[-1:])
+    )
+    grad_out_other = weight_grad(gexp_turned, hid_other, (grad_in_other,))
+    got_in = lax.ppermute(grad_in_other, "fsdp", swapped)
+    (grad_out_other,) = held([grad_out_other], (got_in,))
+    got_out = lax.ppermute(grad_out_other, "fsdp", swapped)
+    pair_in = (grad_in_own.astype(F32) + got_in.astype(F32)).astype(BF16)
+    (got_out,) = held(
+        [got_out], (pair_in, back_attn, normed_turned, mixed_turned, router_rows)
+    )
+    pair_out = (grad_out_own.astype(F32) + got_out.astype(F32)).astype(BF16)
     d_w_in, d_w_out = owners(pair_in), owners(pair_out)
     mades = exchange([made[0]] + list(held(made[1:], (pair_out,))))
 
     d_residual, d_branch, d_mixed, d_gain_f, d_logits = combine_back(
-        backs, dest_row, gates, residual, d_out, gain_f, router_rows, back_attn, (grad_out_other, pair_in, pair_out)
+        backs, dest_row, gates, residual, d_out, gain_f, router_rows, back_attn,
+        (pair_out,),
     )
     d_qkv, near_grad, far_grad = attention_backward(
         qkv_rows, d_mixed, mixed, lse, segments, near, far, HEADS
@@ -945,9 +941,9 @@
     late_cols = jnp.where(place[None, :] == experts, d_gain_f.reshape(width, 1), d_router)
     late_cols = jnp.where(place[None, :] == experts + 1, d_table.reshape(width, 1), late_cols)
     late_cols = jnp.dot(move.T, late_cols.astype(BF16), preferred_element_type=F32)
-    late_cols = jnp.pad(late_cols.astype(BF16), ((0, 0), (0, BLK - 128)))
+    late_cols = late_cols.astype(BF16)
     keep, send = qkv_grad(
-        normed_attn.T, d_qkv, moved_mixed.T, d_branch, late_cols, (d_w_in,)
+        normed_turned, d_qkv, mixed_turned, d_branch, late_cols, (d_w_in,)
     )
     keep, send = held([keep, send], (d_w_out,))
     late = scatter_plane(scatter_pair(keep, send))
@@ -966,8 +962,8 @@
         late[:, 4 * width + experts],
         late[:, 4 * width + experts + 1],
         late[:, 4 * width : 4 * width + experts],
-        d_w_in,
-        d_w_out,
+        d_w_in.astype(F32),
+        d_w_out.astype(F32),
     )
 
 

time: 465 us -> 450 us (0.968)
  waiting for transfers between devices: 58.8 us -> 49 us
    reduce_scatter x2, waiting for transfers between devices: 2.5 us -> 11.9 us  [owners(): return lax.psum_scatter(pair, 'dp', scatter_dimension=0, tiled=True)]
    ppermute x9, waiting for transfers between devices: 7.99 us -> 0.02 us  [exchange(): lax.ppermute(pieces[m], 'fsdp', pairs_of(fsdp_size, 2 * m))]
    unnamed x63 -> x69, local copies, waits for them, and re-layouts: 17.6 us -> 19.1 us
  transfers between devices with their start and end apart: 34 -> 34, of which waited for: 16 -> 15; matrix products, arithmetic and copies ran while one was open for 14% -> 15% of each run, Pallas kernels for 54% -> 55%
where the time goes in v3:
time: 450 us; the launch traced here: 441 us
  Pallas kernels  253 us (56%)
  waiting for transfers between devices  49 us (11%)
  local copies, waits for them, and re-layouts  36.2 us (8%)
  starting transfers between devices  31.3 us (7%)
  other arithmetic  29.4 us (7%)
  matrix products  28.4 us (6%)
  between operations  14.6 us (3%)
    pallas_call x4, Pallas kernels, expert_chunk(): pl.pallas_call(expert_kernel, grid=(steps,), in_specs=[whole((slots + TAI...  83.5 us
    pallas_call x4, Pallas kernels, weight_grad(): pl.pallas_call(functools.partial(weight_grad_kernel, count), grid=(half /...  43.1 us
    pallas_call x1, Pallas kernels, attention_backward(): pl.pallas_call(attn_bwd_kernel, grid_spec=pltpu.PrefetchScalarGridSpec(nu...  30.5 us
    pallas_call x1, Pallas kernels, attention_forward(): pl.pallas_call(attn_fwd_kernel, grid_spec=pltpu.PrefetchScalarGridSpec(nu...  20.7 us
    pallas_call x2, Pallas kernels, dispatch(): pl.pallas_call(functools.partial(dispatch_kernel, experts), grid=(experts...  19.8 us
    unnamed x69, local copies, waits for them, and re-layouts  19.1 us
    pallas_call x1, Pallas kernels, combine_back(): pl.pallas_call(functools.partial(combine_kernel, count), grid=(rows // RO...  14.9 us
    reduce_scatter x2, waiting for transfers between devices, owners(): return lax.psum_scatter(pair, 'dp', scatter_dimension=0, tiled=True)  11.9 us
  transfers between devices with their start and end apart: 34, of which 15 were waited for; matrix products, arithmetic and copies ran while one was open for 15% of the time, Pallas kernels for 55%

profile of v3, /device:TPU:0, one launch (start us, length us, event | category | flops | bytes accessed | tf_op | source)
XLA Modules:
  0.0 441.5 jit_solution(10429882558712280509)
XLA Ops:
  9.0 4.1 collective-permute-start.1
  32.4 3.1 fusion.6
  36.1 9.9 %dispatch_rows.2 = (bf16[656,768]{1,0:T(8,128)(2,1)}, bf16[656,768]{1,0:T(8,128)(2,1)}, bf16[656,768]{1,0:T(8,128)(2,1)}, bf16[656,768]{1,0:T(8,128)(2,1)}) custom-call(s32[8,1024]{1,0:T(8,128)} %pad.8.dest_ref.refs_4_.refs_8_, bf16[1024,768]{1,0:T(8,128)(2,1)} %refs_11_.1, f32[8,1024]{1,0:T(8,128)} %broadcast_in_dim.87.gate_ref, bf16[96,3200]{1,0:T(8,128)(2,1)} %copy-done.13), custom_call_target="tpu_custom_call" | custom-call | flops 1000 | bytes 1000 | tf_op jit(solution)/shard_map/dispatch_rows/pallas_call | solution.py:341
  46.0 3.7 copy.85.refs_2_
  49.7 5.3 %collective-permute-done.3 = bf16[96,3200]{1,0:T(8,128)(2,1)} collective-permute-done((bf16[96,3200]{1,0:T(8,128)(2,1)S(1)}, bf16[96,3200]{1,0:T(8,128)(2,1)}, u32[]{:S(2)}, u32[]{:S(2)}) %collective-permute-start.3) | collective-permute-done | bytes 614432 | tf_op jit(solution)/shard_map/ppermute | solution.py:767
  72.5 7.7 %convolution_convert_fusion.q_ref.k_ref.v_ref = bf16[1024,2304]{1,0:T(8,128)(2,1)} fusion(f32[1024,768]{0,1:T(8,128)S(1)} %copy-done.6, f32[768]{0:T(1024)S(1)} %convert_reduce_fusion, bf16[384,3200]{1,0:T(8,128)(2,1)S(1)} %copy-done.1, bf16[384,3200]{1,0:T(8,128)(2,1)} %collective-permute-done.6.w_rest), kind=kOutput, calls=%fused_computation | convolution fusion | flops 3634888704 | bytes 12782592 | tf_op jit(solution)/shard_map/dot_general | solution.py:879
  80.2 20.7 %attention_forward.1 = (bf16[1024,768]{1,0:T(8,128)(2,1)}, f32[6,2,1024]{2,1,0:T(2,128)}) custom-call(f32[12]{0:T(128)} %bitcast_convert_fusion.far_ref, bf16[1024,2304]{1,0:T(8,128)(2,1)} %convolution_convert_fusion.q_ref.k_ref.v_ref, bf16[1024,2304]{1,0:T(8,128)(2,1)} %convolution_convert_fusion.q_ref.k_ref.v_ref, ...), custom_call_target="tpu_custom_call" | custom-call | flops 1000 | bytes 1000 | tf_op jit(solution)/shard_map/attention_forward/pallas_call | solution.py:190
  102.1 9.8 %post_attention.1 = (f32[1024,768]{1,0:T(8,128)}, bf16[1024,768]{1,0:T(8,128)(2,1)}, f32[1024,128]{1,0:T(8,128)}, f32[8,1024]{1,0:T(8,128)}, bf16[1024,768]{1,0:T(8,128)(2,1)}) custom-call(bf16[1024,768]{1,0:T(8,128)(2,1)} %get-tuple-element.78.mixed_ref.refs_1_.o_ref, bf16[384,3200]{1,0:T(8,128)(2,1)} %held.12.w_ref.refs_3_, ...), custom_call_target="tpu_custom_call" | custom-call | flops 1000 | bytes 1000 | tf_op jit(solution)/shard_map/post_attention/pallas_call | solution.py:406
  112.8 9.9 %dispatch_rows.3 = (bf16[656,768]{1,0:T(8,128)(2,1)}, bf16[656,768]{1,0:T(8,128)(2,1)}, bf16[656,768]{1,0:T(8,128)(2,1)}, bf16[656,768]{1,0:T(8,128)(2,1)}) custom-call(s32[8,1024]{1,0:T(8,128)} %pad.8.dest_ref.refs_4_.refs_8_, bf16[1024,768]{1,0:T(8,128)(2,1)} %get-tuple-element.79.values_ref, f32[8,1024]{1,0:T(8,128)} %get-tuple-element.80.gate_ref, ...), custom_call_target="tpu_custom_call" | custom-call | flops 1000 | bytes 1000 | tf_op jit(solution)/shard_map/dispatch_rows/pallas_call | solution.py:341
  126.7 3.0 collective-permute-done.10.in_other
  131.2 20.7 %expert_chunk.4 = (bf16[640,1536]{1,0:T(8,128)(2,1)}, bf16[640,1536]{1,0:T(8,128)(2,1)}, bf16[640,1536]{1,0:T(8,128)(2,1)}, bf16[640,1536]{1,0:T(8,128)(2,1)}, b...) custom-call(bf16[656,768]{1,0:T(8,128)(2,1)} %get-tuple-element.86.refs, ...), custom_call_target="tpu_custom_call" | custom-call | flops 1000 | bytes 1000 | tf_op jit(solution)/shard_map/expert_chunk/pallas_call | solution.py:497
  152.8 21.2 %expert_chunk.5 = (bf16[640,1536]{1,0:T(8,128)(2,1)}, bf16[640,1536]{1,0:T(8,128)(2,1)}, bf16[640,1536]{1,0:T(8,128)(2,1)}, bf16[640,1536]{1,0:T(8,128)(2,1)}, b...) custom-call(bf16[656,768]{1,0:T(8,128)(2,1)} %copy-done.18, ...), custom_call_target="tpu_custom_call" | custom-call | flops 1000 | bytes 1000 | tf_op jit(solution)/shard_map/expert_chunk/pallas_call | solution.py:497
  175.6 20.8 %expert_chunk.6 = (bf16[640,1536]{1,0:T(8,128)(2,1)}, bf16[640,1536]{1,0:T(8,128)(2,1)}, bf16[640,1536]{1,0:T(8,128)(2,1)}, bf16[640,1536]{1,0:T(8,128)(2,1)}, b...) custom-call(bf16[656,768]{1,0:T(8,128)(2,1)} %collective-permute-done.1, ...), custom_call_target="tpu_custom_call" | custom-call | flops 1000 | bytes 1000 | tf_op jit(solution)/shard_map/expert_chunk/pallas_call | solution.py:497
  199.6 20.8 %expert_chunk.7 = (bf16[640,1536]{1,0:T(8,128)(2,1)}, bf16[640,1536]{1,0:T(8,128)(2,1)}, bf16[640,1536]{1,0:T(8,128)(2,1)}, bf16[640,1536]{1,0:T(8,128)(2,1)}, b...) custom-call(bf16[656,768]{1,0:T(8,128)(2,1)} %collective-permute-done.1, ...), custom_call_target="tpu_custom_call" | custom-call | flops 1000 | bytes 1000 | tf_op jit(solution)/shard_map/expert_chunk/pallas_call | solution.py:497
  222.9 10.7 %weight_grad.4.refs_8_ = bf16[768,1536]{1,0:T(8,128)(2,1)} custom-call(bf16[768,640]{1,0:T(8,128)(2,1)} %get-tuple-element.106.refs_0_, bf16[768,640]{1,0:T(8,128)(2,1)} %get-tuple-element.107.refs_1_, bf16[768,640]{1,0:T(8,128)(2,1)} %get-tuple-element.108.refs_2_, bf16[768,640]{1,0:T(8,128)(2,1)} %get-tuple-element.109.refs_3_, ...), custom_call_target="tpu_custom_call" | custom-call | flops 1000 | bytes 1000 | tf_op jit(solution)/shard_map/weight_grad/pallas_call | solution.py:542
  233.6 10.9 %weight_grad.5.refs_8_ = bf16[768,1536]{1,0:T(8,128)(2,1)} custom-call(bf16[768,640]{1,0:T(8,128)(2,1)} %get-tuple-element.98.refs_0_, bf16[768,640]{1,0:T(8,128)(2,1)} %get-tuple-element.99.refs_1_, bf16[768,640]{1,0:T(8,128)(2,1)} %get-tuple-element.100.refs_2_, bf16[768,640]{1,0:T(8,128)(2,1)} %get-tuple-element.101.refs_3_, ...), custom_call_target="tpu_custom_call" | custom-call | flops 1000 | bytes 1000 | tf_op jit(solution)/shard_map/weight_grad/pallas_call | solution.py:542
  246.1 10.8 %weight_grad.6.refs_8_ = bf16[768,1536]{1,0:T(8,128)(2,1)} custom-call(bf16[768,640]{1,0:T(8,128)(2,1)} %get-tuple-element.106.refs_0_, bf16[768,640]{1,0:T(8,128)(2,1)} %get-tuple-element.107.refs_1_, bf16[768,640]{1,0:T(8,128)(2,1)} %get-tuple-element.108.refs_2_, bf16[768,640]{1,0:T(8,128)(2,1)} %get-tuple-element.109.refs_3_, ...), custom_call_target="tpu_custom_call" | custom-call | flops 1000 | bytes 1000 | tf_op jit(solution)/shard_map/weight_grad/pallas_call | solution.py:542
  256.9 4.7 %collective-permute-done.18.refs_1_ = bf16[768,1536]{1,0:T(8,128)(2,1)S(1)} collective-permute-done((bf16[768,1536]{1,0:T(8,128)(2,1)}, bf16[768,1536]{1,0:T(8,128)(2,1)S(1)}, u32[]{:S(2)}, u32[]{:S(2)}) %collective-permute-start.18) | collective-permute-done | bytes 2359328 | tf_op jit(solution)/shard_map/ppermute | solution.py:915
  265.1 10.7 %weight_grad.7.refs_0_ = bf16[768,1536]{1,0:T(8,128)(2,1)} custom-call(bf16[768,640]{1,0:T(8,128)(2,1)} %get-tuple-element.98.refs_0_, bf16[768,640]{1,0:T(8,128)(2,1)} %get-tuple-element.99.refs_1_, bf16[768,640]{1,0:T(8,128)(2,1)} %get-tuple-element.100.refs_2_, bf16[768,640]{1,0:T(8,128)(2,1)} %get-tuple-element.101.refs_3_, ...), custom_call_target="tpu_custom_call" | custom-call | flops 1000 | bytes 1000 | tf_op jit(solution)/shard_map/weight_grad/pallas_call | solution.py:542
  280.1 3.4 fusion.7.refs_2_.refs_14_
  284.9 4.5 %add_convert_fusion.1.refs_3_.refs_15_ = bf16[768,1536]{1,0:T(8,128)(2,1)} fusion(bf16[768,1536]{1,0:T(8,128)(2,1)} %held.17, bf16[768,1536]{1,0:T(8,128)(2,1)} %weight_grad.5.refs_8_), kind=kLoop, calls=%fused_computation.5 | loop fusion | flops 4718592 | bytes 7077888 | tf_op jit(solution)/shard_map/convert_element_type | solution.py:922
  292.9 14.9 %combine_back.1 = (f32[1024,768]{1,0:T(8,128)}, bf16[1024,768]{1,0:T(8,128)(2,1)}, bf16[1024,768]{1,0:T(8,128)(2,1)}, f32[1,768]{1,0:T(1,128)}, f32[1024,128]{1,0:T(8,128)}) custom-call(bf16[656,768]{1,0:T(8,128)(2,1)} %get-tuple-element.90.rest_0_.refs_0_.refs_4_, bf16[656,768]{1,0:T(8,128)(2,1)} %copy-done.10, bf16[656,768]{1,0:T(8,128)(2,1)} %copy-done.12, ...), custom_call_target="tpu_custom_call" | custom-call | flops 1000 | bytes 1000 | tf_op jit(solution)/shard_map/combine_back/pallas_call | solution.py:615
  307.8 30.5 %attention_backward.1 = (bf16[3,1024,768]{2,1,0:T(8,128)(2,1)}, f32[6,2,256]{2,1,0:T(2,128)}, f32[6,2,128]{2,1,0:T(2,128)}) custom-call(f32[12]{0:T(128)} %bitcast_convert_fusion.far_ref, bf16[1024,2304]{1,0:T(8,128)(2,1)} %convolution_convert_fusion.q_ref.k_ref.v_ref, bf16[1024,2304]{1,0:T(8,128)(2,1)} %convolution_convert_fusion.q_ref.k_ref.v_ref, ...), custom_call_target="tpu_custom_call" | custom-call | flops 1000 | bytes 1000 | tf_op jit(solution)/shard_map/attention_backward/pallas_call | solution.py:230
  347.1 10.7 %qkv_grad.1 = (bf16[384,3200]{1,0:T(8,128)(2,1)}, bf16[384,3200]{1,0:T(8,128)(2,1)}) custom-call(bf16[768,1024]{1,0:T(8,128)(2,1)} %fusion.64.refs_3_.turned_ref, bf16[3,1024,768]{2,1,0:T(8,128)(2,1)} %get-tuple-element.131.dqkv_ref.grad_ref, bf16[768,1024]{1,0:T(8,128)(2,1)} %bitcast.37, bf16[1024,768]{1,0:T(8,128)(2,1)} %get-tuple-element.133.branch_ref, ...), custom_call_target="tpu_custom_call" | custom-call | flops 1000 | bytes 1000 | tf_op jit(solution)/shard_map/qkv_grad/pallas_call | solution.py:734
  357.8 11.9 %reduce-scatter.5.cloned.1.call-done.refs_2_ = bf16[192,1536]{1,0:T(8,128)(2,1)} async-done(((bf16[768,1536]{1,0:T(8,128)(2,1)}), bf16[192,1536]{1,0:T(8,128)(2,1)}) %reduce-scatter.5.cloned.1.call-update) | async-done | bytes 589840 | tf_op jit(solution)/shard_map/reduce_scatter | solution.py:905
  369.7 4.9 %collective-permute-done.23 = bf16[384,3200]{1,0:T(8,128)(2,1)S(1)} collective-permute-done((bf16[384,3200]{1,0:T(8,128)(2,1)}, bf16[384,3200]{1,0:T(8,128)(2,1)S(1)}, u32[]{:S(2)}, u32[]{:S(2)}) %collective-permute-start.23) | collective-permute-done | bytes 2457632 | tf_op jit(solution)/shard_map/ppermute | solution.py:775
  382.9 6.2 %convolution_convert_fusion.1.w_ref = bf16[768,2304]{1,0:T(8,128)(2,1)} fusion(s32[768]{0:T(1024)S(1)} %fusion.48, bf16[384,3200]{1,0:T(8,128)(2,1)S(1)} %copy-done.2, bf16[384,3200]{1,0:T(8,128)(2,1)} %collective-permute-done.6.w_rest), kind=kOutput, calls=%fused_computation.1 | convolution fusion | flops 2727346176 | bytes 8457216 | tf_op jit(solution)/shard_map/dot_general | solution.py:858
  389.1 9.8 %combine_output.1.rest_0_ = bf16[1024,768]{1,0:T(8,128)(2,1)} custom-call(bf16[640,768]{1,0:T(8,128)(2,1)} %get-tuple-element.88.refs_0_, bf16[640,768]{1,0:T(8,128)(2,1)} %copy-done.15, bf16[640,768]{1,0:T(8,128)(2,1)} %collective-permute-done.21.refs_2_.refs_3_, bf16[640,768]{1,0:T(8,128)(2,1)} %collective-permute-done.22.refs_3_.refs_4_, ...), custom_call_target="tpu_custom_call" | custom-call | flops 1000 | bytes 1000 | tf_op jit(solution)/shard_map/combine_output/pallas_call | solution.py:663
  398.9 9.7 %final_tokens.1.refs_1_ = f32[1024,768]{1,0:T(8,128)} custom-call(bf16[3,1024,768]{2,1,0:T(8,128)(2,1)} %get-tuple-element.131.dqkv_ref.grad_ref, bf16[768,2304]{1,0:T(8,128)(2,1)} %convolution_convert_fusion.1.w_ref, bf16[1024,768]{1,0:T(8,128)(2,1)} %tokens_ref.3, f32[1,768]{1,0:T(1,128)} %get-tuple-element.194.gain_ref, ...), custom_call_target="tpu_custom_call" | custom-call | flops 1000 | bytes 1000 | tf_op jit(solution)/shard_map/final_tokens/pallas_call | solution.py:696
  415.4 3.0 collective-permute-start.29
  422.5 2.8 collective-permute-done.29
  425.3 5.0 %collective-permute-done.28 = bf16[24,3200]{1,0:T(8,128)(2,1)S(1)} collective-permute-done((bf16[24,3200]{1,0:T(8,128)(2,1)S(1)}, bf16[24,3200]{1,0:T(8,128)(2,1)S(1)}, u32[]{:S(2)}, u32[]{:S(2)}) %collective-permute-start.28) | collective-permute-done | bytes 153632 | tf_op jit(solution)/shard_map/ppermute | solution.py:794
  (205 shorter events, 101.2 us)
Async XLA Ops:
  7.2 115.5 %all-gather.3.cloned.1.call-start = ((), (), s32[]{:S(2)}) async-start(), calls=%async_computation.2 | async-start | bytes 2949120 | tf_op jit(solution)/shard_map/all_gather | solution.py:824
  9.0 13.0 %collective-permute-start.1 = (bf16[24,3200]{1,0:T(8,128)(2,1)S(1)}, bf16[24,3200]{1,0:T(8,128)(2,1)S(1)}, u32[]{:S(2)}, u32[]{:S(2)}) collective-permute-start(bf16[24,3200]{1,0:T(8,128)(2,1)S(1)} %get-tuple-element.197), channel_id=1, source_target_pairs={{0,16},{8,24},{16,0},{24,8},{1,17},{9,25},{17,1},{25,9},{2,18},{10... | collective-permute-start | bytes 460808 | tf_op jit(solution)/shard_map/ppermute | solution.py:759
  13.1 8.9 %collective-permute-start = (bf16[24,3200]{1,0:T(8,128)(2,1)S(1)}, bf16[24,3200]{1,0:T(8,128)(2,1)S(1)}, u32[]{:S(2)}, u32[]{:S(2)}) collective-permute-start(bf16[24,3200]{1,0:T(8,128)(2,1)S(1)} %get-tuple-element.197), channel_id=1, source_target_pairs={{0,8},{8,0},{16,24},{24,16},{1,9},{9,1},{17,25},{25,17},{2,10},{10... | collective-permute-start | bytes 460808 | tf_op jit(solution)/shard_map/ppermute | solution.py:759
  14.7 10.2 %collective-permute-start.2 = (bf16[24,3200]{1,0:T(8,128)(2,1)S(1)}, bf16[24,3200]{1,0:T(8,128)(2,1)S(1)}, u32[]{:S(2)}, u32[]{:S(2)}) collective-permute-start(bf16[24,3200]{1,0:T(8,128)(2,1)S(1)} %get-tuple-element.197), channel_id=1, source_target_pairs={{0,24},{8,16},{16,8},{24,0},{1,25},{9,17},{17,9},{25,1},{2,26},{10... | collective-permute-start | bytes 460808 | tf_op jit(solution)/shard_map/ppermute | solution.py:759
  14.7 108.0 %all-gather.5.cloned.1.call-start = ((), (), s32[]{:S(2)}) async-start(), calls=%async_computation.3 | async-start | bytes 2949120 | tf_op jit(solution)/shard_map/all_gather | solution.py:825
  25.9 31.3 %collective-permute-start.5 = (bf16[96,3200]{1,0:T(8,128)(2,1)S(1)}, bf16[96,3200]{1,0:T(8,128)(2,1)}, u32[]{:S(2)}, u32[]{:S(2)}) collective-permute-start(bf16[96,3200]{1,0:T(8,128)(2,1)S(1)} %pad_maximum_fusion.2.rest_0_.refs_1_), channel_id=1, source_target_pairs={{0,6},{1,7},{2,4},{3,5},{4,2},{5,3},{6,0},{7,1},{8,14},{9,15},{10,... | collective-permute-start | bytes 1843208 | tf_op jit(solution)/shard_map/ppermute | solution.py:767
  28.4 27.7 %collective-permute-start.4 = (bf16[96,3200]{1,0:T(8,128)(2,1)S(1)}, bf16[96,3200]{1,0:T(8,128)(2,1)}, u32[]{:S(2)}, u32[]{:S(2)}) collective-permute-start(bf16[96,3200]{1,0:T(8,128)(2,1)S(1)} %pad_maximum_fusion.2.rest_0_.refs_1_), channel_id=1, source_target_pairs={{0,4},{1,5},{2,6},{3,7},{4,0},{5,1},{6,2},{7,3},{8,12},{9,13},{10,... | collective-permute-start | bytes 1843208 | tf_op jit(solution)/shard_map/ppermute | solution.py:767
  28.9 26.0 %collective-permute-start.3 = (bf16[96,3200]{1,0:T(8,128)(2,1)S(1)}, bf16[96,3200]{1,0:T(8,128)(2,1)}, u32[]{:S(2)}, u32[]{:S(2)}) collective-permute-start(bf16[96,3200]{1,0:T(8,128)(2,1)S(1)} %pad_maximum_fusion.2.rest_0_.refs_1_), channel_id=1, source_target_pairs={{0,2},{1,3},{2,0},{3,1},{4,6},{5,7},{6,4},{7,5},{8,10},{9,11},{10,... | collective-permute-start | bytes 1843208 | tf_op jit(solution)/shard_map/ppermute | solution.py:767
  59.8 6.7 %collective-permute-start.6 = (bf16[384,3200]{1,0:T(8,128)(2,1)}, bf16[384,3200]{1,0:T(8,128)(2,1)}, u32[]{:S(2)}, u32[]{:S(2)}) collective-permute-start(bf16[384,3200]{1,0:T(8,128)(2,1)} %held.12.w_ref.refs_3_), channel_id=1, source_target_pairs={{0,1},{1,0},{2,3},{3,2},{4,5},{5,4},{6,7},{7,6},{8,9},{9,8},{10,11... | collective-permute-start | bytes 7372808 | tf_op jit(solution)/shard_map/ppermute | solution.py:769
  59.9 287.2 %reduce-scatter.3.cloned.1.call-start = ((), (), s32[]{:S(2)}) async-start(), calls=%async_computation.4 | async-start | bytes 2949120 | tf_op jit(solution)/shard_map/reduce_scatter | solution.py:905
  63.1 48.8 %collective-permute-start.7 = (bf16[656,768]{1,0:T(8,128)(2,1)}, bf16[656,768]{1,0:T(8,128)(2,1)}, u32[]{:S(2)}, u32[]{:S(2)}) collective-permute-start(bf16[656,768]{1,0:T(8,128)(2,1)} %get-tuple-element.83), channel_id=1, source_target_pairs={{0,2},{1,3},{2,0},{3,1},{4,6},{5,7},{6,4},{7,5},{8,10},{9,11},{10,... | collective-permute-start | bytes 3022856 | tf_op jit(solution)/shard_map/ppermute | solution.py:841
  64.6 47.3 %collective-permute-start.8 = (bf16[656,768]{1,0:T(8,128)(2,1)}, bf16[656,768]{1,0:T(8,128)(2,1)}, u32[]{:S(2)}, u32[]{:S(2)}) collective-permute-start(bf16[656,768]{1,0:T(8,128)(2,1)} %get-tuple-element.84), channel_id=1, source_target_pairs={{0,4},{1,5},{2,6},{3,7},{4,0},{5,1},{6,2},{7,3},{8,12},{9,13},{10,... | collective-permute-start | bytes 3022856 | tf_op jit(solution)/shard_map/ppermute | solution.py:841
  65.1 46.8 %collective-permute-start.9 = (bf16[656,768]{1,0:T(8,128)(2,1)}, bf16[656,768]{1,0:T(8,128)(2,1)S(1)}, u32[]{:S(2)}, u32[]{:S(2)}) collective-permute-start(bf16[656,768]{1,0:T(8,128)(2,1)} %get-tuple-element.85), channel_id=1, source_target_pairs={{0,6},{1,7},{2,4},{3,5},{4,2},{5,3},{6,0},{7,1},{8,14},{9,15},{10,... | collective-permute-start | bytes 3022856 | tf_op jit(solution)/shard_map/ppermute | solution.py:841
  122.7 7.0 %collective-permute-start.10 = (bf16[768,1536]{1,0:T(8,128)(2,1)}, bf16[768,1536]{1,0:T(8,128)(2,1)S(1)}, u32[]{:S(2)}, u32[]{:S(2)}) collective-permute-start(bf16[768,1536]{1,0:T(8,128)(2,1)} %held.14.in_own), channel_id=1, source_target_pairs={{0,1},{1,0},{2,3},{3,2},{4,5},{5,4},{6,7},{7,6},{8,9},{9,8},{10,11... | collective-permute-start | bytes 7077896 | tf_op jit(solution)/shard_map/ppermute | solution.py:889
  122.8 8.2 %collective-permute-start.11 = (bf16[768,1536]{1,0:T(8,128)(2,1)}, bf16[768,1536]{1,0:T(8,128)(2,1)}, u32[]{:S(2)}, u32[]{:S(2)}) collective-permute-start(bf16[768,1536]{1,0:T(8,128)(2,1)} %held.15.out_own), channel_id=1, source_target_pairs={{0,1},{1,0},{2,3},{3,2},{4,5},{5,4},{6,7},{7,6},{8,9},{9,8},{10,11... | collective-permute-start | bytes 7077896 | tf_op jit(solution)/shard_map/ppermute | solution.py:890
  123.2 28.6 %collective-permute-start.12 = (bf16[656,768]{1,0:T(8,128)(2,1)}, bf16[656,768]{1,0:T(8,128)(2,1)S(1)}, u32[]{:S(2)}, u32[]{:S(2)}) collective-permute-start(bf16[656,768]{1,0:T(8,128)(2,1)} %get-tuple-element.89), channel_id=1, source_target_pairs={{0,2},{1,3},{2,0},{3,1},{4,6},{5,7},{6,4},{7,5},{8,10},{9,11},{10,... | collective-permute-start | bytes 3022856 | tf_op jit(solution)/shard_map/ppermute | solution.py:841
  124.7 50.9 %collective-permute-start.13 = (bf16[656,768]{1,0:T(8,128)(2,1)}, bf16[656,768]{1,0:T(8,128)(2,1)}, u32[]{:S(2)}, u32[]{:S(2)}) collective-permute-start(bf16[656,768]{1,0:T(8,128)(2,1)} %get-tuple-element.92), channel_id=1, source_target_pairs={{0,4},{1,5},{2,6},{3,7},{4,0},{5,1},{6,2},{7,3},{8,12},{9,13},{10,... | collective-permute-start | bytes 3022856 | tf_op jit(solution)/shard_map/ppermute | solution.py:841
  125.3 71.7 %collective-permute-start.14 = (bf16[656,768]{1,0:T(8,128)(2,1)}, bf16[656,768]{1,0:T(8,128)(2,1)}, u32[]{:S(2)}, u32[]{:S(2)}) collective-permute-start(bf16[656,768]{1,0:T(8,128)(2,1)} %get-tuple-element.95), channel_id=1, source_target_pairs={{0,6},{1,7},{2,4},{3,5},{4,2},{5,3},{6,0},{7,1},{8,14},{9,15},{10,... | collective-permute-start | bytes 3022856 | tf_op jit(solution)/shard_map/ppermute | solution.py:841
  174.0 24.6 %collective-permute-start.15 = (bf16[656,768]{1,0:T(8,128)(2,1)}, bf16[656,768]{1,0:T(8,128)(2,1)S(1)}, u32[]{:S(2)}, u32[]{:S(2)}) collective-permute-start(bf16[656,768]{1,0:T(8,128)(2,1)} %get-tuple-element.93.rest_0_), channel_id=1, source_target_pairs={{0,2},{1,3},{2,0},{3,1},{4,6},{5,7},{6,4},{7,5},{8,10},{9,11},{10,... | collective-permute-start | bytes 3022856 | tf_op jit(solution)/shard_map/ppermute | solution.py:900
  196.4 25.6 %collective-permute-start.16 = (bf16[656,768]{1,0:T(8,128)(2,1)}, bf16[656,768]{1,0:T(8,128)(2,1)S(1)}, u32[]{:S(2)}, u32[]{:S(2)}) collective-permute-start(bf16[656,768]{1,0:T(8,128)(2,1)} %get-tuple-element.96.rest_1_), channel_id=1, source_target_pairs={{0,4},{1,5},{2,6},{3,7},{4,0},{5,1},{6,2},{7,3},{8,12},{9,13},{10,... | collective-permute-start | bytes 3022856 | tf_op jit(solution)/shard_map/ppermute | solution.py:900
  220.4 24.7 %collective-permute-start.17 = (bf16[656,768]{1,0:T(8,128)(2,1)}, bf16[656,768]{1,0:T(8,128)(2,1)S(1)}, u32[]{:S(2)}, u32[]{:S(2)}) collective-permute-start(bf16[656,768]{1,0:T(8,128)(2,1)} %get-tuple-element.122), channel_id=1, source_target_pairs={{0,6},{1,7},{2,4},{3,5},{4,2},{5,3},{6,0},{7,1},{8,14},{9,15},{10,... | collective-permute-start | bytes 3022856 | tf_op jit(solution)/shard_map/ppermute | solution.py:900
  265.0 104.6 %reduce-scatter.5.cloned.1.call-start = ((), (), s32[]{:S(2)}) async-start(), calls=%async_computation.5 | async-start | bytes 2949120 | tf_op jit(solution)/shard_map/reduce_scatter | solution.py:905
  275.8 9.1 %collective-permute-start.19 = (bf16[768,1536]{1,0:T(8,128)(2,1)}, bf16[768,1536]{1,0:T(8,128)(2,1)}, u32[]{:S(2)}, u32[]{:S(2)}) collective-permute-start(bf16[768,1536]{1,0:T(8,128)(2,1)} %held.16), channel_id=1, source_target_pairs={{0,1},{1,0},{2,3},{3,2},{4,5},{5,4},{6,7},{7,6},{8,9},{9,8},{10,11... | collective-permute-start | bytes 7077896 | tf_op jit(solution)/shard_map/ppermute | solution.py:917
  289.3 52.3 %collective-permute-start.20 = (bf16[640,768]{1,0:T(8,128)(2,1)}, bf16[640,768]{1,0:T(8,128)(2,1)S(1)}, u32[]{:S(2)}, u32[]{:S(2)}) collective-permute-start(bf16[640,768]{1,0:T(8,128)(2,1)} %get-tuple-element.124), channel_id=1, source_target_pairs={{0,2},{1,3},{2,0},{3,1},{4,6},{5,7},{6,4},{7,5},{8,10},{9,11},{10,... | collective-permute-start | bytes 2949128 | tf_op jit(solution)/shard_map/ppermute | solution.py:841
  290.9 50.7 %collective-permute-start.21 = (bf16[640,768]{1,0:T(8,128)(2,1)}, bf16[640,768]{1,0:T(8,128)(2,1)}, u32[]{:S(2)}, u32[]{:S(2)}) collective-permute-start(bf16[640,768]{1,0:T(8,128)(2,1)} %get-tuple-element.125), channel_id=1, source_target_pairs={{0,4},{1,5},{2,6},{3,7},{4,0},{5,1},{6,2},{7,3},{8,12},{9,13},{10,... | collective-permute-start | bytes 2949128 | tf_op jit(solution)/shard_map/ppermute | solution.py:841
  291.5 50.1 %collective-permute-start.22 = (bf16[640,768]{1,0:T(8,128)(2,1)}, bf16[640,768]{1,0:T(8,128)(2,1)}, u32[]{:S(2)}, u32[]{:S(2)}) collective-permute-start(bf16[640,768]{1,0:T(8,128)(2,1)} %get-tuple-element.126), channel_id=1, source_target_pairs={{0,6},{1,7},{2,4},{3,5},{4,2},{5,3},{6,0},{7,1},{8,14},{9,15},{10,... | collective-permute-start | bytes 2949128 | tf_op jit(solution)/shard_map/ppermute | solution.py:841
  379.4 29.2 %collective-permute-start.24 = (bf16[96,3200]{1,0:T(8,128)(2,1)}, bf16[96,3200]{1,0:T(8,128)(2,1)}, u32[]{:S(2)}, u32[]{:S(2)}) collective-permute-start(bf16[96,3200]{1,0:T(8,128)(2,1)} %get-tuple-element.188), channel_id=1, source_target_pairs={{0,2},{1,3},{2,0},{3,1},{4,6},{5,7},{6,4},{7,5},{8,10},{9,11},{10,... | collective-permute-start | bytes 1843208 | tf_op jit(solution)/shard_map/ppermute | solution.py:784
  380.8 28.9 %collective-permute-start.26 = (bf16[96,3200]{1,0:T(8,128)(2,1)}, bf16[96,3200]{1,0:T(8,128)(2,1)}, u32[]{:S(2)}, u32[]{:S(2)}) collective-permute-start(bf16[96,3200]{1,0:T(8,128)(2,1)} %get-tuple-element.189), channel_id=1, source_target_pairs={{0,6},{1,7},{2,4},{3,5},{4,2},{5,3},{6,0},{7,1},{8,14},{9,15},{10,... | collective-permute-start | bytes 1843208 | tf_op jit(solution)/shard_map/ppermute | solution.py:784
  382.3 28.6 %collective-permute-start.25 = (bf16[96,3200]{1,0:T(8,128)(2,1)S(1)}, bf16[96,3200]{1,0:T(8,128)(2,1)}, u32[]{:S(2)}, u32[]{:S(2)}) collective-permute-start(bf16[96,3200]{1,0:T(8,128)(2,1)S(1)} %get-tuple-element.190), channel_id=1, source_target_pairs={{0,4},{1,5},{2,6},{3,7},{4,0},{5,1},{6,2},{7,3},{8,12},{9,13},{10,... | collective-permute-start | bytes 1843208 | tf_op jit(solution)/shard_map/ppermute | solution.py:784
  414.9 7.5 %collective-permute-start.27 = (bf16[24,3200]{1,0:T(8,128)(2,1)S(1)}, bf16[24,3200]{1,0:T(8,128)(2,1)S(1)}, u32[]{:S(2)}, u32[]{:S(2)}) collective-permute-start(bf16[24,3200]{1,0:T(8,128)(2,1)S(1)} %get-tuple-element.191), channel_id=1, source_target_pairs={{0,8},{8,0},{16,24},{24,16},{1,9},{9,1},{17,25},{25,17},{2,10},{10... | collective-permute-start | bytes 460808 | tf_op jit(solution)/shard_map/ppermute | solution.py:794
  415.4 9.9 %collective-permute-start.29 = (bf16[24,3200]{1,0:T(8,128)(2,1)S(1)}, bf16[24,3200]{1,0:T(8,128)(2,1)S(1)}, u32[]{:S(2)}, u32[]{:S(2)}) collective-permute-start(bf16[24,3200]{1,0:T(8,128)(2,1)S(1)} %get-tuple-element.192), channel_id=1, source_target_pairs={{0,24},{8,16},{16,8},{24,0},{1,25},{9,17},{17,9},{25,1},{2,26},{10... | collective-permute-start | bytes 460808 | tf_op jit(solution)/shard_map/ppermute | solution.py:794
  418.4 11.9 %collective-permute-start.28 = (bf16[24,3200]{1,0:T(8,128)(2,1)S(1)}, bf16[24,3200]{1,0:T(8,128)(2,1)S(1)}, u32[]{:S(2)}, u32[]{:S(2)}) collective-permute-start(bf16[24,3200]{1,0:T(8,128)(2,1)S(1)} %get-tuple-element.193), channel_id=1, source_target_pairs={{0,16},{8,24},{16,0},{24,8},{1,17},{9,25},{17,1},{25,9},{2,18},{10... | collective-permute-start | bytes 460808 | tf_op jit(solution)/shard_map/ppermute | solution.py:794
  (32 other events, 202.7 us)
Sparse Core Ops, SparseCore 0:
  14.9 51.9 all-gather.2
  68.5 50.4 all-gather.4
  265.1 54.7 reduce-scatter.2
  322.1 47.5 reduce-scatter.4
